TPU v7x, 512 devices: a whole 4x4x16 slice. The times are simulated.
512 devices in a mesh: tensor: 4 (over z_hi, core), row: 8 (over z_lo), col: 16 (over x, y).
Axes of the slice: x: 4, y: 4, z: 16 (z_hi: 2, z_lo: 8; z = z_hi * 8 + z_lo), core: 2. Of those that a mesh axis runs over, the one named last changes fastest.
Arguments:
- features: bfloat16 [16384, 6144], P(('row', 'col'), 'tensor'), may hold values from -8 to 8
- w_proj: bfloat16 [6144, 1024], P('tensor'), may hold values from -0.078125 to 0.078125
- flags: int32 [16384], P(('row', 'col')), may hold values 0 or 1
- rates: float32 [5], replicated, may hold values from 0.25 to 4
Outputs:
- feature_grad: bfloat16 [16384, 6144], P(('row', 'col'), 'tensor')
All inputs are finite; a program needn't handle non-finite values. No bound on the sum of `flags` on one device may be relied on, other than what follows from the above.
Results may differ from a plain program's by a relative error of at most 0.029.
Values may be sent and summed in bfloat16 or wider, within the bound.
No kernel may reach another device: no remote copies, remote signals or barrier semaphores. Data moves between devices by JAX's collectives and lax.ppermute only.
A program may use at most 64 MiB of HBM per device.

v0:
```python
import jax
import jax.numpy as jnp
from jax import lax
from jax.sharding import PartitionSpec as P


def tensor_sum(value):
    return lax.psum(value.astype(jnp.bfloat16), "tensor").astype(jnp.float32)


def shards(features, w_proj, flags, rates):
    group = features.shape[0]
    width = w_proj.shape[1]
    n_tensor = lax.axis_size("tensor")
    quarter = group // n_tensor
    tpos = lax.axis_index("tensor")
    signs = (1 - 2 * flags).astype(jnp.bfloat16)
    own_s = lax.dynamic_slice_in_dim(signs, tpos * quarter, quarter, 0)
    proj_full = tensor_sum(jnp.dot(features, w_proj, preferred_element_type=jnp.float32)).astype(
        jnp.bfloat16
    )
    own_z = lax.dynamic_slice_in_dim(proj_full, tpos * quarter, quarter, 0)
    row_z, row_s = (
        lax.all_gather(proj_full, "row", axis=0, tiled=True),
        lax.all_gather(signs, "row", axis=0, tiled=True),
    )
    col_z, col_s = (
        lax.all_gather(own_z, "col", axis=0, tiled=True),
        lax.all_gather(own_s, "col", axis=0, tiled=True),
    )
    row_norm = jnp.sum(jnp.square(row_z.astype(jnp.float32)), axis=1)
    col_norm = jnp.sum(jnp.square(col_z.astype(jnp.float32)), axis=1)
    cross = lax.dot_general(
        row_z, col_z, (((1,), (1,)), ((), ())), preferred_element_type=jnp.float32
    )
    dist = jnp.maximum(row_norm[:, None] + col_norm[None, :] - 2.0 * cross, 0.0) / width
    kernel = jnp.zeros_like(dist)
    for band in range(rates.shape[0]):
        kernel = kernel + rates[band] * jnp.exp(-rates[band] * dist)
    mixed = (
        -16.0
        / width
        * row_s.astype(jnp.float32)[:, None]
        * col_s.astype(jnp.float32)[None, :]
        * kernel
    )
    rounded = mixed.astype(jnp.bfloat16)
    row_total = jnp.sum(mixed, axis=1)
    col_total = jnp.sum(mixed, axis=0)
    block = rounded
    lead = col_total
    own_rows = col_z
    other = lax.dot_general(
        block, row_z, (((0,), (0,)), ((), ())), preferred_element_type=jnp.float32
    )
    col_part = lax.psum_scatter(
        (lead[:, None] * own_rows.astype(jnp.float32) - other).astype(jnp.bfloat16),
        "col",
        scatter_dimension=0,
        tiled=True,
    ).astype(jnp.float32)
    block = rounded
    lead = row_total
    own_rows = row_z
    row_part = lax.psum_scatter(
        (
            lead[:, None] * own_rows.astype(jnp.float32)
            - jnp.dot(block, col_z, preferred_element_type=jnp.float32)
        ).astype(jnp.bfloat16),
        "row",
        scatter_dimension=0,
        tiled=True,
    ).astype(jnp.float32)
    placed = lax.dynamic_update_slice_in_dim(
        jnp.zeros((group, width), jnp.float32), col_part, tpos * quarter, 0
    )
    grad_z = tensor_sum(row_part + placed).astype(jnp.bfloat16)
    result = lax.dot_general(
        grad_z, w_proj, (((1,), (1,)), ((), ())), preferred_element_type=jnp.float32
    )
    return result.astype(jnp.bfloat16)


def solution(mesh):
    in_specs = (P(("row", "col"), "tensor"), P("tensor", None), P(("row", "col")), P())
    out_specs = P(("row", "col"), "tensor")
    return jax.shard_map(shards, mesh=mesh, in_specs=in_specs, out_specs=out_specs, check_vma=False)
```

profile of v0, /device:TPU:1, one launch (start us, length us, event | category | flops | bytes accessed | tf_op | source)
XLA Modules:
  0.0 494.9 jit_solution(233492675417268353)
XLA Ops:
  6.5 1.9 copy-done
  8.4 2.3 convolution_convert_fusion.1
  10.7 0.0 all-reduce.4.cloned.1.call-update
  10.7 0.0 all-gather.6.cloned.1.call-start
  10.8 90.4 %all-reduce.4.cloned.1.call-done = bf16[128,1024]{1,0:T(8,128)(2,1)} async-done(((bf16[128,1024]{1,0:T(8,128)(2,1)}), bf16[128,1024]{1,0:T(8,128)(2,1)}) %all-reduce.4.cloned.1.call-update) | async-done | bytes 262160 | tf_op jit(solution)/shard_map/psum | solution.py:8
  101.2 1.5 constant_dynamic-slice_fusion
  102.7 0.0 all-gather.6.cloned.1.call-update
  102.7 0.0 all-gather.4.cloned.1.call-start
  102.7 0.7 all-gather.4.cloned.1.call-update
  103.4 0.0 reduce-scatter.3.cloned.1.call-start
  103.5 0.1 dynamic_slice.6
  103.6 1.3 dynamic-slice.1
  105.5 0.2 dynamic-update-slice.1
  105.7 31.4 %all-reduce = bf16[512]{0:T(512)(128)(2,1)S(1)} all-reduce(bf16[512]{0:T(512)(128)(2,1)S(1)} %dynamic-update-slice.1), channel_id=1, replica_groups=mesh['tensor'=4,'row'=8,'col'=16] {'col'}, use_global_device_ids=true, to_apply=%add | all-reduce | flops 512 | bytes 2048
  137.1 0.7 fusion.10
  140.9 22.1 %all-gather = bf16[8,1,128]{2,1,0:T(2,128)(2,1)S(1)} all-gather(bf16[1,1,128]{2,1,0:T(2,128)(2,1)S(1)} %get-tuple-element.7), channel_id=1, replica_groups=mesh['tensor'=4,'row'=8,'col'=16] {'row'}, dimensions={0}, use_global_device_ids=true | all-gather | bytes 2304 | tf_op jit(solution)/shard_map/all_gather | solution.py:25
  163.1 1.5 fusion.3
  164.6 55.9 %all-gather.4.cloned.1.call-done = bf16[1024,1024]{1,0:T(8,128)(2,1)} async-done(((bf16[128,1024]{1,0:T(8,128)(2,1)}), bf16[1024,1024]{1,0:T(8,128)(2,1)}) %all-gather.4.cloned.1.call-update) | async-done | bytes 2097168 | tf_op jit(solution)/shard_map/all_gather | solution.py:24
  220.5 2.2 fusion
  222.7 8.2 %fusion.9 = (f32[512]{0:T(512)S(1)}, f32[1024]{0:T(1024)S(1)}, bf16[1024,512]{1,0:T(8,128)(2,1)S(1)}) fusion(f32[]{:T(128)S(6)} %mul.157, f32[]{:T(128)} %bitcast.7, f32[]{:T(128)S(6)} %mul.152, f32[]{:T(128)} %bitcast.6, f32[]{:T(128)S(6)} %mul.147, f32[]{:T(128)} %bitcast.5, f32[]{:T(128)S(6)} %mul.142, f32[]{:T(128)} %bitcast.4, f32[]{:T(128)S(6)} %mul.137, ...), kind=kOutput, calls=%fused_computation.20 | convolution fusion | flops 1085798912 | bytes 4212776 | tf_op jit(solution)/shard_map/dot_general | solution.py:33
  230.9 1.0 copy-done.5
  231.9 2.6 fusion.2
  234.5 0.0 reduce-scatter.5.cloned.1.call-start
  234.5 4.5 fusion.5
  239.0 0.0 all-reduce.6.cloned.1.call-start
  239.1 64.8 %reduce-scatter.3.cloned.1.call-done = bf16[128,1024]{1,0:T(8,128)(2,1)} async-done(((bf16[1024,1024]{1,0:T(8,128)(2,1)}), bf16[128,1024]{1,0:T(8,128)(2,1)}) %reduce-scatter.3.cloned.1.call-update) | async-done | bytes 262160 | tf_op jit(solution)/shard_map/reduce_scatter | solution.py:65
  303.9 1.8 convert_element_type.55
  305.7 89.9 %reduce-scatter.5.cloned.1.call-done = bf16[32,1024]{1,0:T(8,128)(2,1)} async-done(((bf16[512,1024]{1,0:T(8,128)(2,1)}), bf16[32,1024]{1,0:T(8,128)(2,1)}) %reduce-scatter.5.cloned.1.call-update) | async-done | bytes 65552 | tf_op jit(solution)/shard_map/reduce_scatter | solution.py:56
  395.5 1.6 add_dynamic-update-slice_fusion
  397.1 1.8 convert_element_type.59
  398.9 86.3 %all-reduce.6.cloned.1.call-done = bf16[128,1024]{1,0:T(8,128)(2,1)} async-done(((bf16[128,1024]{1,0:T(8,128)(2,1)}), bf16[128,1024]{1,0:T(8,128)(2,1)}) %all-reduce.6.cloned.1.call-update) | async-done | bytes 262160 | tf_op jit(solution)/shard_map/psum | solution.py:8
  485.2 2.9 convolution_convert_fusion
  (19 shorter events, 0.1 us)
Async XLA Ops:
  6.5 1.9 copy-start
  6.5 96.9 %copy-start.4 = (s32[128]{0:T(128)S(1)}, s32[128]{0:T(128)}, u32[]{:S(2)}) copy-start(s32[128]{0:T(128)} %param.6) | copy-start | bytes 1540
  6.5 130.6 %copy-start.3 = (f32[5]{0:T(128)S(1)}, f32[5]{0:T(128)}, u32[]{:S(2)}) copy-start(f32[5]{0:T(128)} %param.7) | copy-start | bytes 64
  6.5 94.7 %all-reduce.4.cloned.1.call-start = ((), (), s32[]{:S(2)}) async-start(), calls=%async_computation.2 | async-start | bytes 524288 | tf_op jit(solution)/shard_map/psum | solution.py:8
  10.7 152.3 %all-gather.6.cloned.1.call-start = ((), (), s32[]{:S(2)}) async-start(), calls=%async_computation.4 | async-start | bytes 1114112 | tf_op jit(solution)/shard_map/all_gather | solution.py:28
  102.7 117.8 %all-gather.4.cloned.1.call-start = ((), (), s32[]{:S(2)}) async-start(), calls=%async_computation.3 | async-start | bytes 2359296 | tf_op jit(solution)/shard_map/all_gather | solution.py:24
  103.4 200.4 %reduce-scatter.3.cloned.1.call-start = ((), (), s32[]{:S(2)}) async-start(), calls=%async_computation.5 | async-start | bytes 2359296 | tf_op jit(solution)/shard_map/reduce_scatter | solution.py:65
  220.5 2.2 copy-start.1
  222.7 9.2 %copy-start.2 = (bf16[512,1024]{1,0:T(8,128)(2,1)S(1)}, bf16[512,1024]{1,0:T(8,128)(2,1)}, u32[]{:S(2)}) copy-start(bf16[512,1024]{1,0:T(8,128)(2,1)} %all-gather.6.cloned.1.call-done) | copy-start | bytes 3145732
  230.9 1.0 copy-start.5
  234.5 161.1 %reduce-scatter.5.cloned.1.call-start = ((), (), s32[]{:S(2)}) async-start(), calls=%async_computation.6 | async-start | bytes 1114112 | tf_op jit(solution)/shard_map/reduce_scatter | solution.py:56
  239.0 246.2 %all-reduce.6.cloned.1.call-start = ((), (), s32[]{:S(2)}) async-start(), calls=%async_computation.7 | async-start | bytes 524288 | tf_op jit(solution)/shard_map/psum | solution.py:8
Sparse Core Ops, SparseCore 0:
  10.9 90.2 all-reduce.3
  104.6 46.9 all-gather.5
  153.9 66.4 all-gather.3
  234.6 69.2 reduce-scatter.2
  308.3 87.1 reduce-scatter.4
  399.0 86.0 all-reduce.5
where the time goes:
time: 495 us
  waiting for transfers between devices  388 us (78%)
  blocking collectives  53.5 us (11%)
  matrix products  20.4 us (4%)
  between operations  17.3 us (3%)
  other arithmetic  8.87 us (2%)
  local copies, waits for them, and re-layouts  6.63 us (1%)
    psum x2, waiting for transfers between devices, tensor_sum(): return lax.psum(value.astype(jnp.bfloat16), 'tensor').astype(jnp.float32)  177 us
    reduce_scatter x1, waiting for transfers between devices, shards(): lax.psum_scatter((lead[:, None] * own_rows.astype(jnp.float32) - other).a...  89.9 us
    reduce_scatter x1, waiting for transfers between devices, shards(): lax.psum_scatter((lead[:, None] * own_rows.astype(jnp.float32) - jnp.dot(...  64.8 us
    all_gather x1, waiting for transfers between devices, shards(): lax.all_gather(proj_full, 'row', axis=0, tiled=True)  55.9 us
    unnamed x1, blocking collectives  31.4 us
    all_gather x1, blocking collectives, shards(): lax.all_gather(signs, 'row', axis=0, tiled=True)  22.1 us
  transfers between devices with their start and end apart: 6, of which 5 were waited for; matrix products, arithmetic and copies ran while one was open for 2% of the time, Pallas kernels for 0%

commit v1 on v0

v1 whole, which is shorter than its diff:
```python
import jax
import jax.numpy as jnp
from jax import lax
from jax.sharding import PartitionSpec as P

ZLINE = ("tensor", "row")
PAD = 128


def line_permutation(shift, n_row):
    length = 2 * n_row
    pairs = []
    for chip in range(length):
        for core in range(2):
            chip2, core2 = shift(chip, core)
            chip2 %= length
            source = ((chip // n_row) * 2 + core) * n_row + chip % n_row
            target = ((chip2 // n_row) * 2 + core2) * n_row + chip2 % n_row
            pairs.append((source, target))
    return pairs


def pick(second, low, high):
    return jnp.where(second, high, low)


def shards(features, w_proj, flags, rates):
    f32, bf16 = jnp.float32, jnp.bfloat16
    group = features.shape[0]
    width = w_proj.shape[1]
    n_row = lax.axis_size("row")
    n_col = lax.axis_size("col")
    half, quarter = group // 2, group // 4
    tpos = lax.axis_index("tensor")
    high, core = tpos // 2 == 1, tpos % 2 == 1

    def move(value, shift):
        return lax.ppermute(value, ZLINE, line_permutation(shift, n_row))

    def other_core(value):
        return move(value, lambda chip, core: (chip, 1 - core))

    away = pick(core, features[half:], features[:half])
    mine = pick(core, features[:half], features[half:])
    sent = other_core(jnp.dot(away, w_proj, preferred_element_type=f32).astype(bf16))
    kept = jnp.dot(mine, w_proj, preferred_element_type=f32)
    partial = (kept + sent.astype(f32)).astype(bf16)
    far = move(partial, lambda chip, core: (chip + n_row, core))
    z_half = (partial.astype(f32) + far.astype(f32)).astype(bf16)
    signs = (1 - 2 * flags).astype(bf16)
    s_half = pick(core, signs[:half], signs[half:])
    block = jnp.concatenate([z_half, jnp.broadcast_to(s_half[:, None], (half, PAD))], axis=1)

    blocks = [block]
    for shift in range(1, n_row // 2 + 1):
        blocks.append(move(block, lambda chip, core: (chip - shift, core)))
        if shift < n_row // 2:
            blocks.append(move(block, lambda chip, core: (chip + shift, core)))
    own = pick(high, block[:quarter], block[quarter:])
    col = lax.all_to_all(
        jnp.broadcast_to(own[None], (n_col,) + own.shape), "col", 0, 0, tiled=True
    ).reshape(n_col * quarter, width + PAD)
    near = jnp.concatenate(blocks, axis=0)
    rows = jnp.concatenate([near, other_core(near)], axis=0)
    row_z, row_s = rows[:, :width], rows[:, width].astype(f32)
    col_z, col_s = col[:, :width], col[:, width].astype(f32)

    row_norm = jnp.sum(jnp.square(row_z.astype(f32)), axis=1)
    col_norm = jnp.sum(jnp.square(col_z.astype(f32)), axis=1)
    cross = lax.dot_general(col_z, row_z, (((1,), (1,)), ((), ())), preferred_element_type=f32)
    dist = jnp.maximum(col_norm[:, None] + row_norm[None, :] - 2.0 * cross, 0.0) / width
    kernel = jnp.zeros_like(dist)
    for band in range(rates.shape[0]):
        kernel = kernel + rates[band] * jnp.exp(-rates[band] * dist)
    mixed = -16.0 / width * col_s[:, None] * row_s[None, :] * kernel
    total = jnp.sum(mixed, axis=1)
    other = jnp.dot(mixed.astype(bf16), row_z, preferred_element_type=f32)
    part = (2.0 * (total[:, None] * col_z.astype(f32) - other)).astype(bf16)
    parts = lax.all_to_all(part.reshape(n_col, quarter, width), "col", 0, 0, tiled=True)
    grad = jnp.sum(parts.astype(f32), axis=0).astype(bf16)
    grad_far = move(grad, lambda chip, core: (chip + n_row, core))
    grad = pick(
        high, jnp.concatenate([grad, grad_far], axis=0), jnp.concatenate([grad_far, grad], axis=0)
    )
    grad_other = other_core(grad)
    grad = pick(
        core,
        jnp.concatenate([grad, grad_other], axis=0),
        jnp.concatenate([grad_other, grad], axis=0),
    )
    result = lax.dot_general(grad, w_proj, (((1,), (1,)), ((), ())), preferred_element_type=f32)
    return result.astype(bf16)


def solution(mesh):
    in_specs = (P(("row", "col"), "tensor"), P("tensor", None), P(("row", "col")), P())
    out_specs = P(("row", "col"), "tensor")
    return jax.shard_map(shards, mesh=mesh, in_specs=in_specs, out_specs=out_specs, check_vma=False)
```

time: 495 us -> 162 us (0.33)
  the two profiles are of different devices: /device:TPU:1 before, /device:TPU:33 now
where the time goes in v1:
time: 162 us; the launch traced here: 161 us
  starting transfers between devices  77.8 us (48%)
  blocking collectives  22.3 us (14%)
  waiting for transfers between devices  19.6 us (12%)
  matrix products  15.7 us (10%)
  local copies, waits for them, and re-layouts  14.1 us (9%)
  other arithmetic  8.24 us (5%)
  between operations  3.37 us (2%)
    ppermute x12, starting transfers between devices, move(): return lax.ppermute(value, ZLINE, line_permutation(shift, n_row))  70.9 us
    all_to_all x1, blocking collectives, shards(): lax.all_to_all(part.reshape(n_col, quarter, width), 'col', 0, 0, tiled=True)  22.3 us
    ppermute x12, waiting for transfers between devices, move(): return lax.ppermute(value, ZLINE, line_permutation(shift, n_row))  19.6 us
    unnamed x16, local copies, waits for them, and re-layouts  9.09 us
    dot_general x1, matrix products, shards(): lax.dot_general(col_z, row_z, (((1,), (1,)), ((), ())), preferred_element...  7.38 us
    all_to_all x1, starting transfers between devices, shards(): lax.all_to_all(jnp.broadcast_to(own[None], (n_col,) + own.shape), 'col',...  6.86 us
  transfers between devices with their start and end apart: 13, of which 5 were waited for; matrix products, arithmetic and copies ran while one was open for 8% of the time, Pallas kernels for 0%

profile of v1, /device:TPU:33, one launch (start us, length us, event | category | flops | bytes accessed | tf_op | source)
XLA Modules:
  0.0 161.1 jit_solution(13126116460007616534)
XLA Ops:
  0.0 1.9 %copy-done = bf16[1536,1024]{1,0:T(8,128)(2,1)S(1)} copy-done((bf16[1536,1024]{1,0:T(8,128)(2,1)S(1)}, bf16[1536,1024]{1,0:T(8,128)(2,1)}, u32[]{:S(2)}) %copy-start) | copy-done | bytes 3145752
  1.9 2.3 %convolution_convert_fusion.1 = bf16[64,1024]{1,0:T(8,128)(2,1)} fusion(bf16[1536,1024]{1,0:T(8,128)(2,1)S(1)} %copy-done, pred[]{:T(512)S(6)} %eq.8, bf16[128,1536]{1,0:T(8,128)(2,1)} %param.4), kind=kOutput, calls=%fused_computation.12 | convolution fusion | flops 201490432 | bytes 3670017 | tf_op jit(solution)/shard_map/dot_general | solution.py:45
  4.2 2.6 %collective-permute-start = (bf16[64,1024]{1,0:T(8,128)(2,1)}, bf16[64,1024]{1,0:T(8,128)(2,1)}, u32[]{:S(2)}, u32[]{:S(2)}) collective-permute-start(bf16[64,1024]{1,0:T(8,128)(2,1)} %convolution_convert_fusion.1), channel_id=1, source_target_pairs={{0,128},{128,0},{16,144},{144,16},{32,160},{160,32},{48,176},{176,... | collective-permute-start | bytes 393224 | tf_op jit(solution)/shard_map/ppermute | solution.py:38
  6.9 1.3 collective-permute-done
  8.1 1.6 add_convert_fusion.1
  9.7 14.5 %collective-permute-start.1 = (bf16[64,1024]{1,0:T(8,128)(2,1)S(1)}, bf16[64,1024]{1,0:T(8,128)(2,1)S(1)}, u32[]{:S(2)}, u32[]{:S(2)}) collective-permute-start(bf16[64,1024]{1,0:T(8,128)(2,1)S(1)} %add_convert_fusion.1), channel_id=1, source_target_pairs={{0,256},{128,384},{16,272},{144,400},{32,288},{160,416},{48,304},{... | collective-permute-start | bytes 393224 | tf_op jit(solution)/shard_map/ppermute | solution.py:38
  24.3 11.9 %collective-permute-done.1 = bf16[64,1024]{1,0:T(8,128)(2,1)S(1)} collective-permute-done((bf16[64,1024]{1,0:T(8,128)(2,1)S(1)}, bf16[64,1024]{1,0:T(8,128)(2,1)S(1)}, u32[]{:S(2)}, u32[]{:S(2)}) %collective-permute-start.1) | collective-permute-done | bytes 131104 | tf_op jit(solution)/shard_map/ppermute | solution.py:38
  37.2 1.9 %collective-permute-start.2 = (bf16[64,1152]{1,0:T(8,128)(2,1)}, bf16[64,1152]{1,0:T(8,128)(2,1)}, u32[]{:S(2)}, u32[]{:S(2)}) collective-permute-start(bf16[64,1152]{1,0:T(8,128)(2,1)} %get-tuple-element.21), channel_id=1, source_target_pairs={{0,368},{128,496},{16,0},{144,128},{32,16},{160,144},{48,32},{176,... | collective-permute-start | bytes 442376 | tf_op jit(solution)/shard_map/ppermute | solution.py:38
  39.1 3.4 %collective-permute-start.3 = (bf16[64,1152]{1,0:T(8,128)(2,1)}, bf16[64,1152]{1,0:T(8,128)(2,1)}, u32[]{:S(2)}, u32[]{:S(2)}) collective-permute-start(bf16[64,1152]{1,0:T(8,128)(2,1)} %get-tuple-element.21), channel_id=1, source_target_pairs={{0,16},{128,144},{16,32},{144,160},{32,48},{160,176},{48,64},{176,... | collective-permute-start | bytes 442376 | tf_op jit(solution)/shard_map/ppermute | solution.py:38
  42.4 7.1 %collective-permute-start.4 = (bf16[64,1152]{1,0:T(8,128)(2,1)}, bf16[64,1152]{1,0:T(8,128)(2,1)}, u32[]{:S(2)}, u32[]{:S(2)}) collective-permute-start(bf16[64,1152]{1,0:T(8,128)(2,1)} %get-tuple-element.21), channel_id=1, source_target_pairs={{0,352},{128,480},{16,368},{144,496},{32,0},{160,128},{48,16},{176... | collective-permute-start | bytes 442376 | tf_op jit(solution)/shard_map/ppermute | solution.py:38
  49.5 1.9 %collective-permute-start.5 = (bf16[64,1152]{1,0:T(8,128)(2,1)}, bf16[64,1152]{1,0:T(8,128)(2,1)S(1)}, u32[]{:S(2)}, u32[]{:S(2)}) collective-permute-start(bf16[64,1152]{1,0:T(8,128)(2,1)} %get-tuple-element.21), channel_id=1, source_target_pairs={{0,32},{128,160},{16,48},{144,176},{32,64},{160,192},{48,80},{176,... | collective-permute-start | bytes 442376 | tf_op jit(solution)/shard_map/ppermute | solution.py:38
  51.5 6.6 %collective-permute-start.6 = (bf16[64,1152]{1,0:T(8,128)(2,1)}, bf16[64,1152]{1,0:T(8,128)(2,1)S(1)}, u32[]{:S(2)}, u32[]{:S(2)}) collective-permute-start(bf16[64,1152]{1,0:T(8,128)(2,1)} %get-tuple-element.21), channel_id=1, source_target_pairs={{0,336},{128,464},{16,352},{144,480},{32,368},{160,496},{48,0},{17... | collective-permute-start | bytes 442376 | tf_op jit(solution)/shard_map/ppermute | solution.py:38
  59.3 6.9 %all-to-all-start = ((bf16[16,32,1152]{2,1,0:T(8,128)(2,1)}), bf16[16,32,1152]{2,1,0:T(8,128)(2,1)}, u32[]{:S(2)}, u32[]{:S(2)}) async-start(bf16[16,32,1152]{2,1,0:T(8,128)(2,1)} %broadcast_in_dim.5), calls=%async_computation | async-start | bytes 2359296 | tf_op jit(solution)/shard_map/all_to_all | solution.py:60
  66.2 1.9 %collective-permute-start.7 = (bf16[64,1152]{1,0:T(8,128)(2,1)}, bf16[64,1152]{1,0:T(8,128)(2,1)S(1)}, u32[]{:S(2)}, u32[]{:S(2)}) collective-permute-start(bf16[64,1152]{1,0:T(8,128)(2,1)} %get-tuple-element.21), channel_id=1, source_target_pairs={{0,48},{128,176},{16,64},{144,192},{32,80},{160,208},{48,96},{176,... | collective-permute-start | bytes 442376 | tf_op jit(solution)/shard_map/ppermute | solution.py:38
  68.1 1.7 %constant_dynamic-update-slice_fusion.6 = (bf16[512,1152]{1,0:T(8,128)(2,1)}, bf16[1024,1152]{1,0:T(8,128)(2,1)}) fusion(bf16[512,1152]{1,0:T(8,128)(2,1)} %get-tuple-element.19, bf16[64,1152]{1,0:T(8,128)(2,1)} %collective-permute-done.2, bf16[1024,1152]{1,0:T(8,128)(2,1)} %get-tuple-element.20), kind=kLoop, calls=%fused_computation.50 | loop fusion | bytes 442368
  69.7 4.9 %collective-permute-start.8 = (bf16[64,1152]{1,0:T(8,128)(2,1)}, bf16[64,1152]{1,0:T(8,128)(2,1)S(1)}, u32[]{:S(2)}, u32[]{:S(2)}) collective-permute-start(bf16[64,1152]{1,0:T(8,128)(2,1)} %get-tuple-element.21), channel_id=1, source_target_pairs={{0,320},{128,448},{16,336},{144,464},{32,352},{160,480},{48,368},{... | collective-permute-start | bytes 442376 | tf_op jit(solution)/shard_map/ppermute | solution.py:38
  74.6 1.6 %constant_dynamic-update-slice_fusion.5 = (bf16[512,1152]{1,0:T(8,128)(2,1)}, bf16[1024,1152]{1,0:T(8,128)(2,1)}) fusion(bf16[512,1152]{1,0:T(8,128)(2,1)} %get-tuple-element.17, bf16[64,1152]{1,0:T(8,128)(2,1)} %collective-permute-done.3, bf16[1024,1152]{1,0:T(8,128)(2,1)} %get-tuple-element.18), kind=kLoop, calls=%fused_computation.49 | loop fusion | bytes 442368
  76.3 1.6 %constant_dynamic-update-slice_fusion.4 = (bf16[512,1152]{1,0:T(8,128)(2,1)}, bf16[1024,1152]{1,0:T(8,128)(2,1)}) fusion(bf16[512,1152]{1,0:T(8,128)(2,1)} %get-tuple-element.15, bf16[64,1152]{1,0:T(8,128)(2,1)} %collective-permute-done.4, bf16[1024,1152]{1,0:T(8,128)(2,1)} %get-tuple-element.16), kind=kLoop, calls=%fused_computation.48 | loop fusion | bytes 442368
  80.2 1.3 collective-permute-done.8
  82.2 8.9 %collective-permute-start.9 = (bf16[512,1152]{1,0:T(8,128)(2,1)}, bf16[512,1152]{1,0:T(8,128)(2,1)}, u32[]{:S(2)}, u32[]{:S(2)}) collective-permute-start(bf16[512,1152]{1,0:T(8,128)(2,1)} %get-tuple-element.5), channel_id=1, source_target_pairs={{0,128},{128,0},{16,144},{144,16},{32,160},{160,32},{48,176},{176,... | collective-permute-start | bytes 3538952 | tf_op jit(solution)/shard_map/ppermute | solution.py:38
  96.0 1.5 fusion
  97.5 2.4 %constant_dynamic-update-slice_fusion.8 = bf16[1024,1152]{1,0:T(8,128)(2,1)} fusion(bf16[1024,1152]{1,0:T(8,128)(2,1)} %get-tuple-element.6, bf16[512,1152]{1,0:T(8,128)(2,1)} %collective-permute-done.9), kind=kLoop, calls=%fused_computation.52 | loop fusion | bytes 2359296 | tf_op jit(solution)/shard_map/concatenate | solution.py:64
  99.9 1.2 convert_reduce_fusion
  101.2 2.1 %multiply_reduce_fusion = f32[1024]{0:T(1024)S(1)} fusion(bf16[1024,1152]{1,0:T(8,128)(2,1)} %constant_dynamic-update-slice_fusion.8), kind=kLoop, calls=%fused_computation | loop fusion | flops 3144704 | bytes 2101248 | tf_op jit(solution)/shard_map/reduce_sum | solution.py:68
  103.3 7.4 %fusion.33 = (f32[512]{0:T(512)S(1)}, bf16[512,1024]{1,0:T(8,128)(2,1)S(1)}) fusion(f32[]{:T(128)S(6)} %mul.146, f32[]{:T(128)} %bitcast.5, f32[]{:T(128)S(6)} %mul.141, f32[]{:T(128)} %bitcast.4, f32[]{:T(128)S(6)} %mul.136, f32[]{:T(128)} %bitcast.3, f32[]{:T(128)S(6)} %mul.131, f32[]{:T(128)} %bitcast.2, f32[]{:T(128)S(6)} %mul.126, ...), kind=kOutput, calls=%fused_computation.65 | convolution fusion | flops 1085275648 | bytes 4211220 | tf_op jit(solution)/shard_map/dot_general | solution.py:70
  110.6 2.5 %fusion.3 = bf16[512,1024]{1,0:T(8,128)(2,1)S(1)} fusion(bf16[1024,1152]{1,0:T(8,128)(2,1)S(1)} %copy-done.1, bf16[512,1024]{1,0:T(8,128)(2,1)S(1)} %get-tuple-element.28, f32[512]{0:T(512)S(1)} %get-tuple-element.27, bf16[512,1152]{1,0:T(8,128)(2,1)} %bitcast), kind=kOutput, calls=%fused_computation.7 | convolution fusion | flops 1076363264 | bytes 5244928 | tf_op jit(solution)/shard_map/dot_general | solution.py:77
  113.1 22.3 %all_to_all.10 = bf16[16,32,1024]{2,1,0:T(8,128)(2,1)} all-to-all(bf16[16,32,1024]{2,1,0:T(8,128)(2,1)S(1)} %bitcast.11), channel_id=1, replica_groups=mesh['tensor'=4,'row'=8,'col'=16] {'col'}, dimensions={0} | all-to-all | bytes 2097152 | tf_op jit(solution)/shard_map/all_to_all | solution.py:79
  135.5 1.4 reduce_sum.42
  136.9 11.0 %collective-permute-start.10 = (bf16[32,1024]{1,0:T(8,128)(2,1)S(1)}, bf16[32,1024]{1,0:T(8,128)(2,1)S(1)}, u32[]{:S(2)}, u32[]{:S(2)}) collective-permute-start(bf16[32,1024]{1,0:T(8,128)(2,1)S(1)} %reduce_sum.42), channel_id=1, source_target_pairs={{0,256},{128,384},{16,272},{144,400},{32,288},{160,416},{48,304},{... | collective-permute-start | bytes 196616 | tf_op jit(solution)/shard_map/ppermute | solution.py:38
  147.9 4.1 %collective-permute-done.10 = bf16[32,1024]{1,0:T(8,128)(2,1)S(1)} collective-permute-done((bf16[32,1024]{1,0:T(8,128)(2,1)S(1)}, bf16[32,1024]{1,0:T(8,128)(2,1)S(1)}, u32[]{:S(2)}, u32[]{:S(2)}) %collective-permute-start.10) | collective-permute-done | bytes 65568 | tf_op jit(solution)/shard_map/ppermute | solution.py:38
  152.1 6.1 %collective-permute-start.11 = (bf16[64,1024]{1,0:T(8,128)(2,1)S(1)}, bf16[64,1024]{1,0:T(8,128)(2,1)S(1)}, u32[]{:S(2)}, u32[]{:S(2)}) collective-permute-start(bf16[64,1024]{1,0:T(8,128)(2,1)S(1)} %maximum_select_fusion.2), channel_id=1, source_target_pairs={{0,128},{128,0},{16,144},{144,16},{32,160},{160,32},{48,176},{176,... | collective-permute-start | bytes 393224 | tf_op jit(solution)/shard_map/ppermute | solution.py:38
  159.1 1.9 %convolution_convert_fusion = bf16[128,1536]{1,0:T(8,128)(2,1)} fusion(bf16[1536,1024]{1,0:T(8,128)(2,1)S(1)} %copy-done, bf16[64,1024]{1,0:T(8,128)(2,1)S(1)} %maximum_select_fusion.2, bf16[64,1024]{1,0:T(8,128)(2,1)S(1)} %collective-permute-done.11, pred[]{:T(512)S(6)} %eq.8), kind=kOutput, calls=%fused_computation.3 | convolution fusion | flops 404029440 | bytes 3801089 | tf_op jit(solution)/shard_map/dot_general | solution.py:91
  (32 shorter events, 7.8 us)
Async XLA Ops:
  0.0 1.9 %copy-start = (bf16[1536,1024]{1,0:T(8,128)(2,1)S(1)}, bf16[1536,1024]{1,0:T(8,128)(2,1)}, u32[]{:S(2)}) copy-start(bf16[1536,1024]{1,0:T(8,128)(2,1)} %param.5) | copy-start | bytes 9437188
  0.0 8.1 %copy-start.2 = (bf16[128,1536]{1,0:T(8,128)(2,1)S(1)}, bf16[128,1536]{1,0:T(8,128)(2,1)}, u32[]{:S(2)}) copy-start(bf16[128,1536]{1,0:T(8,128)(2,1)} %param.4) | copy-start | bytes 1179652
  0.0 6.8 %copy-start.4 = (s32[128]{0:T(128)S(1)}, s32[128]{0:T(128)}, u32[]{:S(2)}) copy-start(s32[128]{0:T(128)} %param.6) | copy-start | bytes 1540
  4.2 3.9 %collective-permute-start = (bf16[64,1024]{1,0:T(8,128)(2,1)}, bf16[64,1024]{1,0:T(8,128)(2,1)}, u32[]{:S(2)}, u32[]{:S(2)}) collective-permute-start(bf16[64,1024]{1,0:T(8,128)(2,1)} %convolution_convert_fusion.1), channel_id=1, source_target_pairs={{0,128},{128,0},{16,144},{144,16},{32,160},{160,32},{48,176},{176,... | collective-permute-start | bytes 393224 | tf_op jit(solution)/shard_map/ppermute | solution.py:38
  9.7 26.5 %collective-permute-start.1 = (bf16[64,1024]{1,0:T(8,128)(2,1)S(1)}, bf16[64,1024]{1,0:T(8,128)(2,1)S(1)}, u32[]{:S(2)}, u32[]{:S(2)}) collective-permute-start(bf16[64,1024]{1,0:T(8,128)(2,1)S(1)} %add_convert_fusion.1), channel_id=1, source_target_pairs={{0,256},{128,384},{16,272},{144,400},{32,288},{160,416},{48,304},{... | collective-permute-start | bytes 393224 | tf_op jit(solution)/shard_map/ppermute | solution.py:38
  37.2 29.0 %collective-permute-start.2 = (bf16[64,1152]{1,0:T(8,128)(2,1)}, bf16[64,1152]{1,0:T(8,128)(2,1)}, u32[]{:S(2)}, u32[]{:S(2)}) collective-permute-start(bf16[64,1152]{1,0:T(8,128)(2,1)} %get-tuple-element.21), channel_id=1, source_target_pairs={{0,368},{128,496},{16,0},{144,128},{32,16},{160,144},{48,32},{176,... | collective-permute-start | bytes 442376 | tf_op jit(solution)/shard_map/ppermute | solution.py:38
  39.1 30.7 %collective-permute-start.3 = (bf16[64,1152]{1,0:T(8,128)(2,1)}, bf16[64,1152]{1,0:T(8,128)(2,1)}, u32[]{:S(2)}, u32[]{:S(2)}) collective-permute-start(bf16[64,1152]{1,0:T(8,128)(2,1)} %get-tuple-element.21), channel_id=1, source_target_pairs={{0,16},{128,144},{16,32},{144,160},{32,48},{160,176},{48,64},{176,... | collective-permute-start | bytes 442376 | tf_op jit(solution)/shard_map/ppermute | solution.py:38
  42.4 33.8 %collective-permute-start.4 = (bf16[64,1152]{1,0:T(8,128)(2,1)}, bf16[64,1152]{1,0:T(8,128)(2,1)}, u32[]{:S(2)}, u32[]{:S(2)}) collective-permute-start(bf16[64,1152]{1,0:T(8,128)(2,1)} %get-tuple-element.21), channel_id=1, source_target_pairs={{0,352},{128,480},{16,368},{144,496},{32,0},{160,128},{48,16},{176... | collective-permute-start | bytes 442376 | tf_op jit(solution)/shard_map/ppermute | solution.py:38
  49.5 28.4 %collective-permute-start.5 = (bf16[64,1152]{1,0:T(8,128)(2,1)}, bf16[64,1152]{1,0:T(8,128)(2,1)S(1)}, u32[]{:S(2)}, u32[]{:S(2)}) collective-permute-start(bf16[64,1152]{1,0:T(8,128)(2,1)} %get-tuple-element.21), channel_id=1, source_target_pairs={{0,32},{128,160},{16,48},{144,176},{32,64},{160,192},{48,80},{176,... | collective-permute-start | bytes 442376 | tf_op jit(solution)/shard_map/ppermute | solution.py:38
  51.5 27.2 %collective-permute-start.6 = (bf16[64,1152]{1,0:T(8,128)(2,1)}, bf16[64,1152]{1,0:T(8,128)(2,1)S(1)}, u32[]{:S(2)}, u32[]{:S(2)}) collective-permute-start(bf16[64,1152]{1,0:T(8,128)(2,1)} %get-tuple-element.21), channel_id=1, source_target_pairs={{0,336},{128,464},{16,352},{144,480},{32,368},{160,496},{48,0},{17... | collective-permute-start | bytes 442376 | tf_op jit(solution)/shard_map/ppermute | solution.py:38
  59.3 35.7 %all-to-all-start = ((bf16[16,32,1152]{2,1,0:T(8,128)(2,1)}), bf16[16,32,1152]{2,1,0:T(8,128)(2,1)}, u32[]{:S(2)}, u32[]{:S(2)}) async-start(bf16[16,32,1152]{2,1,0:T(8,128)(2,1)} %broadcast_in_dim.5), calls=%async_computation | async-start | bytes 2359296 | tf_op jit(solution)/shard_map/all_to_all | solution.py:60
  66.1 25.0 %copy-start.3 = (f32[5]{0:T(128)S(1)}, f32[5]{0:T(128)}, u32[]{:S(2)}) copy-start(f32[5]{0:T(128)} %param.7) | copy-start | bytes 64
  66.2 13.3 %collective-permute-start.7 = (bf16[64,1152]{1,0:T(8,128)(2,1)}, bf16[64,1152]{1,0:T(8,128)(2,1)S(1)}, u32[]{:S(2)}, u32[]{:S(2)}) collective-permute-start(bf16[64,1152]{1,0:T(8,128)(2,1)} %get-tuple-element.21), channel_id=1, source_target_pairs={{0,48},{128,176},{16,64},{144,192},{32,80},{160,208},{48,96},{176,... | collective-permute-start | bytes 442376 | tf_op jit(solution)/shard_map/ppermute | solution.py:38
  69.7 11.8 %collective-permute-start.8 = (bf16[64,1152]{1,0:T(8,128)(2,1)}, bf16[64,1152]{1,0:T(8,128)(2,1)S(1)}, u32[]{:S(2)}, u32[]{:S(2)}) collective-permute-start(bf16[64,1152]{1,0:T(8,128)(2,1)} %get-tuple-element.21), channel_id=1, source_target_pairs={{0,320},{128,448},{16,336},{144,464},{32,352},{160,480},{48,368},{... | collective-permute-start | bytes 442376 | tf_op jit(solution)/shard_map/ppermute | solution.py:38
  82.2 15.3 %collective-permute-start.9 = (bf16[512,1152]{1,0:T(8,128)(2,1)}, bf16[512,1152]{1,0:T(8,128)(2,1)}, u32[]{:S(2)}, u32[]{:S(2)}) collective-permute-start(bf16[512,1152]{1,0:T(8,128)(2,1)} %get-tuple-element.5), channel_id=1, source_target_pairs={{0,128},{128,0},{16,144},{144,16},{32,160},{160,32},{48,176},{176,... | collective-permute-start | bytes 3538952 | tf_op jit(solution)/shard_map/ppermute | solution.py:38
  99.9 3.3 %copy-start.1 = (bf16[1024,1152]{1,0:T(8,128)(2,1)S(1)}, bf16[1024,1152]{1,0:T(8,128)(2,1)}, u32[]{:S(2)}) copy-start(bf16[1024,1152]{1,0:T(8,128)(2,1)} %constant_dynamic-update-slice_fusion.8) | copy-start | bytes 7077892
  136.9 15.1 %collective-permute-start.10 = (bf16[32,1024]{1,0:T(8,128)(2,1)S(1)}, bf16[32,1024]{1,0:T(8,128)(2,1)S(1)}, u32[]{:S(2)}, u32[]{:S(2)}) collective-permute-start(bf16[32,1024]{1,0:T(8,128)(2,1)S(1)} %reduce_sum.42), channel_id=1, source_target_pairs={{0,256},{128,384},{16,272},{144,400},{32,288},{160,416},{48,304},{... | collective-permute-start | bytes 196616 | tf_op jit(solution)/shard_map/ppermute | solution.py:38
  152.1 7.1 %collective-permute-start.11 = (bf16[64,1024]{1,0:T(8,128)(2,1)S(1)}, bf16[64,1024]{1,0:T(8,128)(2,1)S(1)}, u32[]{:S(2)}, u32[]{:S(2)}) collective-permute-start(bf16[64,1024]{1,0:T(8,128)(2,1)S(1)} %maximum_select_fusion.2), channel_id=1, source_target_pairs={{0,128},{128,0},{16,144},{144,16},{32,160},{160,32},{48,176},{176,... | collective-permute-start | bytes 393224 | tf_op jit(solution)/shard_map/ppermute | solution.py:38

commit v2 on v1

--- a/solution.py
+++ b/solution.py
@@ -1,10 +1,16 @@
+import functools
+import math
+
 import jax
 import jax.numpy as jnp
 from jax import lax
+from jax.experimental import pallas as pl
+from jax.experimental.pallas import tpu as pltpu
 from jax.sharding import PartitionSpec as P
 
 ZLINE = ("tensor", "row")
 PAD = 128
+LOG2E = math.log2(math.e)
 
 
 def line_permutation(shift, n_row):
@@ -22,6 +28,84 @@
 
 def pick(second, low, high):
     return jnp.where(second, high, low)
+
+def tile_kernel(count, *refs):
+    f32, bf16 = jnp.float32, jnp.bfloat16
+    rates_ref, col_ref = refs[:2]
+    pieces, refs = refs[2 : 2 + count], refs[2 + count :]
+    last = len(refs) == 5
+    held, refs = (refs[:2], refs[2:]) if last else (None, refs)
+    outs, (rows_ref, signed_ref) = refs[:-2], refs[-2:]
+    width = col_ref.shape[1] - PAD
+    depth = pieces[0].shape[0]
+    n_rows = count * depth
+
+    turned = []
+    for index, piece in enumerate(pieces):
+        place = slice(index * depth, (index + 1) * depth)
+        sign = piece[:, width:]
+        square = jnp.zeros((depth, PAD), f32)
+        for at in range(0, width, PAD):
+            part = piece[:, at : at + PAD]
+            rows_ref[place, at : at + PAD] = part
+            signed_ref[place, at : at + PAD] = part * sign
+            square += jnp.square(part.astype(f32))
+        norm = jnp.sum(square, axis=1, keepdims=True)
+        lane = lax.broadcasted_iota(jnp.int32, (depth, PAD), 1)
+        turned.append(jnp.where(lane == 0, norm, sign.astype(f32)).T)
+    row_norm = jnp.concatenate([value[0:1] for value in turned], axis=1)
+    row_sign = jnp.concatenate([value[1:2] for value in turned], axis=1)
+
+    scales = [rates_ref[band] * (-LOG2E / width) for band in range(rates_ref.shape[0])]
+    step = min(128, col_ref.shape[0])
+    for start in range(0, col_ref.shape[0], step):
+        place = slice(start, start + step)
+        col_z = col_ref[place, :width]
+        wide = col_z.astype(f32)
+        col_norm = jnp.sum(jnp.square(wide), axis=1, keepdims=True)
+        cross = lax.dot_general(
+            col_z, rows_ref[...], (((1,), (1,)), ((), ())), preferred_element_type=f32
+        )
+        dist = jnp.maximum(col_norm + row_norm - 2.0 * cross, 0.0)
+        kernel = jnp.zeros((step, n_rows), f32)
+        for band, scale in enumerate(scales):
+            kernel += rates_ref[band] * jnp.exp2(scale * dist)
+        total = jnp.broadcast_to(jnp.sum(kernel * row_sign, axis=1, keepdims=True), (step, PAD))
+        other = jnp.dot(kernel.astype(bf16), signed_ref[...], preferred_element_type=f32)
+        if last:
+            total += held[0][place]
+            other += held[1][place]
+            factor = (-32.0 / width) * col_ref[place, width : width + 1].astype(f32)
+            outs[0][place] = (factor * (total[:, :1] * wide - other)).astype(bf16)
+        else:
+            outs[0][place] = total
+            outs[1][place] = other
+
+
+def tiles(pieces, col, rates, held=()):
+    f32, bf16 = jnp.float32, jnp.bfloat16
+    n_cols, width = col.shape[0], col.shape[1] - PAD
+    n_rows = sum(piece.shape[0] for piece in pieces)
+    vmem = pl.BlockSpec(memory_space=pltpu.VMEM)
+    if held:
+        out_shape = jax.ShapeDtypeStruct((n_cols, width), bf16)
+    else:
+        out_shape = (
+            jax.ShapeDtypeStruct((n_cols, PAD), f32),
+            jax.ShapeDtypeStruct((n_cols, width), f32),
+        )
+    pairs = n_rows * n_cols
+    return pl.pallas_call(
+        functools.partial(tile_kernel, len(pieces)),
+        out_shape=out_shape,
+        in_specs=[pl.BlockSpec(memory_space=pltpu.SMEM)] + [vmem] * (1 + len(pieces) + len(held)),
+        out_specs=vmem if held else (vmem, vmem),
+        scratch_shapes=[pltpu.VMEM((n_rows, width), bf16), pltpu.VMEM((n_rows, width), bf16)],
+        compiler_params=pltpu.CompilerParams(vmem_limit_bytes=32 * 2**20),
+        cost_estimate=pl.CostEstimate(
+            flops=4 * pairs * width, bytes_accessed=4 * n_cols * width, transcendentals=5 * pairs
+        ),
+    )(rates, col, *pieces, *held)
 
 
 def shards(features, w_proj, flags, rates):
@@ -51,31 +135,20 @@
     s_half = pick(core, signs[:half], signs[half:])
     block = jnp.concatenate([z_half, jnp.broadcast_to(s_half[:, None], (half, PAD))], axis=1)
 
-    blocks = [block]
-    for shift in range(1, n_row // 2 + 1):
-        blocks.append(move(block, lambda chip, core: (chip - shift, core)))
-        if shift < n_row // 2:
-            blocks.append(move(block, lambda chip, core: (chip + shift, core)))
+    far_block = move(block, lambda chip, core: (chip + (n_row // 2) * (1 - 2 * core), core))
+    pair = jnp.concatenate([block, far_block], axis=0)
+    near = [
+        pair,
+        move(pair, lambda chip, core: (chip + 1, core)),
+        move(pair, lambda chip, core: (chip - 1, core)),
+        move(pair, lambda chip, core: (chip + 2 - 4 * core, core)),
+    ]
     own = pick(high, block[:quarter], block[quarter:])
     col = lax.all_to_all(
         jnp.broadcast_to(own[None], (n_col,) + own.shape), "col", 0, 0, tiled=True
     ).reshape(n_col * quarter, width + PAD)
-    near = jnp.concatenate(blocks, axis=0)
-    rows = jnp.concatenate([near, other_core(near)], axis=0)
-    row_z, row_s = rows[:, :width], rows[:, width].astype(f32)
-    col_z, col_s = col[:, :width], col[:, width].astype(f32)
-
-    row_norm = jnp.sum(jnp.square(row_z.astype(f32)), axis=1)
-    col_norm = jnp.sum(jnp.square(col_z.astype(f32)), axis=1)
-    cross = lax.dot_general(col_z, row_z, (((1,), (1,)), ((), ())), preferred_element_type=f32)
-    dist = jnp.maximum(col_norm[:, None] + row_norm[None, :] - 2.0 * cross, 0.0) / width
-    kernel = jnp.zeros_like(dist)
-    for band in range(rates.shape[0]):
-        kernel = kernel + rates[band] * jnp.exp(-rates[band] * dist)
-    mixed = -16.0 / width * col_s[:, None] * row_s[None, :] * kernel
-    total = jnp.sum(mixed, axis=1)
-    other = jnp.dot(mixed.astype(bf16), row_z, preferred_element_type=f32)
-    part = (2.0 * (total[:, None] * col_z.astype(f32) - other)).astype(bf16)
+    sums = tiles(near, col, rates)
+    part = tiles([other_core(value) for value in near], col, rates, sums)
     parts = lax.all_to_all(part.reshape(n_col, quarter, width), "col", 0, 0, tiled=True)
     grad = jnp.sum(parts.astype(f32), axis=0).astype(bf16)
     grad_far = move(grad, lambda chip, core: (chip + n_row, core))

time: 162 us -> 143 us (0.88)
  the two profiles are of different devices: /device:TPU:33 before, /device:TPU:1 now
where the time goes in v2:
time: 143 us; the launch traced here: 142 us
  starting transfers between devices  79 us (55%)
  blocking collectives  22.5 us (16%)
  waiting for transfers between devices  18.7 us (13%)
  Pallas kernels  10.3 us (7%)
  matrix products  5.82 us (4%)
  local copies, waits for them, and re-layouts  3.08 us (2%)
  other arithmetic  2.34 us (2%)
    ppermute x12, starting transfers between devices, move(): return lax.ppermute(value, ZLINE, line_permutation(shift, n_row))  73.8 us
    all_to_all x1, blocking collectives, shards(): lax.all_to_all(part.reshape(n_col, quarter, width), 'col', 0, 0, tiled=True)  22.5 us
    ppermute x12, waiting for transfers between devices, move(): return lax.ppermute(value, ZLINE, line_permutation(shift, n_row))  18.7 us
    pallas_call x2, Pallas kernels, tiles(): pl.pallas_call(functools.partial(tile_kernel, len(pieces)), out_shape=out...  10.3 us
    all_to_all x1, starting transfers between devices, shards(): lax.all_to_all(jnp.broadcast_to(own[None], (n_col,) + own.shape), 'col',...  5.12 us
  transfers between devices with their start and end apart: 13, of which 5 were waited for; matrix products, arithmetic and copies ran while one was open for 1% of the time, Pallas kernels for 4%

profile of v2, /device:TPU:1, one launch (start us, length us, event | category | flops | bytes accessed | tf_op | source)
XLA Modules:
  0.0 142.1 jit_solution(11330157401693182152)
XLA Ops:
  0.0 1.9 %copy-done = bf16[1536,1024]{1,0:T(8,128)(2,1)S(1)} copy-done((bf16[1536,1024]{1,0:T(8,128)(2,1)S(1)}, bf16[1536,1024]{1,0:T(8,128)(2,1)}, u32[]{:S(2)}) %copy-start) | copy-done | bytes 3145752
  1.9 2.3 %convolution_convert_fusion.1 = bf16[64,1024]{1,0:T(8,128)(2,1)} fusion(bf16[1536,1024]{1,0:T(8,128)(2,1)S(1)} %copy-done, pred[]{:T(512)S(6)} %eq.8, bf16[128,1536]{1,0:T(8,128)(2,1)} %param.4), kind=kOutput, calls=%fused_computation.1 | convolution fusion | flops 201490432 | bytes 3670017 | tf_op jit(solution)/shard_map/dot_general | solution.py:129
  4.2 8.8 %collective-permute-start = (bf16[64,1024]{1,0:T(8,128)(2,1)}, bf16[64,1024]{1,0:T(8,128)(2,1)}, u32[]{:S(2)}, u32[]{:S(2)}) collective-permute-start(bf16[64,1024]{1,0:T(8,128)(2,1)} %convolution_convert_fusion.1), channel_id=1, source_target_pairs={{0,128},{128,0},{16,144},{144,16},{32,160},{160,32},{48,176},{176,... | collective-permute-start | bytes 393224 | tf_op jit(solution)/shard_map/ppermute | solution.py:122
  13.1 1.3 collective-permute-done
  14.3 1.6 %add_convert_fusion.1 = bf16[64,1024]{1,0:T(8,128)(2,1)S(1)} fusion(bf16[64,1024]{1,0:T(8,128)(2,1)} %collective-permute-done, bf16[1536,1024]{1,0:T(8,128)(2,1)S(1)} %copy-done, pred[]{:T(512)S(6)} %eq.8, bf16[128,1536]{1,0:T(8,128)(2,1)S(1)} %copy-done.2), kind=kOutput, calls=%fused_computation.10 | convolution fusion | flops 201621504 | bytes 3801089 | tf_op jit(solution)/shard_map/dot_general | solution.py:130
  15.9 0.0 copy-start.1
  15.9 10.1 %collective-permute-start.1 = (bf16[64,1024]{1,0:T(8,128)(2,1)S(1)}, bf16[64,1024]{1,0:T(8,128)(2,1)S(1)}, u32[]{:S(2)}, u32[]{:S(2)}) collective-permute-start(bf16[64,1024]{1,0:T(8,128)(2,1)S(1)} %add_convert_fusion.1), channel_id=1, source_target_pairs={{0,256},{128,384},{16,272},{144,400},{32,288},{160,416},{48,304},{... | collective-permute-start | bytes 393224 | tf_op jit(solution)/shard_map/ppermute | solution.py:122
  26.0 0.1 broadcast_select_fusion
  26.1 5.2 %collective-permute-done.1 = bf16[64,1024]{1,0:T(8,128)(2,1)S(1)} collective-permute-done((bf16[64,1024]{1,0:T(8,128)(2,1)S(1)}, bf16[64,1024]{1,0:T(8,128)(2,1)S(1)}, u32[]{:S(2)}, u32[]{:S(2)}) %collective-permute-start.1) | collective-permute-done | bytes 131104 | tf_op jit(solution)/shard_map/ppermute | solution.py:122
  31.3 0.1 broadcast_in_dim.4
  31.4 1.1 broadcast_in_dim.5
  32.5 5.1 %all-to-all-start = ((bf16[16,32,1152]{2,1,0:T(8,128)(2,1)}), bf16[16,32,1152]{2,1,0:T(8,128)(2,1)}, u32[]{:S(2)}, u32[]{:S(2)}) async-start(bf16[16,32,1152]{2,1,0:T(8,128)(2,1)} %broadcast_in_dim.5), calls=%async_computation | async-start | bytes 2359296 | tf_op jit(solution)/shard_map/all_to_all | solution.py:147
  37.7 8.8 %collective-permute-start.2 = (bf16[64,1152]{1,0:T(8,128)(2,1)S(1)}, bf16[64,1152]{1,0:T(8,128)(2,1)S(1)}, u32[]{:S(2)}, u32[]{:S(2)}) collective-permute-start(bf16[64,1152]{1,0:T(8,128)(2,1)S(1)} %pad_maximum_fusion.1), channel_id=1, source_target_pairs={{0,64},{128,448},{16,80},{144,464},{32,96},{160,480},{48,112},{176... | collective-permute-start | bytes 442376 | tf_op jit(solution)/shard_map/ppermute | solution.py:122
  46.4 5.7 %collective-permute-done.2 = bf16[64,1152]{1,0:T(8,128)(2,1)S(1)} collective-permute-done((bf16[64,1152]{1,0:T(8,128)(2,1)S(1)}, bf16[64,1152]{1,0:T(8,128)(2,1)S(1)}, u32[]{:S(2)}, u32[]{:S(2)}) %collective-permute-start.2) | collective-permute-done | bytes 147488 | tf_op jit(solution)/shard_map/ppermute | solution.py:122
  52.1 0.7 pad_maximum_fusion.refs_2_
  52.9 9.6 %collective-permute-start.4 = (bf16[128,1152]{1,0:T(8,128)(2,1)}, bf16[128,1152]{1,0:T(8,128)(2,1)}, u32[]{:S(2)}, u32[]{:S(2)}) collective-permute-start(bf16[128,1152]{1,0:T(8,128)(2,1)} %pad_maximum_fusion.refs_2_), channel_id=1, source_target_pairs={{0,16},{128,144},{16,32},{144,160},{32,48},{160,176},{48,64},{176,... | collective-permute-start | bytes 884744 | tf_op jit(solution)/shard_map/ppermute | solution.py:122
  62.5 1.9 %collective-permute-start.6 = (bf16[128,1152]{1,0:T(8,128)(2,1)}, bf16[128,1152]{1,0:T(8,128)(2,1)}, u32[]{:S(2)}, u32[]{:S(2)}) collective-permute-start(bf16[128,1152]{1,0:T(8,128)(2,1)} %pad_maximum_fusion.refs_2_), channel_id=1, source_target_pairs={{0,368},{128,496},{16,0},{144,128},{32,16},{160,144},{48,32},{176,... | collective-permute-start | bytes 884744 | tf_op jit(solution)/shard_map/ppermute | solution.py:122
  64.4 7.3 %collective-permute-start.8 = (bf16[128,1152]{1,0:T(8,128)(2,1)}, bf16[128,1152]{1,0:T(8,128)(2,1)}, u32[]{:S(2)}, u32[]{:S(2)}) collective-permute-start(bf16[128,1152]{1,0:T(8,128)(2,1)} %pad_maximum_fusion.refs_2_), channel_id=1, source_target_pairs={{0,32},{128,480},{16,48},{144,496},{32,64},{160,128},{48,80},{176,... | collective-permute-start | bytes 884744 | tf_op jit(solution)/shard_map/ppermute | solution.py:122
  71.7 2.9 %collective-permute-start.3 = (bf16[128,1152]{1,0:T(8,128)(2,1)}, bf16[128,1152]{1,0:T(8,128)(2,1)S(1)}, u32[]{:S(2)}, u32[]{:S(2)}) collective-permute-start(bf16[128,1152]{1,0:T(8,128)(2,1)} %pad_maximum_fusion.refs_2_), channel_id=1, source_target_pairs={{0,128},{128,0},{16,144},{144,16},{32,160},{160,32},{48,176},{176,... | collective-permute-start | bytes 884744 | tf_op jit(solution)/shard_map/ppermute | solution.py:122
  74.6 1.9 %collective-permute-start.5 = (bf16[128,1152]{1,0:T(8,128)(2,1)}, bf16[128,1152]{1,0:T(8,128)(2,1)}, u32[]{:S(2)}, u32[]{:S(2)}) collective-permute-start(bf16[128,1152]{1,0:T(8,128)(2,1)} %collective-permute-done.4.refs_3_), channel_id=1, source_target_pairs={{0,128},{128,0},{16,144},{144,16},{32,160},{160,32},{48,176},{176,... | collective-permute-start | bytes 884744 | tf_op jit(solution)/shard_map/ppermute | solution.py:122
  76.5 4.7 %collective-permute-start.7 = (bf16[128,1152]{1,0:T(8,128)(2,1)}, bf16[128,1152]{1,0:T(8,128)(2,1)}, u32[]{:S(2)}, u32[]{:S(2)}) collective-permute-start(bf16[128,1152]{1,0:T(8,128)(2,1)} %collective-permute-done.6.refs_4_), channel_id=1, source_target_pairs={{0,128},{128,0},{16,144},{144,16},{32,160},{160,32},{48,176},{176,... | collective-permute-start | bytes 884744 | tf_op jit(solution)/shard_map/ppermute | solution.py:122
  81.2 0.0 collective-permute-done.8.refs_5_
  81.2 3.8 %collective-permute-start.9 = (bf16[128,1152]{1,0:T(8,128)(2,1)}, bf16[128,1152]{1,0:T(8,128)(2,1)}, u32[]{:S(2)}, u32[]{:S(2)}) collective-permute-start(bf16[128,1152]{1,0:T(8,128)(2,1)} %collective-permute-done.8.refs_5_), channel_id=1, source_target_pairs={{0,128},{128,0},{16,144},{144,16},{32,160},{160,32},{48,176},{176,... | collective-permute-start | bytes 884744 | tf_op jit(solution)/shard_map/ppermute | solution.py:122
  85.0 5.2 %shard_map.46 = (f32[512,128]{1,0:T(8,128)S(1)}, f32[512,1024]{1,0:T(8,128)S(1)}) custom-call(f32[5]{0:T(128)S(1)} %copy-done.1, bf16[512,1152]{1,0:T(8,128)(2,1)} %bitcast.refs_1_, bf16[128,1152]{1,0:T(8,128)(2,1)} %pad_maximum_fusion.refs_2_, bf16[128,1152]{1,0:T(8,128)(2,1)} %collective-permute-done.4.refs_3_, ...), custom_call_target="tpu_custom_call" | custom-call | flops 1073741824 | bytes 2097152 | tf_op jit(solution)/shard_map/pallas_call | solution.py:98
  90.2 5.2 %shard_map.47 = bf16[512,1024]{1,0:T(8,128)(2,1)S(1)} custom-call(f32[5]{0:T(128)S(1)} %copy-done.1, bf16[512,1152]{1,0:T(8,128)(2,1)} %bitcast.refs_1_, bf16[128,1152]{1,0:T(8,128)(2,1)S(1)} %collective-permute-done.3.refs_2_, bf16[128,1152]{1,0:T(8,128)(2,1)} %collective-permute-done.5.refs_3_, bf16[128,1152]{1,0:T(8,128)(2,1)} %collective-permute-done.7.refs_4_, ...), custom_call_target="tpu_custom_call" | custom-call | flops 1073741824 | bytes 2097152 | tf_op jit(solution)/shard_map/pallas_call | solution.py:98
  95.4 22.5 %all_to_all.10 = bf16[16,32,1024]{2,1,0:T(8,128)(2,1)} all-to-all(bf16[16,32,1024]{2,1,0:T(8,128)(2,1)S(1)} %bitcast.5), channel_id=1, replica_groups=mesh['tensor'=4,'row'=8,'col'=16] {'col'}, dimensions={0} | all-to-all | bytes 2097152 | tf_op jit(solution)/shard_map/all_to_all | solution.py:152
  117.9 1.4 reduce_sum.12
  119.4 8.2 %collective-permute-start.10 = (bf16[32,1024]{1,0:T(8,128)(2,1)S(1)}, bf16[32,1024]{1,0:T(8,128)(2,1)S(1)}, u32[]{:S(2)}, u32[]{:S(2)}) collective-permute-start(bf16[32,1024]{1,0:T(8,128)(2,1)S(1)} %reduce_sum.12), channel_id=1, source_target_pairs={{0,256},{128,384},{16,272},{144,400},{32,288},{160,416},{48,304},{... | collective-permute-start | bytes 196616 | tf_op jit(solution)/shard_map/ppermute | solution.py:122
  127.6 5.6 %collective-permute-done.10 = bf16[32,1024]{1,0:T(8,128)(2,1)S(1)} collective-permute-done((bf16[32,1024]{1,0:T(8,128)(2,1)S(1)}, bf16[32,1024]{1,0:T(8,128)(2,1)S(1)}, u32[]{:S(2)}, u32[]{:S(2)}) %collective-permute-start.10) | collective-permute-done | bytes 65568 | tf_op jit(solution)/shard_map/ppermute | solution.py:122
  133.2 6.0 %collective-permute-start.11 = (bf16[64,1024]{1,0:T(8,128)(2,1)S(1)}, bf16[64,1024]{1,0:T(8,128)(2,1)S(1)}, u32[]{:S(2)}, u32[]{:S(2)}) collective-permute-start(bf16[64,1024]{1,0:T(8,128)(2,1)S(1)} %maximum_select_fusion.2), channel_id=1, source_target_pairs={{0,128},{128,0},{16,144},{144,16},{32,160},{160,32},{48,176},{176,... | collective-permute-start | bytes 393224 | tf_op jit(solution)/shard_map/ppermute | solution.py:122
  139.2 1.0 collective-permute-done.11
  140.2 1.9 %convolution_convert_fusion = bf16[128,1536]{1,0:T(8,128)(2,1)} fusion(bf16[1536,1024]{1,0:T(8,128)(2,1)S(1)} %copy-done, bf16[64,1024]{1,0:T(8,128)(2,1)S(1)} %maximum_select_fusion.2, bf16[64,1024]{1,0:T(8,128)(2,1)S(1)} %collective-permute-done.11, pred[]{:T(512)S(6)} %eq.8), kind=kOutput, calls=%fused_computation | convolution fusion | flops 404029440 | bytes 3801089 | tf_op jit(solution)/shard_map/dot_general | solution.py:164
  (18 shorter events, 0.1 us)
Async XLA Ops:
  0.0 1.9 %copy-start = (bf16[1536,1024]{1,0:T(8,128)(2,1)S(1)}, bf16[1536,1024]{1,0:T(8,128)(2,1)}, u32[]{:S(2)}) copy-start(bf16[1536,1024]{1,0:T(8,128)(2,1)} %param.5) | copy-start | bytes 9437188
  0.0 14.3 %copy-start.2 = (bf16[128,1536]{1,0:T(8,128)(2,1)S(1)}, bf16[128,1536]{1,0:T(8,128)(2,1)}, u32[]{:S(2)}) copy-start(bf16[128,1536]{1,0:T(8,128)(2,1)} %param.4) | copy-start | bytes 1179652
  0.0 13.0 %copy-start.3 = (s32[128]{0:T(128)S(1)}, s32[128]{0:T(128)}, u32[]{:S(2)}) copy-start(s32[128]{0:T(128)} %param.6) | copy-start | bytes 1540
  4.2 10.1 %collective-permute-start = (bf16[64,1024]{1,0:T(8,128)(2,1)}, bf16[64,1024]{1,0:T(8,128)(2,1)}, u32[]{:S(2)}, u32[]{:S(2)}) collective-permute-start(bf16[64,1024]{1,0:T(8,128)(2,1)} %convolution_convert_fusion.1), channel_id=1, source_target_pairs={{0,128},{128,0},{16,144},{144,16},{32,160},{160,32},{48,176},{176,... | collective-permute-start | bytes 393224 | tf_op jit(solution)/shard_map/ppermute | solution.py:122
  15.9 69.1 %copy-start.1 = (f32[5]{0:T(128)S(1)}, f32[5]{0:T(128)}, u32[]{:S(2)}) copy-start(f32[5]{0:T(128)} %refs_0_.3) | copy-start | bytes 64
  15.9 15.3 %collective-permute-start.1 = (bf16[64,1024]{1,0:T(8,128)(2,1)S(1)}, bf16[64,1024]{1,0:T(8,128)(2,1)S(1)}, u32[]{:S(2)}, u32[]{:S(2)}) collective-permute-start(bf16[64,1024]{1,0:T(8,128)(2,1)S(1)} %add_convert_fusion.1), channel_id=1, source_target_pairs={{0,256},{128,384},{16,272},{144,400},{32,288},{160,416},{48,304},{... | collective-permute-start | bytes 393224 | tf_op jit(solution)/shard_map/ppermute | solution.py:122
  32.5 52.5 %all-to-all-start = ((bf16[16,32,1152]{2,1,0:T(8,128)(2,1)}), bf16[16,32,1152]{2,1,0:T(8,128)(2,1)}, u32[]{:S(2)}, u32[]{:S(2)}) async-start(bf16[16,32,1152]{2,1,0:T(8,128)(2,1)} %broadcast_in_dim.5), calls=%async_computation | async-start | bytes 2359296 | tf_op jit(solution)/shard_map/all_to_all | solution.py:147
  37.7 14.5 %collective-permute-start.2 = (bf16[64,1152]{1,0:T(8,128)(2,1)S(1)}, bf16[64,1152]{1,0:T(8,128)(2,1)S(1)}, u32[]{:S(2)}, u32[]{:S(2)}) collective-permute-start(bf16[64,1152]{1,0:T(8,128)(2,1)S(1)} %pad_maximum_fusion.1), channel_id=1, source_target_pairs={{0,64},{128,448},{16,80},{144,464},{32,96},{160,480},{48,112},{176... | collective-permute-start | bytes 442376 | tf_op jit(solution)/shard_map/ppermute | solution.py:122
  52.9 21.7 %collective-permute-start.4 = (bf16[128,1152]{1,0:T(8,128)(2,1)}, bf16[128,1152]{1,0:T(8,128)(2,1)}, u32[]{:S(2)}, u32[]{:S(2)}) collective-permute-start(bf16[128,1152]{1,0:T(8,128)(2,1)} %pad_maximum_fusion.refs_2_), channel_id=1, source_target_pairs={{0,16},{128,144},{16,32},{144,160},{32,48},{160,176},{48,64},{176,... | collective-permute-start | bytes 884744 | tf_op jit(solution)/shard_map/ppermute | solution.py:122
  62.5 14.0 %collective-permute-start.6 = (bf16[128,1152]{1,0:T(8,128)(2,1)}, bf16[128,1152]{1,0:T(8,128)(2,1)}, u32[]{:S(2)}, u32[]{:S(2)}) collective-permute-start(bf16[128,1152]{1,0:T(8,128)(2,1)} %pad_maximum_fusion.refs_2_), channel_id=1, source_target_pairs={{0,368},{128,496},{16,0},{144,128},{32,16},{160,144},{48,32},{176,... | collective-permute-start | bytes 884744 | tf_op jit(solution)/shard_map/ppermute | solution.py:122
  64.4 16.8 %collective-permute-start.8 = (bf16[128,1152]{1,0:T(8,128)(2,1)}, bf16[128,1152]{1,0:T(8,128)(2,1)}, u32[]{:S(2)}, u32[]{:S(2)}) collective-permute-start(bf16[128,1152]{1,0:T(8,128)(2,1)} %pad_maximum_fusion.refs_2_), channel_id=1, source_target_pairs={{0,32},{128,480},{16,48},{144,496},{32,64},{160,128},{48,80},{176,... | collective-permute-start | bytes 884744 | tf_op jit(solution)/shard_map/ppermute | solution.py:122
  71.7 18.5 %collective-permute-start.3 = (bf16[128,1152]{1,0:T(8,128)(2,1)}, bf16[128,1152]{1,0:T(8,128)(2,1)S(1)}, u32[]{:S(2)}, u32[]{:S(2)}) collective-permute-start(bf16[128,1152]{1,0:T(8,128)(2,1)} %pad_maximum_fusion.refs_2_), channel_id=1, source_target_pairs={{0,128},{128,0},{16,144},{144,16},{32,160},{160,32},{48,176},{176,... | collective-permute-start | bytes 884744 | tf_op jit(solution)/shard_map/ppermute | solution.py:122
  74.6 15.6 %collective-permute-start.5 = (bf16[128,1152]{1,0:T(8,128)(2,1)}, bf16[128,1152]{1,0:T(8,128)(2,1)}, u32[]{:S(2)}, u32[]{:S(2)}) collective-permute-start(bf16[128,1152]{1,0:T(8,128)(2,1)} %collective-permute-done.4.refs_3_), channel_id=1, source_target_pairs={{0,128},{128,0},{16,144},{144,16},{32,160},{160,32},{48,176},{176,... | collective-permute-start | bytes 884744 | tf_op jit(solution)/shard_map/ppermute | solution.py:122
  76.5 13.7 %collective-permute-start.7 = (bf16[128,1152]{1,0:T(8,128)(2,1)}, bf16[128,1152]{1,0:T(8,128)(2,1)}, u32[]{:S(2)}, u32[]{:S(2)}) collective-permute-start(bf16[128,1152]{1,0:T(8,128)(2,1)} %collective-permute-done.6.refs_4_), channel_id=1, source_target_pairs={{0,128},{128,0},{16,144},{144,16},{32,160},{160,32},{48,176},{176,... | collective-permute-start | bytes 884744 | tf_op jit(solution)/shard_map/ppermute | solution.py:122
  81.2 9.0 %collective-permute-start.9 = (bf16[128,1152]{1,0:T(8,128)(2,1)}, bf16[128,1152]{1,0:T(8,128)(2,1)}, u32[]{:S(2)}, u32[]{:S(2)}) collective-permute-start(bf16[128,1152]{1,0:T(8,128)(2,1)} %collective-permute-done.8.refs_5_), channel_id=1, source_target_pairs={{0,128},{128,0},{16,144},{144,16},{32,160},{160,32},{48,176},{176,... | collective-permute-start | bytes 884744 | tf_op jit(solution)/shard_map/ppermute | solution.py:122
  119.4 13.8 %collective-permute-start.10 = (bf16[32,1024]{1,0:T(8,128)(2,1)S(1)}, bf16[32,1024]{1,0:T(8,128)(2,1)S(1)}, u32[]{:S(2)}, u32[]{:S(2)}) collective-permute-start(bf16[32,1024]{1,0:T(8,128)(2,1)S(1)} %reduce_sum.12), channel_id=1, source_target_pairs={{0,256},{128,384},{16,272},{144,400},{32,288},{160,416},{48,304},{... | collective-permute-start | bytes 196616 | tf_op jit(solution)/shard_map/ppermute | solution.py:122
  133.2 6.9 %collective-permute-start.11 = (bf16[64,1024]{1,0:T(8,128)(2,1)S(1)}, bf16[64,1024]{1,0:T(8,128)(2,1)S(1)}, u32[]{:S(2)}, u32[]{:S(2)}) collective-permute-start(bf16[64,1024]{1,0:T(8,128)(2,1)S(1)} %maximum_select_fusion.2), channel_id=1, source_target_pairs={{0,128},{128,0},{16,144},{144,16},{32,160},{160,32},{48,176},{176,... | collective-permute-start | bytes 393224 | tf_op jit(solution)/shard_map/ppermute | solution.py:122

commit v3 on v2

--- a/solution.py
+++ b/solution.py
@@ -11,6 +11,7 @@
 ZLINE = ("tensor", "row")
 PAD = 128
 LOG2E = math.log2(math.e)
+FLOPS = 4 * 10**10
 
 
 def line_permutation(shift, n_row):
@@ -28,6 +29,81 @@
 
 def pick(second, low, high):
     return jnp.where(second, high, low)
+
+CHUNKS = 4
+
+
+def projection_kernel(core_ref, features_ref, w_ref, away_ref, kept_ref, rows, weights, total, sem):
+    copies = []
+    depth = rows.shape[1] // CHUNKS
+    for index in range(CHUNKS):
+        place = pl.ds(index * depth, depth)
+        copies.append(
+            (
+                pltpu.make_async_copy(features_ref.at[:, place], rows.at[:, place], sem.at[0, index]),
+                pltpu.make_async_copy(w_ref.at[place], weights.at[place], sem.at[1, index]),
+            )
+        )
+        for copy in copies[-1]:
+            copy.start()
+    value = None
+    for index in range(CHUNKS):
+        place = slice(index * depth, (index + 1) * depth)
+        for copy in copies[index]:
+            copy.wait()
+        term = jnp.dot(rows[:, place], weights[place], preferred_element_type=jnp.float32)
+        value = term if value is None else value + term
+    total[...] = value
+    half = kept_ref.shape[0]
+    core = core_ref[0]
+    away = total[pl.ds(pl.multiple_of((1 - core) * half, half), half)]
+    away_ref[...] = away.astype(away_ref.dtype)
+    kept_ref[...] = total[pl.ds(pl.multiple_of(core * half, half), half)]
+
+
+def projection(core, features, w_proj):
+    rows, width = features.shape[0], w_proj.shape[1]
+    vmem, anywhere = pl.BlockSpec(memory_space=pltpu.VMEM), pl.BlockSpec(memory_space=pl.ANY)
+    return pl.pallas_call(
+        projection_kernel,
+        out_shape=(
+            jax.ShapeDtypeStruct((rows // 2, width), jnp.bfloat16),
+            jax.ShapeDtypeStruct((rows // 2, width), jnp.float32),
+        ),
+        in_specs=[pl.BlockSpec(memory_space=pltpu.SMEM), anywhere, anywhere],
+        out_specs=(vmem, vmem),
+        scratch_shapes=[
+            pltpu.VMEM(features.shape, features.dtype),
+            pltpu.VMEM(w_proj.shape, w_proj.dtype),
+            pltpu.VMEM((rows, width), jnp.float32),
+            pltpu.SemaphoreType.DMA((2, CHUNKS)),
+        ],
+        compiler_params=pltpu.CompilerParams(vmem_limit_bytes=60 * 2**20),
+        cost_estimate=pl.CostEstimate(
+            flops=2 * rows * width * w_proj.shape[0],
+            bytes_accessed=2 * w_proj.shape[0] * width,
+            transcendentals=0,
+        ),
+    )(core, features, w_proj)
+
+
+def pair_kernel(first_ref, second_ref, out_ref):
+    half = first_ref.shape[0]
+    out_ref[:half] = first_ref[...]
+    out_ref[half:] = second_ref[...]
+
+
+def side_by_side(first, second):
+    vmem = pl.BlockSpec(memory_space=pltpu.VMEM)
+    return pl.pallas_call(
+        pair_kernel,
+        out_shape=jax.ShapeDtypeStruct((2 * first.shape[0], first.shape[1]), first.dtype),
+        in_specs=[vmem, vmem],
+        out_specs=vmem,
+        compiler_params=pltpu.CompilerParams(vmem_limit_bytes=16 * 2**20),
+        cost_estimate=pl.CostEstimate(flops=FLOPS, bytes_accessed=0, transcendentals=0),
+    )(first, second)
+
 
 def tile_kernel(count, *refs):
     f32, bf16 = jnp.float32, jnp.bfloat16
@@ -57,7 +133,7 @@
     row_sign = jnp.concatenate([value[1:2] for value in turned], axis=1)
 
     scales = [rates_ref[band] * (-LOG2E / width) for band in range(rates_ref.shape[0])]
-    step = min(128, col_ref.shape[0])
+    step = min(256, col_ref.shape[0])
     for start in range(0, col_ref.shape[0], step):
         place = slice(start, start + step)
         col_z = col_ref[place, :width]
@@ -124,11 +200,8 @@
     def other_core(value):
         return move(value, lambda chip, core: (chip, 1 - core))
 
-    away = pick(core, features[half:], features[:half])
-    mine = pick(core, features[:half], features[half:])
-    sent = other_core(jnp.dot(away, w_proj, preferred_element_type=f32).astype(bf16))
-    kept = jnp.dot(mine, w_proj, preferred_element_type=f32)
-    partial = (kept + sent.astype(f32)).astype(bf16)
+    away, kept = projection(jnp.reshape(tpos % 2, (1,)), features, w_proj)
+    partial = (kept + other_core(away).astype(f32)).astype(bf16)
     far = move(partial, lambda chip, core: (chip + n_row, core))
     z_half = (partial.astype(f32) + far.astype(f32)).astype(bf16)
     signs = (1 - 2 * flags).astype(bf16)
@@ -136,7 +209,7 @@
     block = jnp.concatenate([z_half, jnp.broadcast_to(s_half[:, None], (half, PAD))], axis=1)
 
     far_block = move(block, lambda chip, core: (chip + (n_row // 2) * (1 - 2 * core), core))
-    pair = jnp.concatenate([block, far_block], axis=0)
+    pair = side_by_side(block, far_block)
     near = [
         pair,
         move(pair, lambda chip, core: (chip + 1, core)),

time: 143 us -> 128 us (0.90)
  starting transfers between devices: 79 us -> 70.9 us
  matrix products: 5.82 us -> 3.81 us
  local copies, waits for them, and re-layouts: 3.08 us -> 1.2 us
    ppermute x12, starting transfers between devices: 73.8 us -> 64.2 us  [move(): return lax.ppermute(value, ZLINE, line_permutation(shift, n_row))]
    dot_general x2 -> x0, matrix products: 3.91 us -> none  [the longest x1 2.34 us: shards(): jnp.dot(away, w_proj, preferred_element_type=f32).astype(bf16)]
    pallas_call x2, Pallas kernels: 10.3 us -> 6.47 us  [tiles(): pl.pallas_call(functools.partial(tile_kernel, len(pieces)), out_shape=out...]
    pallas_call x0 -> x2, Pallas kernels: none -> 3.18 us  [the longest x1 3.15 us: projection(): pl.pallas_call(projection_kernel, out_shape=(jax.ShapeDtypeStruct((rows /...]
    dot_general x1, matrix products: 1.91 us -> 3.81 us  [shards(): lax.dot_general(grad, w_proj, (((1,), (1,)), ((), ())), preferred_element...]
    unnamed x8 -> x4, local copies, waits for them, and re-layouts: 1.9 us -> 0.01 us
    all_to_all x1, starting transfers between devices: 5.12 us -> 6.74 us  [shards(): lax.all_to_all(jnp.broadcast_to(own[None], (n_col,) + own.shape), 'col',...]
  transfers between devices with their start and end apart: 13 -> 13, of which waited for: 5 -> 5; matrix products, arithmetic and copies ran while one was open for 1% -> 1% of each run, Pallas kernels for 4% -> 2%
where the time goes in v3:
time: 128 us
  starting transfers between devices  70.9 us (55%)
  blocking collectives  22.3 us (17%)
  waiting for transfers between devices  18.2 us (14%)
  Pallas kernels  9.65 us (8%)
  matrix products  3.81 us (3%)
  other arithmetic  1.35 us (1%)
    ppermute x12, starting transfers between devices, move(): return lax.ppermute(value, ZLINE, line_permutation(shift, n_row))  64.2 us
    all_to_all x1, blocking collectives, shards(): lax.all_to_all(part.reshape(n_col, quarter, width), 'col', 0, 0, tiled=True)  22.3 us
    ppermute x12, waiting for transfers between devices, move(): return lax.ppermute(value, ZLINE, line_permutation(shift, n_row))  18.2 us
    all_to_all x1, starting transfers between devices, shards(): lax.all_to_all(jnp.broadcast_to(own[None], (n_col,) + own.shape), 'col',...  6.74 us
    pallas_call x2, Pallas kernels, tiles(): pl.pallas_call(functools.partial(tile_kernel, len(pieces)), out_shape=out...  6.47 us
    dot_general x1, matrix products, shards(): lax.dot_general(grad, w_proj, (((1,), (1,)), ((), ())), preferred_element...  3.81 us
    pallas_call x1, Pallas kernels, projection(): pl.pallas_call(projection_kernel, out_shape=(jax.ShapeDtypeStruct((rows /...  3.15 us
  transfers between devices with their start and end apart: 13, of which 5 were waited for; matrix products, arithmetic and copies ran while one was open for 1% of the time, Pallas kernels for 2%

profile of v3, /device:TPU:1, one launch (start us, length us, event | category | flops | bytes accessed | tf_op | source)
XLA Modules:
  0.0 127.8 jit_solution(9419260775675540285)
XLA Ops:
  0.0 3.2 %shard_map.46 = (bf16[64,1024]{1,0:T(8,128)(2,1)}, f32[64,1024]{1,0:T(8,128)}) custom-call(s32[1]{0:T(128)} %bitcast.core_ref, bf16[128,1536]{1,0:T(8,128)(2,1)} %features_ref.1, bf16[1536,1024]{1,0:T(8,128)(2,1)} %w_ref.1), custom_call_target="tpu_custom_call" | custom-call | flops 402653184 | bytes 3145728 | tf_op jit(solution)/shard_map/pallas_call | solution.py:67
  3.2 8.8 %collective-permute-start = (bf16[64,1024]{1,0:T(8,128)(2,1)}, bf16[64,1024]{1,0:T(8,128)(2,1)S(1)}, u32[]{:S(2)}, u32[]{:S(2)}) collective-permute-start(bf16[64,1024]{1,0:T(8,128)(2,1)} %get-tuple-element.10), channel_id=1, source_target_pairs={{0,128},{128,0},{16,144},{144,16},{32,160},{160,32},{48,176},{176,... | collective-permute-start | bytes 393224 | tf_op jit(solution)/shard_map/ppermute | solution.py:198
  12.0 1.1 collective-permute-done
  13.1 1.0 add_convert_fusion.1
  14.1 10.1 %collective-permute-start.1 = (bf16[64,1024]{1,0:T(8,128)(2,1)S(1)}, bf16[64,1024]{1,0:T(8,128)(2,1)S(1)}, u32[]{:S(2)}, u32[]{:S(2)}) collective-permute-start(bf16[64,1024]{1,0:T(8,128)(2,1)S(1)} %add_convert_fusion.1), channel_id=1, source_target_pairs={{0,256},{128,384},{16,272},{144,400},{32,288},{160,416},{48,304},{... | collective-permute-start | bytes 393224 | tf_op jit(solution)/shard_map/ppermute | solution.py:198
  24.2 0.1 broadcast_select_fusion
  24.3 5.2 %collective-permute-done.1 = bf16[64,1024]{1,0:T(8,128)(2,1)S(1)} collective-permute-done((bf16[64,1024]{1,0:T(8,128)(2,1)S(1)}, bf16[64,1024]{1,0:T(8,128)(2,1)S(1)}, u32[]{:S(2)}, u32[]{:S(2)}) %collective-permute-start.1) | collective-permute-done | bytes 131104 | tf_op jit(solution)/shard_map/ppermute | solution.py:198
  29.5 0.1 broadcast_in_dim.4
  29.6 7.1 %collective-permute-start.2 = (bf16[64,1152]{1,0:T(8,128)(2,1)S(1)}, bf16[64,1152]{1,0:T(8,128)(2,1)S(1)}, u32[]{:S(2)}, u32[]{:S(2)}) collective-permute-start(bf16[64,1152]{1,0:T(8,128)(2,1)S(1)} %pad_maximum_fusion.first_ref), channel_id=1, source_target_pairs={{0,64},{128,448},{16,80},{144,464},{32,96},{160,480},{48,112},{176... | collective-permute-start | bytes 442376 | tf_op jit(solution)/shard_map/ppermute | solution.py:198
  36.7 1.1 broadcast_in_dim.5
  37.8 6.7 %all-to-all-start = ((bf16[16,32,1152]{2,1,0:T(8,128)(2,1)}), bf16[16,32,1152]{2,1,0:T(8,128)(2,1)S(1)}, u32[]{:S(2)}, u32[]{:S(2)}) async-start(bf16[16,32,1152]{2,1,0:T(8,128)(2,1)} %broadcast_in_dim.5), calls=%async_computation | async-start | bytes 2359296 | tf_op jit(solution)/shard_map/all_to_all | solution.py:220
  44.6 0.0 copy-start
  44.6 0.0 collective-permute-done.2.second_ref
  44.6 7.3 %collective-permute-start.4 = (bf16[128,1152]{1,0:T(8,128)(2,1)S(1)}, bf16[128,1152]{1,0:T(8,128)(2,1)S(1)}, u32[]{:S(2)}, u32[]{:S(2)}) collective-permute-start(bf16[128,1152]{1,0:T(8,128)(2,1)S(1)} %shard_map.47.refs_2_), channel_id=1, source_target_pairs={{0,16},{128,144},{16,32},{144,160},{32,48},{160,176},{48,64},{176,... | collective-permute-start | bytes 884744 | tf_op jit(solution)/shard_map/ppermute | solution.py:198
  52.0 1.9 %collective-permute-start.6 = (bf16[128,1152]{1,0:T(8,128)(2,1)S(1)}, bf16[128,1152]{1,0:T(8,128)(2,1)S(1)}, u32[]{:S(2)}, u32[]{:S(2)}) collective-permute-start(bf16[128,1152]{1,0:T(8,128)(2,1)S(1)} %shard_map.47.refs_2_), channel_id=1, source_target_pairs={{0,368},{128,496},{16,0},{144,128},{32,16},{160,144},{48,32},{176,... | collective-permute-start | bytes 884744 | tf_op jit(solution)/shard_map/ppermute | solution.py:198
  53.9 7.9 %collective-permute-start.8 = (bf16[128,1152]{1,0:T(8,128)(2,1)S(1)}, bf16[128,1152]{1,0:T(8,128)(2,1)S(1)}, u32[]{:S(2)}, u32[]{:S(2)}) collective-permute-start(bf16[128,1152]{1,0:T(8,128)(2,1)S(1)} %shard_map.47.refs_2_), channel_id=1, source_target_pairs={{0,32},{128,480},{16,48},{144,496},{32,64},{160,128},{48,80},{176,... | collective-permute-start | bytes 884744 | tf_op jit(solution)/shard_map/ppermute | solution.py:198
  61.9 1.9 %collective-permute-start.3 = (bf16[128,1152]{1,0:T(8,128)(2,1)S(1)}, bf16[128,1152]{1,0:T(8,128)(2,1)S(1)}, u32[]{:S(2)}, u32[]{:S(2)}) collective-permute-start(bf16[128,1152]{1,0:T(8,128)(2,1)S(1)} %shard_map.47.refs_2_), channel_id=1, source_target_pairs={{0,128},{128,0},{16,144},{144,16},{32,160},{160,32},{48,176},{176,... | collective-permute-start | bytes 884744 | tf_op jit(solution)/shard_map/ppermute | solution.py:198
  63.8 0.0 collective-permute-done.4.refs_3_
  63.8 2.4 %collective-permute-start.5 = (bf16[128,1152]{1,0:T(8,128)(2,1)S(1)}, bf16[128,1152]{1,0:T(8,128)(2,1)S(1)}, u32[]{:S(2)}, u32[]{:S(2)}) collective-permute-start(bf16[128,1152]{1,0:T(8,128)(2,1)S(1)} %collective-permute-done.4.refs_3_), channel_id=1, source_target_pairs={{0,128},{128,0},{16,144},{144,16},{32,160},{160,32},{48,176},{176,... | collective-permute-start | bytes 884744 | tf_op jit(solution)/shard_map/ppermute | solution.py:198
  66.2 2.0 %collective-permute-start.7 = (bf16[128,1152]{1,0:T(8,128)(2,1)S(1)}, bf16[128,1152]{1,0:T(8,128)(2,1)S(1)}, u32[]{:S(2)}, u32[]{:S(2)}) collective-permute-start(bf16[128,1152]{1,0:T(8,128)(2,1)S(1)} %collective-permute-done.6.refs_4_), channel_id=1, source_target_pairs={{0,128},{128,0},{16,144},{144,16},{32,160},{160,32},{48,176},{176,... | collective-permute-start | bytes 884744 | tf_op jit(solution)/shard_map/ppermute | solution.py:198
  68.2 4.9 %collective-permute-done.8.refs_5_ = bf16[128,1152]{1,0:T(8,128)(2,1)S(1)} collective-permute-done((bf16[128,1152]{1,0:T(8,128)(2,1)S(1)}, bf16[128,1152]{1,0:T(8,128)(2,1)S(1)}, u32[]{:S(2)}, u32[]{:S(2)}) %collective-permute-start.8) | collective-permute-done | bytes 294944 | tf_op jit(solution)/shard_map/ppermute | solution.py:198
  73.1 1.9 %collective-permute-start.9 = (bf16[128,1152]{1,0:T(8,128)(2,1)S(1)}, bf16[128,1152]{1,0:T(8,128)(2,1)S(1)}, u32[]{:S(2)}, u32[]{:S(2)}) collective-permute-start(bf16[128,1152]{1,0:T(8,128)(2,1)S(1)} %collective-permute-done.8.refs_5_), channel_id=1, source_target_pairs={{0,128},{128,0},{16,144},{144,16},{32,160},{160,32},{48,176},{176,... | collective-permute-start | bytes 884744 | tf_op jit(solution)/shard_map/ppermute | solution.py:198
  75.0 0.0 all-to-all-done
  75.0 3.2 %shard_map.48 = (f32[512,128]{1,0:T(8,128)S(1)}, f32[512,1024]{1,0:T(8,128)S(1)}) custom-call(f32[5]{0:T(128)S(1)} %copy-done, bf16[512,1152]{1,0:T(8,128)(2,1)S(1)} %bitcast.4, bf16[128,1152]{1,0:T(8,128)(2,1)S(1)} %shard_map.47.refs_2_, bf16[128,1152]{1,0:T(8,128)(2,1)S(1)} %collective-permute-done.4.refs_3_, ...), custom_call_target="tpu_custom_call" | custom-call | flops 1073741824 | bytes 2097152 | tf_op jit(solution)/shard_map/pallas_call | solution.py:174
  78.3 3.3 %shard_map.49 = bf16[512,1024]{1,0:T(8,128)(2,1)S(1)} custom-call(f32[5]{0:T(128)S(1)} %copy-done, bf16[512,1152]{1,0:T(8,128)(2,1)S(1)} %bitcast.5, bf16[128,1152]{1,0:T(8,128)(2,1)S(1)} %collective-permute-done.3.refs_2_, bf16[128,1152]{1,0:T(8,128)(2,1)S(1)} %collective-permute-done.5.refs_3_, bf16[128,1152]{1,0:T(8,128)(2,1)S(1)} %collective-permute-done.7.refs_4_, ...), custom_call_target="tpu_custom_call" | custom-call | flops 1073741824 | bytes 2097152 | tf_op jit(solution)/shard_map/pallas_call | solution.py:174
  81.6 22.3 %all_to_all.10 = bf16[16,32,1024]{2,1,0:T(8,128)(2,1)S(1)} all-to-all(bf16[16,32,1024]{2,1,0:T(8,128)(2,1)S(1)} %bitcast.6), channel_id=1, replica_groups=mesh['tensor'=4,'row'=8,'col'=16] {'col'}, dimensions={0} | all-to-all | bytes 2097152 | tf_op jit(solution)/shard_map/all_to_all | solution.py:225
  103.9 0.2 reduce_sum.12
  104.1 7.7 %collective-permute-start.10 = (bf16[32,1024]{1,0:T(8,128)(2,1)S(1)}, bf16[32,1024]{1,0:T(8,128)(2,1)S(1)}, u32[]{:S(2)}, u32[]{:S(2)}) collective-permute-start(bf16[32,1024]{1,0:T(8,128)(2,1)S(1)} %reduce_sum.12), channel_id=1, source_target_pairs={{0,256},{128,384},{16,272},{144,400},{32,288},{160,416},{48,304},{... | collective-permute-start | bytes 196616 | tf_op jit(solution)/shard_map/ppermute | solution.py:198
  111.8 6.1 %collective-permute-done.10 = bf16[32,1024]{1,0:T(8,128)(2,1)S(1)} collective-permute-done((bf16[32,1024]{1,0:T(8,128)(2,1)S(1)}, bf16[32,1024]{1,0:T(8,128)(2,1)S(1)}, u32[]{:S(2)}, u32[]{:S(2)}) %collective-permute-start.10) | collective-permute-done | bytes 65568 | tf_op jit(solution)/shard_map/ppermute | solution.py:198
  117.9 5.1 %collective-permute-start.11 = (bf16[64,1024]{1,0:T(8,128)(2,1)S(1)}, bf16[64,1024]{1,0:T(8,128)(2,1)S(1)}, u32[]{:S(2)}, u32[]{:S(2)}) collective-permute-start(bf16[64,1024]{1,0:T(8,128)(2,1)S(1)} %maximum_select_fusion.2), channel_id=1, source_target_pairs={{0,128},{128,0},{16,144},{144,16},{32,160},{160,32},{48,176},{176,... | collective-permute-start | bytes 393224 | tf_op jit(solution)/shard_map/ppermute | solution.py:198
  123.0 1.0 collective-permute-done.11
  124.0 3.8 %convolution_convert_fusion = bf16[128,1536]{1,0:T(8,128)(2,1)} fusion(bf16[1536,1024]{1,0:T(8,128)(2,1)} %w_ref.1, bf16[64,1024]{1,0:T(8,128)(2,1)S(1)} %maximum_select_fusion.2, bf16[64,1024]{1,0:T(8,128)(2,1)S(1)} %collective-permute-done.11, pred[]{:T(512)S(6)} %eq.9), kind=kOutput, calls=%fused_computation | convolution fusion | flops 404029440 | bytes 3801089 | tf_op jit(solution)/shard_map/dot_general | solution.py:237
  (14 shorter events, 0.1 us)
Async XLA Ops:
  0.0 12.0 %copy-start.1 = (s32[128]{0:T(128)S(1)}, s32[128]{0:T(128)}, u32[]{:S(2)}) copy-start(s32[128]{0:T(128)} %param.6) | copy-start | bytes 1540
  3.2 10.0 %collective-permute-start = (bf16[64,1024]{1,0:T(8,128)(2,1)}, bf16[64,1024]{1,0:T(8,128)(2,1)S(1)}, u32[]{:S(2)}, u32[]{:S(2)}) collective-permute-start(bf16[64,1024]{1,0:T(8,128)(2,1)} %get-tuple-element.10), channel_id=1, source_target_pairs={{0,128},{128,0},{16,144},{144,16},{32,160},{160,32},{48,176},{176,... | collective-permute-start | bytes 393224 | tf_op jit(solution)/shard_map/ppermute | solution.py:198
  14.1 15.3 %collective-permute-start.1 = (bf16[64,1024]{1,0:T(8,128)(2,1)S(1)}, bf16[64,1024]{1,0:T(8,128)(2,1)S(1)}, u32[]{:S(2)}, u32[]{:S(2)}) collective-permute-start(bf16[64,1024]{1,0:T(8,128)(2,1)S(1)} %add_convert_fusion.1), channel_id=1, source_target_pairs={{0,256},{128,384},{16,272},{144,400},{32,288},{160,416},{48,304},{... | collective-permute-start | bytes 393224 | tf_op jit(solution)/shard_map/ppermute | solution.py:198
  29.6 15.0 %collective-permute-start.2 = (bf16[64,1152]{1,0:T(8,128)(2,1)S(1)}, bf16[64,1152]{1,0:T(8,128)(2,1)S(1)}, u32[]{:S(2)}, u32[]{:S(2)}) collective-permute-start(bf16[64,1152]{1,0:T(8,128)(2,1)S(1)} %pad_maximum_fusion.first_ref), channel_id=1, source_target_pairs={{0,64},{128,448},{16,80},{144,464},{32,96},{160,480},{48,112},{176... | collective-permute-start | bytes 442376 | tf_op jit(solution)/shard_map/ppermute | solution.py:198
  37.8 37.2 %all-to-all-start = ((bf16[16,32,1152]{2,1,0:T(8,128)(2,1)}), bf16[16,32,1152]{2,1,0:T(8,128)(2,1)S(1)}, u32[]{:S(2)}, u32[]{:S(2)}) async-start(bf16[16,32,1152]{2,1,0:T(8,128)(2,1)} %broadcast_in_dim.5), calls=%async_computation | async-start | bytes 2359296 | tf_op jit(solution)/shard_map/all_to_all | solution.py:220
  44.6 30.5 %copy-start = (f32[5]{0:T(128)S(1)}, f32[5]{0:T(128)}, u32[]{:S(2)}) copy-start(f32[5]{0:T(128)} %refs_0_.3) | copy-start | bytes 64
  44.6 19.2 %collective-permute-start.4 = (bf16[128,1152]{1,0:T(8,128)(2,1)S(1)}, bf16[128,1152]{1,0:T(8,128)(2,1)S(1)}, u32[]{:S(2)}, u32[]{:S(2)}) collective-permute-start(bf16[128,1152]{1,0:T(8,128)(2,1)S(1)} %shard_map.47.refs_2_), channel_id=1, source_target_pairs={{0,16},{128,144},{16,32},{144,160},{32,48},{160,176},{48,64},{176,... | collective-permute-start | bytes 884744 | tf_op jit(solution)/shard_map/ppermute | solution.py:198
  52.0 14.2 %collective-permute-start.6 = (bf16[128,1152]{1,0:T(8,128)(2,1)S(1)}, bf16[128,1152]{1,0:T(8,128)(2,1)S(1)}, u32[]{:S(2)}, u32[]{:S(2)}) collective-permute-start(bf16[128,1152]{1,0:T(8,128)(2,1)S(1)} %shard_map.47.refs_2_), channel_id=1, source_target_pairs={{0,368},{128,496},{16,0},{144,128},{32,16},{160,144},{48,32},{176,... | collective-permute-start | bytes 884744 | tf_op jit(solution)/shard_map/ppermute | solution.py:198
  53.9 19.2 %collective-permute-start.8 = (bf16[128,1152]{1,0:T(8,128)(2,1)S(1)}, bf16[128,1152]{1,0:T(8,128)(2,1)S(1)}, u32[]{:S(2)}, u32[]{:S(2)}) collective-permute-start(bf16[128,1152]{1,0:T(8,128)(2,1)S(1)} %shard_map.47.refs_2_), channel_id=1, source_target_pairs={{0,32},{128,480},{16,48},{144,496},{32,64},{160,128},{48,80},{176,... | collective-permute-start | bytes 884744 | tf_op jit(solution)/shard_map/ppermute | solution.py:198
  61.9 16.4 %collective-permute-start.3 = (bf16[128,1152]{1,0:T(8,128)(2,1)S(1)}, bf16[128,1152]{1,0:T(8,128)(2,1)S(1)}, u32[]{:S(2)}, u32[]{:S(2)}) collective-permute-start(bf16[128,1152]{1,0:T(8,128)(2,1)S(1)} %shard_map.47.refs_2_), channel_id=1, source_target_pairs={{0,128},{128,0},{16,144},{144,16},{32,160},{160,32},{48,176},{176,... | collective-permute-start | bytes 884744 | tf_op jit(solution)/shard_map/ppermute | solution.py:198
  63.8 14.4 %collective-permute-start.5 = (bf16[128,1152]{1,0:T(8,128)(2,1)S(1)}, bf16[128,1152]{1,0:T(8,128)(2,1)S(1)}, u32[]{:S(2)}, u32[]{:S(2)}) collective-permute-start(bf16[128,1152]{1,0:T(8,128)(2,1)S(1)} %collective-permute-done.4.refs_3_), channel_id=1, source_target_pairs={{0,128},{128,0},{16,144},{144,16},{32,160},{160,32},{48,176},{176,... | collective-permute-start | bytes 884744 | tf_op jit(solution)/shard_map/ppermute | solution.py:198
  66.2 12.0 %collective-permute-start.7 = (bf16[128,1152]{1,0:T(8,128)(2,1)S(1)}, bf16[128,1152]{1,0:T(8,128)(2,1)S(1)}, u32[]{:S(2)}, u32[]{:S(2)}) collective-permute-start(bf16[128,1152]{1,0:T(8,128)(2,1)S(1)} %collective-permute-done.6.refs_4_), channel_id=1, source_target_pairs={{0,128},{128,0},{16,144},{144,16},{32,160},{160,32},{48,176},{176,... | collective-permute-start | bytes 884744 | tf_op jit(solution)/shard_map/ppermute | solution.py:198
  73.1 5.1 %collective-permute-start.9 = (bf16[128,1152]{1,0:T(8,128)(2,1)S(1)}, bf16[128,1152]{1,0:T(8,128)(2,1)S(1)}, u32[]{:S(2)}, u32[]{:S(2)}) collective-permute-start(bf16[128,1152]{1,0:T(8,128)(2,1)S(1)} %collective-permute-done.8.refs_5_), channel_id=1, source_target_pairs={{0,128},{128,0},{16,144},{144,16},{32,160},{160,32},{48,176},{176,... | collective-permute-start | bytes 884744 | tf_op jit(solution)/shard_map/ppermute | solution.py:198
  104.1 13.7 %collective-permute-start.10 = (bf16[32,1024]{1,0:T(8,128)(2,1)S(1)}, bf16[32,1024]{1,0:T(8,128)(2,1)S(1)}, u32[]{:S(2)}, u32[]{:S(2)}) collective-permute-start(bf16[32,1024]{1,0:T(8,128)(2,1)S(1)} %reduce_sum.12), channel_id=1, source_target_pairs={{0,256},{128,384},{16,272},{144,400},{32,288},{160,416},{48,304},{... | collective-permute-start | bytes 196616 | tf_op jit(solution)/shard_map/ppermute | solution.py:198
  117.9 6.1 %collective-permute-start.11 = (bf16[64,1024]{1,0:T(8,128)(2,1)S(1)}, bf16[64,1024]{1,0:T(8,128)(2,1)S(1)}, u32[]{:S(2)}, u32[]{:S(2)}) collective-permute-start(bf16[64,1024]{1,0:T(8,128)(2,1)S(1)} %maximum_select_fusion.2), channel_id=1, source_target_pairs={{0,128},{128,0},{16,144},{144,16},{32,160},{160,32},{48,176},{176,... | collective-permute-start | bytes 393224 | tf_op jit(solution)/shard_map/ppermute | solution.py:198

commit v4 on v3

--- a/solution.py
+++ b/solution.py
@@ -87,13 +87,63 @@
     )(core, features, w_proj)
 
 
+def block_kernel(near_ref, far_ref, signs_ref, block_ref):
+    f32, bf16 = jnp.float32, jnp.bfloat16
+    half, width = near_ref.shape
+    rows = (near_ref[...].astype(f32) + far_ref[...].astype(f32)).astype(bf16)
+    block_ref[:, :width] = rows
+    norm = jnp.sum(jnp.square(rows.astype(f32)), axis=1, keepdims=True)
+    first = norm.astype(bf16).astype(f32)
+    second = (norm - first).astype(bf16).astype(f32)
+    third = norm - first - second
+    lane = lax.broadcasted_iota(jnp.int32, (half, PAD), 1)
+    tail = jnp.where(lane == 1, first, jnp.where(lane == 2, second, third))
+    block_ref[:, width:] = jnp.where(lane == 0, signs_ref[...], tail).astype(bf16)
+
+
+def whole_block(near, far, signs):
+    vmem = pl.BlockSpec(memory_space=pltpu.VMEM)
+    half, width = near.shape
+    return pl.pallas_call(
+        block_kernel,
+        out_shape=jax.ShapeDtypeStruct((half, width + PAD), near.dtype),
+        in_specs=[vmem] * 3,
+        out_specs=vmem,
+        compiler_params=pltpu.CompilerParams(vmem_limit_bytes=16 * 2**20),
+        cost_estimate=pl.CostEstimate(
+            flops=4 * half * width, bytes_accessed=6 * half * width, transcendentals=0
+        ),
+    )(near, far, signs)
+
+
+def result_kernel(grad_ref, w_ref, out_ref):
+    out_ref[...] = lax.dot_general(
+        grad_ref[...], w_ref[...], (((1,), (1,)), ((), ())), preferred_element_type=jnp.float32
+    ).astype(out_ref.dtype)
+
+
+def result(grad, w_proj):
+    vmem = pl.BlockSpec(memory_space=pltpu.VMEM)
+    rows, depth = grad.shape[0], w_proj.shape[0]
+    return pl.pallas_call(
+        result_kernel,
+        out_shape=jax.ShapeDtypeStruct((rows, depth), grad.dtype),
+        in_specs=[vmem] * 2,
+        out_specs=vmem,
+        compiler_params=pltpu.CompilerParams(vmem_limit_bytes=16 * 2**20),
+        cost_estimate=pl.CostEstimate(
+            flops=2 * rows * w_proj.size, bytes_accessed=2 * w_proj.size, transcendentals=0
+        ),
+    )(grad, w_proj)
+
+
 def pair_kernel(first_ref, second_ref, out_ref):
     half = first_ref.shape[0]
     out_ref[:half] = first_ref[...]
     out_ref[half:] = second_ref[...]
 
 
-def side_by_side(first, second):
+def side_by_side(first, second, flops):
     vmem = pl.BlockSpec(memory_space=pltpu.VMEM)
     return pl.pallas_call(
         pair_kernel,
@@ -101,44 +151,52 @@
         in_specs=[vmem, vmem],
         out_specs=vmem,
         compiler_params=pltpu.CompilerParams(vmem_limit_bytes=16 * 2**20),
-        cost_estimate=pl.CostEstimate(flops=FLOPS, bytes_accessed=0, transcendentals=0),
+        cost_estimate=pl.CostEstimate(flops=flops, bytes_accessed=0, transcendentals=0),
     )(first, second)
 
 
-def tile_kernel(count, *refs):
+def after_kernel(value_ref, first_ref, same_ref):
+    pass
+
+
+def after(value, first):
+    anywhere = pl.BlockSpec(memory_space=pl.ANY)
+    return pl.pallas_call(
+        after_kernel,
+        out_shape=jax.ShapeDtypeStruct(value.shape, value.dtype),
+        in_specs=[anywhere, anywhere],
+        out_specs=anywhere,
+        input_output_aliases={0: 0},
+        compiler_params=pltpu.CompilerParams(vmem_limit_bytes=16 * 2**20),
+        cost_estimate=pl.CostEstimate(flops=0, bytes_accessed=0, transcendentals=0),
+    )(value, first)
+
+
+def tile_kernel(count, more, last, *refs):
     f32, bf16 = jnp.float32, jnp.bfloat16
     rates_ref, col_ref = refs[:2]
     pieces, refs = refs[2 : 2 + count], refs[2 + count :]
-    last = len(refs) == 5
-    held, refs = (refs[:2], refs[2:]) if last else (None, refs)
-    outs, (rows_ref, signed_ref) = refs[:-2], refs[-2:]
+    held, refs = (refs[:2], refs[2:]) if more else (None, refs)
+    outs, rows_ref = refs[:-1], refs[-1]
     width = col_ref.shape[1] - PAD
-    depth = pieces[0].shape[0]
-    n_rows = count * depth
-
-    turned = []
-    for index, piece in enumerate(pieces):
-        place = slice(index * depth, (index + 1) * depth)
-        sign = piece[:, width:]
-        square = jnp.zeros((depth, PAD), f32)
-        for at in range(0, width, PAD):
-            part = piece[:, at : at + PAD]
-            rows_ref[place, at : at + PAD] = part
-            signed_ref[place, at : at + PAD] = part * sign
-            square += jnp.square(part.astype(f32))
-        norm = jnp.sum(square, axis=1, keepdims=True)
-        lane = lax.broadcasted_iota(jnp.int32, (depth, PAD), 1)
-        turned.append(jnp.where(lane == 0, norm, sign.astype(f32)).T)
-    row_norm = jnp.concatenate([value[0:1] for value in turned], axis=1)
-    row_sign = jnp.concatenate([value[1:2] for value in turned], axis=1)
+    n_rows = rows_ref.shape[0]
+
+    turned, filled = [], 0
+    for piece in pieces:
+        rows_ref[filled : filled + piece.shape[0]] = piece[:, :width]
+        filled += piece.shape[0]
+        turned.append(piece[:, width:].astype(f32).T)
+    turned = jnp.concatenate([value[:8] for value in turned], axis=1)
+    row_sign = turned[0:1]
+    row_norm = turned[1:2] + turned[2:3] + turned[3:4]
 
     scales = [rates_ref[band] * (-LOG2E / width) for band in range(rates_ref.shape[0])]
     step = min(256, col_ref.shape[0])
     for start in range(0, col_ref.shape[0], step):
         place = slice(start, start + step)
         col_z = col_ref[place, :width]
-        wide = col_z.astype(f32)
-        col_norm = jnp.sum(jnp.square(wide), axis=1, keepdims=True)
+        tail = col_ref[place, width:].astype(f32)
+        col_norm = tail[:, 1:2] + tail[:, 2:3] + tail[:, 3:4]
         cross = lax.dot_general(
             col_z, rows_ref[...], (((1,), (1,)), ((), ())), preferred_element_type=f32
         )
@@ -146,24 +204,27 @@
         kernel = jnp.zeros((step, n_rows), f32)
         for band, scale in enumerate(scales):
             kernel += rates_ref[band] * jnp.exp2(scale * dist)
-        total = jnp.broadcast_to(jnp.sum(kernel * row_sign, axis=1, keepdims=True), (step, PAD))
-        other = jnp.dot(kernel.astype(bf16), signed_ref[...], preferred_element_type=f32)
-        if last:
+        kernel *= row_sign
+        total = jnp.broadcast_to(jnp.sum(kernel, axis=1, keepdims=True), (step, PAD))
+        other = jnp.dot(kernel.astype(bf16), rows_ref[...], preferred_element_type=f32)
+        if more:
             total += held[0][place]
             other += held[1][place]
-            factor = (-32.0 / width) * col_ref[place, width : width + 1].astype(f32)
+        if last:
+            factor = (-32.0 / width) * tail[:, 0:1]
+            wide = col_z.astype(f32)
             outs[0][place] = (factor * (total[:, :1] * wide - other)).astype(bf16)
         else:
             outs[0][place] = total
             outs[1][place] = other
 
 
-def tiles(pieces, col, rates, held=()):
+def tiles(pieces, col, rates, held=(), last=False):
     f32, bf16 = jnp.float32, jnp.bfloat16
     n_cols, width = col.shape[0], col.shape[1] - PAD
     n_rows = sum(piece.shape[0] for piece in pieces)
     vmem = pl.BlockSpec(memory_space=pltpu.VMEM)
-    if held:
+    if last:
         out_shape = jax.ShapeDtypeStruct((n_cols, width), bf16)
     else:
         out_shape = (
@@ -172,11 +233,11 @@
         )
     pairs = n_rows * n_cols
     return pl.pallas_call(
-        functools.partial(tile_kernel, len(pieces)),
+        functools.partial(tile_kernel, len(pieces), bool(held), last),
         out_shape=out_shape,
         in_specs=[pl.BlockSpec(memory_space=pltpu.SMEM)] + [vmem] * (1 + len(pieces) + len(held)),
-        out_specs=vmem if held else (vmem, vmem),
-        scratch_shapes=[pltpu.VMEM((n_rows, width), bf16), pltpu.VMEM((n_rows, width), bf16)],
+        out_specs=vmem if last else (vmem, vmem),
+        scratch_shapes=[pltpu.VMEM((n_rows, width), bf16)],
         compiler_params=pltpu.CompilerParams(vmem_limit_bytes=32 * 2**20),
         cost_estimate=pl.CostEstimate(
             flops=4 * pairs * width, bytes_accessed=4 * n_cols * width, transcendentals=5 * pairs
@@ -203,25 +264,25 @@
     away, kept = projection(jnp.reshape(tpos % 2, (1,)), features, w_proj)
     partial = (kept + other_core(away).astype(f32)).astype(bf16)
     far = move(partial, lambda chip, core: (chip + n_row, core))
-    z_half = (partial.astype(f32) + far.astype(f32)).astype(bf16)
-    signs = (1 - 2 * flags).astype(bf16)
+    signs = (1 - 2 * flags).astype(f32)
     s_half = pick(core, signs[:half], signs[half:])
-    block = jnp.concatenate([z_half, jnp.broadcast_to(s_half[:, None], (half, PAD))], axis=1)
+    block = whole_block(partial, far, jnp.broadcast_to(s_half[:, None], (half, PAD)))
 
     far_block = move(block, lambda chip, core: (chip + (n_row // 2) * (1 - 2 * core), core))
-    pair = side_by_side(block, far_block)
-    near = [
-        pair,
-        move(pair, lambda chip, core: (chip + 1, core)),
-        move(pair, lambda chip, core: (chip - 1, core)),
-        move(pair, lambda chip, core: (chip + 2 - 4 * core, core)),
-    ]
+    pair = side_by_side(block, far_block, FLOPS)
+    two_away = move(pair, lambda chip, core: (chip + 2 - 4 * core, core))
+    other_pair = other_core(pair)
+    one_away = move(
+        side_by_side(pair, other_pair, 0), lambda chip, core: (chip + 1 - 2 * core, core)
+    )
     own = pick(high, block[:quarter], block[quarter:])
     col = lax.all_to_all(
         jnp.broadcast_to(own[None], (n_col,) + own.shape), "col", 0, 0, tiled=True
     ).reshape(n_col * quarter, width + PAD)
-    sums = tiles(near, col, rates)
-    part = tiles([other_core(value) for value in near], col, rates, sums)
+    sums = tiles([pair, other_pair], col, rates)
+    one_away = after(one_away, sums[0])
+    sums = tiles([two_away, other_core(two_away)], col, rates, sums, False)
+    part = tiles([one_away, other_core(one_away)], col, rates, sums, True)
     parts = lax.all_to_all(part.reshape(n_col, quarter, width), "col", 0, 0, tiled=True)
     grad = jnp.sum(parts.astype(f32), axis=0).astype(bf16)
     grad_far = move(grad, lambda chip, core: (chip + n_row, core))
@@ -234,8 +295,7 @@
         jnp.concatenate([grad, grad_other], axis=0),
         jnp.concatenate([grad_other, grad], axis=0),
     )
-    result = lax.dot_general(grad, w_proj, (((1,), (1,)), ((), ())), preferred_element_type=f32)
-    return result.astype(bf16)
+    return result(grad, w_proj)
 
 
 def solution(mesh):

time: 128 us -> 128 us (level)
  waiting for transfers between devices: 18.2 us -> 14.2 us
  matrix products: 3.81 us -> 0 us
  starting transfers between devices: 70.9 us -> 73.9 us
  Pallas kernels: 9.65 us -> 12.5 us
    ppermute x12 -> x10, waiting for transfers between devices: 18.2 us -> 14.2 us  [move(): return lax.ppermute(value, ZLINE, line_permutation(shift, n_row))]
    dot_general x1 -> x0, matrix products: 3.81 us -> none  [shards(): lax.dot_general(grad, w_proj, (((1,), (1,)), ((), ())), preferred_element...]
    ppermute x12 -> x10, starting transfers between devices: 64.2 us -> 67.2 us  [move(): return lax.ppermute(value, ZLINE, line_permutation(shift, n_row))]
    pallas_call x2 -> x6, Pallas kernels: 6.47 us -> 9.24 us  [the longest x3 7.21 us: tiles(): pl.pallas_call(functools.partial(tile_kernel, len(pieces), bool(held), la...]
  transfers between devices with their start and end apart: 13 -> 11, of which waited for: 5 -> 7; matrix products, arithmetic and copies ran while one was open for 1% -> 1% of each run, Pallas kernels for 2% -> 4%
where the time goes in v4:
time: 128 us; the launch traced here: 127 us
  starting transfers between devices  73.9 us (58%)
  blocking collectives  22.9 us (18%)
  waiting for transfers between devices  14.2 us (11%)
  Pallas kernels  12.5 us (10%)
  other arithmetic  2.56 us (2%)
    ppermute x10, starting transfers between devices, move(): return lax.ppermute(value, ZLINE, line_permutation(shift, n_row))  67.2 us
    all_to_all x1, blocking collectives, shards(): lax.all_to_all(part.reshape(n_col, quarter, width), 'col', 0, 0, tiled=True)  22.9 us
    ppermute x10, waiting for transfers between devices, move(): return lax.ppermute(value, ZLINE, line_permutation(shift, n_row))  14.2 us
    pallas_call x3, Pallas kernels, tiles(): pl.pallas_call(functools.partial(tile_kernel, len(pieces), bool(held), la...  7.21 us
    all_to_all x1, starting transfers between devices, shards(): lax.all_to_all(jnp.broadcast_to(own[None], (n_col,) + own.shape), 'col',...  6.74 us
    pallas_call x1, Pallas kernels, projection(): pl.pallas_call(projection_kernel, out_shape=(jax.ShapeDtypeStruct((rows /...  3.15 us
  transfers between devices with their start and end apart: 11, of which 7 were waited for; matrix products, arithmetic and copies ran while one was open for 1% of the time, Pallas kernels for 4%

profile of v4, /device:TPU:1, one launch (start us, length us, event | category | flops | bytes accessed | tf_op | source)
XLA Modules:
  0.0 127.5 jit_solution(18004505218081893003)
XLA Ops:
  0.0 3.2 %shard_map.46 = (bf16[64,1024]{1,0:T(8,128)(2,1)}, f32[64,1024]{1,0:T(8,128)}) custom-call(s32[1]{0:T(128)} %bitcast.core_ref, bf16[128,1536]{1,0:T(8,128)(2,1)} %features_ref.1, bf16[1536,1024]{1,0:T(8,128)(2,1)} %w_ref.3), custom_call_target="tpu_custom_call" | custom-call | flops 402653184 | bytes 3145728 | tf_op jit(solution)/shard_map/pallas_call | solution.py:67
  3.2 8.8 %collective-permute-start = (bf16[64,1024]{1,0:T(8,128)(2,1)}, bf16[64,1024]{1,0:T(8,128)(2,1)S(1)}, u32[]{:S(2)}, u32[]{:S(2)}) collective-permute-start(bf16[64,1024]{1,0:T(8,128)(2,1)} %get-tuple-element.12), channel_id=1, source_target_pairs={{0,128},{128,0},{16,144},{144,16},{32,160},{160,32},{48,176},{176,... | collective-permute-start | bytes 393224 | tf_op jit(solution)/shard_map/ppermute | solution.py:259
  12.0 1.1 collective-permute-done
  13.1 1.0 add_convert_fusion.near_ref
  14.1 10.1 %collective-permute-start.1 = (bf16[64,1024]{1,0:T(8,128)(2,1)S(1)}, bf16[64,1024]{1,0:T(8,128)(2,1)S(1)}, u32[]{:S(2)}, u32[]{:S(2)}) collective-permute-start(bf16[64,1024]{1,0:T(8,128)(2,1)S(1)} %add_convert_fusion.near_ref), channel_id=1, source_target_pairs={{0,256},{128,384},{16,272},{144,400},{32,288},{160,416},{48,304},{... | collective-permute-start | bytes 393224 | tf_op jit(solution)/shard_map/ppermute | solution.py:259
  24.2 0.1 broadcast_select_fusion
  24.3 5.2 %collective-permute-done.1.far_ref = bf16[64,1024]{1,0:T(8,128)(2,1)S(1)} collective-permute-done((bf16[64,1024]{1,0:T(8,128)(2,1)S(1)}, bf16[64,1024]{1,0:T(8,128)(2,1)S(1)}, u32[]{:S(2)}, u32[]{:S(2)}) %collective-permute-start.1) | collective-permute-done | bytes 131104 | tf_op jit(solution)/shard_map/ppermute | solution.py:259
  29.4 0.1 broadcast_in_dim.4.signs_ref
  29.5 0.1 shard_map.47.first_ref
  29.6 7.1 %collective-permute-start.2 = (bf16[64,1152]{1,0:T(8,128)(2,1)S(1)}, bf16[64,1152]{1,0:T(8,128)(2,1)S(1)}, u32[]{:S(2)}, u32[]{:S(2)}) collective-permute-start(bf16[64,1152]{1,0:T(8,128)(2,1)S(1)} %shard_map.47.first_ref), channel_id=1, source_target_pairs={{0,64},{128,448},{16,80},{144,464},{32,96},{160,480},{48,112},{176... | collective-permute-start | bytes 442376 | tf_op jit(solution)/shard_map/ppermute | solution.py:259
  36.8 1.1 broadcast_in_dim.5
  37.9 6.7 %all-to-all-start = ((bf16[16,32,1152]{2,1,0:T(8,128)(2,1)}), bf16[16,32,1152]{2,1,0:T(8,128)(2,1)S(1)}, u32[]{:S(2)}, u32[]{:S(2)}) async-start(bf16[16,32,1152]{2,1,0:T(8,128)(2,1)} %broadcast_in_dim.5), calls=%async_computation | async-start | bytes 2359296 | tf_op jit(solution)/shard_map/all_to_all | solution.py:279
  44.6 0.0 copy-start.1
  44.7 7.0 %collective-permute-start.3 = (bf16[128,1152]{1,0:T(8,128)(2,1)S(1)}, bf16[128,1152]{1,0:T(8,128)(2,1)S(1)}, u32[]{:S(2)}, u32[]{:S(2)}) collective-permute-start(bf16[128,1152]{1,0:T(8,128)(2,1)S(1)} %shard_map.48.first_ref.refs_2_), channel_id=1, source_target_pairs={{0,128},{128,0},{16,144},{144,16},{32,160},{160,32},{48,176},{176,... | collective-permute-start | bytes 884744 | tf_op jit(solution)/shard_map/ppermute | solution.py:259
  51.6 1.2 collective-permute-done.3.second_ref.refs_3_
  52.9 3.0 %collective-permute-start.4 = (bf16[256,1152]{1,0:T(8,128)(2,1)S(1)}, bf16[256,1152]{1,0:T(8,128)(2,1)S(1)}, u32[]{:S(2)}, u32[]{:S(2)}) collective-permute-start(bf16[256,1152]{1,0:T(8,128)(2,1)S(1)} %shard_map.49), channel_id=1, source_target_pairs={{0,16},{128,496},{16,32},{144,128},{32,48},{160,144},{48,64},{176,... | collective-permute-start | bytes 1769480 | tf_op jit(solution)/shard_map/ppermute | solution.py:259
  55.9 7.6 %collective-permute-start.6 = (bf16[128,1152]{1,0:T(8,128)(2,1)S(1)}, bf16[128,1152]{1,0:T(8,128)(2,1)S(1)}, u32[]{:S(2)}, u32[]{:S(2)}) collective-permute-start(bf16[128,1152]{1,0:T(8,128)(2,1)S(1)} %shard_map.48.first_ref.refs_2_), channel_id=1, source_target_pairs={{0,32},{128,480},{16,48},{144,496},{32,64},{160,128},{48,80},{176,... | collective-permute-start | bytes 884744 | tf_op jit(solution)/shard_map/ppermute | solution.py:259
  63.5 2.2 %shard_map.50 = (f32[512,128]{1,0:T(8,128)S(1)}, f32[512,1024]{1,0:T(8,128)S(1)}) custom-call(f32[5]{0:T(128)S(1)} %copy-done.1, bf16[512,1152]{1,0:T(8,128)(2,1)S(1)} %bitcast.3, bf16[128,1152]{1,0:T(8,128)(2,1)S(1)} %shard_map.48.first_ref.refs_2_, bf16[128,1152]{1,0:T(8,128)(2,1)S(1)} %collective-permute-done.3.second_ref.refs_3_), custom_call_target="tpu_custom_call" | custom-call | flops 536870912 | bytes 2097152 | tf_op jit(solution)/shard_map/pallas_call | solution.py:235
  65.8 2.6 %collective-permute-start.5 = (bf16[256,1152]{1,0:T(8,128)(2,1)S(1)}, bf16[256,1152]{1,0:T(8,128)(2,1)S(1)}, u32[]{:S(2)}, u32[]{:S(2)}) collective-permute-start(bf16[256,1152]{1,0:T(8,128)(2,1)S(1)} %shard_map.51.refs_2_), channel_id=1, source_target_pairs={{0,128},{128,0},{16,144},{144,16},{32,160},{160,32},{48,176},{176,... | collective-permute-start | bytes 1769480 | tf_op jit(solution)/shard_map/ppermute | solution.py:259
  68.4 2.2 %collective-permute-done.6.refs_2_ = bf16[128,1152]{1,0:T(8,128)(2,1)S(1)} collective-permute-done((bf16[128,1152]{1,0:T(8,128)(2,1)S(1)}, bf16[128,1152]{1,0:T(8,128)(2,1)S(1)}, u32[]{:S(2)}, u32[]{:S(2)}) %collective-permute-start.6) | collective-permute-done | bytes 294944 | tf_op jit(solution)/shard_map/ppermute | solution.py:259
  70.5 4.6 %collective-permute-start.7 = (bf16[128,1152]{1,0:T(8,128)(2,1)S(1)}, bf16[128,1152]{1,0:T(8,128)(2,1)S(1)}, u32[]{:S(2)}, u32[]{:S(2)}) collective-permute-start(bf16[128,1152]{1,0:T(8,128)(2,1)S(1)} %collective-permute-done.6.refs_2_), channel_id=1, source_target_pairs={{0,128},{128,0},{16,144},{144,16},{32,160},{160,32},{48,176},{176,... | collective-permute-start | bytes 884744 | tf_op jit(solution)/shard_map/ppermute | solution.py:259
  75.1 1.2 collective-permute-done.7.refs_3_
  76.3 2.2 %shard_map.52 = (f32[512,128]{1,0:T(8,128)S(1)}, f32[512,1024]{1,0:T(8,128)S(1)}) custom-call(f32[5]{0:T(128)S(1)} %copy-done.1, bf16[512,1152]{1,0:T(8,128)(2,1)S(1)} %bitcast.4, bf16[128,1152]{1,0:T(8,128)(2,1)S(1)} %collective-permute-done.6.refs_2_, bf16[128,1152]{1,0:T(8,128)(2,1)S(1)} %collective-permute-done.7.refs_3_, ...), custom_call_target="tpu_custom_call" | custom-call | flops 536870912 | bytes 2097152 | tf_op jit(solution)/shard_map/pallas_call | solution.py:235
  78.5 2.8 %shard_map.53 = bf16[512,1024]{1,0:T(8,128)(2,1)S(1)} custom-call(f32[5]{0:T(128)S(1)} %copy-done.1, bf16[512,1152]{1,0:T(8,128)(2,1)S(1)} %bitcast.5, bf16[256,1152]{1,0:T(8,128)(2,1)S(1)} %shard_map.51.refs_2_, bf16[256,1152]{1,0:T(8,128)(2,1)S(1)} %collective-permute-done.5.refs_3_, f32[512,128]{1,0:T(8,128)S(1)} %get-tuple-element.15.refs_4_, ...), custom_call_target="tpu_custom_call" | custom-call | flops 1073741824 | bytes 2097152 | tf_op jit(solution)/shard_map/pallas_call | solution.py:235
  81.3 0.0 copy-start
  81.3 22.9 %all_to_all.10 = bf16[16,32,1024]{2,1,0:T(8,128)(2,1)} all-to-all(bf16[16,32,1024]{2,1,0:T(8,128)(2,1)S(1)} %bitcast.6), channel_id=1, replica_groups=mesh['tensor'=4,'row'=8,'col'=16] {'col'}, dimensions={0} | all-to-all | bytes 2097152 | tf_op jit(solution)/shard_map/all_to_all | solution.py:286
  104.2 1.4 %reduce_sum.12 = bf16[32,1024]{1,0:T(8,128)(2,1)S(1)} reduce(bf16[16,32,1024]{2,1,0:T(8,128)(2,1)} %all_to_all.10, bf16[]{:T(256)} %constant.37.clone.1), dimensions={0}, to_apply=%region_0.1 | reduce | flops 491520 | bytes 1114114 | tf_op jit(solution)/shard_map/reduce_sum | solution.py:287
  105.6 11.3 %collective-permute-start.8 = (bf16[32,1024]{1,0:T(8,128)(2,1)S(1)}, bf16[32,1024]{1,0:T(8,128)(2,1)S(1)}, u32[]{:S(2)}, u32[]{:S(2)}) collective-permute-start(bf16[32,1024]{1,0:T(8,128)(2,1)S(1)} %reduce_sum.12), channel_id=1, source_target_pairs={{0,256},{128,384},{16,272},{144,400},{32,288},{160,416},{48,304},{... | collective-permute-start | bytes 196616 | tf_op jit(solution)/shard_map/ppermute | solution.py:259
  117.0 2.4 %collective-permute-done.8 = bf16[32,1024]{1,0:T(8,128)(2,1)S(1)} collective-permute-done((bf16[32,1024]{1,0:T(8,128)(2,1)S(1)}, bf16[32,1024]{1,0:T(8,128)(2,1)S(1)}, u32[]{:S(2)}, u32[]{:S(2)}) %collective-permute-start.8) | collective-permute-done | bytes 65568 | tf_op jit(solution)/shard_map/ppermute | solution.py:259
  119.4 5.2 %collective-permute-start.9 = (bf16[64,1024]{1,0:T(8,128)(2,1)S(1)}, bf16[64,1024]{1,0:T(8,128)(2,1)S(1)}, u32[]{:S(2)}, u32[]{:S(2)}) collective-permute-start(bf16[64,1024]{1,0:T(8,128)(2,1)S(1)} %maximum_select_fusion.1), channel_id=1, source_target_pairs={{0,128},{128,0},{16,144},{144,16},{32,160},{160,32},{48,176},{176,... | collective-permute-start | bytes 393224 | tf_op jit(solution)/shard_map/ppermute | solution.py:259
  124.6 1.0 collective-permute-done.9
  125.6 1.9 %shard_map.54 = bf16[128,1536]{1,0:T(8,128)(2,1)} custom-call(bf16[128,1024]{1,0:T(8,128)(2,1)S(1)} %maximum_select_fusion.grad_ref, bf16[1536,1024]{1,0:T(8,128)(2,1)S(1)} %copy-done), custom_call_target="tpu_custom_call" | custom-call | flops 402653184 | bytes 3145728 | tf_op jit(solution)/shard_map/pallas_call | solution.py:128
  (15 shorter events, 0.2 us)
Async XLA Ops:
  0.0 12.0 %copy-start.2 = (s32[128]{0:T(128)S(1)}, s32[128]{0:T(128)}, u32[]{:S(2)}) copy-start(s32[128]{0:T(128)} %param.6) | copy-start | bytes 1540
  3.2 10.0 %collective-permute-start = (bf16[64,1024]{1,0:T(8,128)(2,1)}, bf16[64,1024]{1,0:T(8,128)(2,1)S(1)}, u32[]{:S(2)}, u32[]{:S(2)}) collective-permute-start(bf16[64,1024]{1,0:T(8,128)(2,1)} %get-tuple-element.12), channel_id=1, source_target_pairs={{0,128},{128,0},{16,144},{144,16},{32,160},{160,32},{48,176},{176,... | collective-permute-start | bytes 393224 | tf_op jit(solution)/shard_map/ppermute | solution.py:259
  14.1 15.3 %collective-permute-start.1 = (bf16[64,1024]{1,0:T(8,128)(2,1)S(1)}, bf16[64,1024]{1,0:T(8,128)(2,1)S(1)}, u32[]{:S(2)}, u32[]{:S(2)}) collective-permute-start(bf16[64,1024]{1,0:T(8,128)(2,1)S(1)} %add_convert_fusion.near_ref), channel_id=1, source_target_pairs={{0,256},{128,384},{16,272},{144,400},{32,288},{160,416},{48,304},{... | collective-permute-start | bytes 393224 | tf_op jit(solution)/shard_map/ppermute | solution.py:259
  29.6 15.0 %collective-permute-start.2 = (bf16[64,1152]{1,0:T(8,128)(2,1)S(1)}, bf16[64,1152]{1,0:T(8,128)(2,1)S(1)}, u32[]{:S(2)}, u32[]{:S(2)}) collective-permute-start(bf16[64,1152]{1,0:T(8,128)(2,1)S(1)} %shard_map.47.first_ref), channel_id=1, source_target_pairs={{0,64},{128,448},{16,80},{144,464},{32,96},{160,480},{48,112},{176... | collective-permute-start | bytes 442376 | tf_op jit(solution)/shard_map/ppermute | solution.py:259
  37.9 25.6 %all-to-all-start = ((bf16[16,32,1152]{2,1,0:T(8,128)(2,1)}), bf16[16,32,1152]{2,1,0:T(8,128)(2,1)S(1)}, u32[]{:S(2)}, u32[]{:S(2)}) async-start(bf16[16,32,1152]{2,1,0:T(8,128)(2,1)} %broadcast_in_dim.5), calls=%async_computation | async-start | bytes 2359296 | tf_op jit(solution)/shard_map/all_to_all | solution.py:279
  44.6 18.9 %copy-start.1 = (f32[5]{0:T(128)S(1)}, f32[5]{0:T(128)}, u32[]{:S(2)}) copy-start(f32[5]{0:T(128)} %refs_0_.5) | copy-start | bytes 64
  44.7 8.1 %collective-permute-start.3 = (bf16[128,1152]{1,0:T(8,128)(2,1)S(1)}, bf16[128,1152]{1,0:T(8,128)(2,1)S(1)}, u32[]{:S(2)}, u32[]{:S(2)}) collective-permute-start(bf16[128,1152]{1,0:T(8,128)(2,1)S(1)} %shard_map.48.first_ref.refs_2_), channel_id=1, source_target_pairs={{0,128},{128,0},{16,144},{144,16},{32,160},{160,32},{48,176},{176,... | collective-permute-start | bytes 884744 | tf_op jit(solution)/shard_map/ppermute | solution.py:259
  52.9 12.9 %collective-permute-start.4 = (bf16[256,1152]{1,0:T(8,128)(2,1)S(1)}, bf16[256,1152]{1,0:T(8,128)(2,1)S(1)}, u32[]{:S(2)}, u32[]{:S(2)}) collective-permute-start(bf16[256,1152]{1,0:T(8,128)(2,1)S(1)} %shard_map.49), channel_id=1, source_target_pairs={{0,16},{128,496},{16,32},{144,128},{32,48},{160,144},{48,64},{176,... | collective-permute-start | bytes 1769480 | tf_op jit(solution)/shard_map/ppermute | solution.py:259
  55.9 14.6 %collective-permute-start.6 = (bf16[128,1152]{1,0:T(8,128)(2,1)S(1)}, bf16[128,1152]{1,0:T(8,128)(2,1)S(1)}, u32[]{:S(2)}, u32[]{:S(2)}) collective-permute-start(bf16[128,1152]{1,0:T(8,128)(2,1)S(1)} %shard_map.48.first_ref.refs_2_), channel_id=1, source_target_pairs={{0,32},{128,480},{16,48},{144,496},{32,64},{160,128},{48,80},{176,... | collective-permute-start | bytes 884744 | tf_op jit(solution)/shard_map/ppermute | solution.py:259
  65.8 12.7 %collective-permute-start.5 = (bf16[256,1152]{1,0:T(8,128)(2,1)S(1)}, bf16[256,1152]{1,0:T(8,128)(2,1)S(1)}, u32[]{:S(2)}, u32[]{:S(2)}) collective-permute-start(bf16[256,1152]{1,0:T(8,128)(2,1)S(1)} %shard_map.51.refs_2_), channel_id=1, source_target_pairs={{0,128},{128,0},{16,144},{144,16},{32,160},{160,32},{48,176},{176,... | collective-permute-start | bytes 1769480 | tf_op jit(solution)/shard_map/ppermute | solution.py:259
  70.5 5.8 %collective-permute-start.7 = (bf16[128,1152]{1,0:T(8,128)(2,1)S(1)}, bf16[128,1152]{1,0:T(8,128)(2,1)S(1)}, u32[]{:S(2)}, u32[]{:S(2)}) collective-permute-start(bf16[128,1152]{1,0:T(8,128)(2,1)S(1)} %collective-permute-done.6.refs_2_), channel_id=1, source_target_pairs={{0,128},{128,0},{16,144},{144,16},{32,160},{160,32},{48,176},{176,... | collective-permute-start | bytes 884744 | tf_op jit(solution)/shard_map/ppermute | solution.py:259
  81.3 44.2 %copy-start = (bf16[1536,1024]{1,0:T(8,128)(2,1)S(1)}, bf16[1536,1024]{1,0:T(8,128)(2,1)}, u32[]{:S(2)}) copy-start(bf16[1536,1024]{1,0:T(8,128)(2,1)} %w_ref.3) | copy-start | bytes 9437188
  105.6 13.7 %collective-permute-start.8 = (bf16[32,1024]{1,0:T(8,128)(2,1)S(1)}, bf16[32,1024]{1,0:T(8,128)(2,1)S(1)}, u32[]{:S(2)}, u32[]{:S(2)}) collective-permute-start(bf16[32,1024]{1,0:T(8,128)(2,1)S(1)} %reduce_sum.12), channel_id=1, source_target_pairs={{0,256},{128,384},{16,272},{144,400},{32,288},{160,416},{48,304},{... | collective-permute-start | bytes 196616 | tf_op jit(solution)/shard_map/ppermute | solution.py:259
  119.4 6.1 %collective-permute-start.9 = (bf16[64,1024]{1,0:T(8,128)(2,1)S(1)}, bf16[64,1024]{1,0:T(8,128)(2,1)S(1)}, u32[]{:S(2)}, u32[]{:S(2)}) collective-permute-start(bf16[64,1024]{1,0:T(8,128)(2,1)S(1)} %maximum_select_fusion.1), channel_id=1, source_target_pairs={{0,128},{128,0},{16,144},{144,16},{32,160},{160,32},{48,176},{176,... | collective-permute-start | bytes 393224 | tf_op jit(solution)/shard_map/ppermute | solution.py:259

commit v5 on v4

--- a/solution.py
+++ b/solution.py
@@ -159,7 +159,7 @@
     pass
 
 
-def after(value, first):
+def after(value, first, flops):
     anywhere = pl.BlockSpec(memory_space=pl.ANY)
     return pl.pallas_call(
         after_kernel,
@@ -168,7 +168,7 @@
         out_specs=anywhere,
         input_output_aliases={0: 0},
         compiler_params=pltpu.CompilerParams(vmem_limit_bytes=16 * 2**20),
-        cost_estimate=pl.CostEstimate(flops=0, bytes_accessed=0, transcendentals=0),
+        cost_estimate=pl.CostEstimate(flops=flops, bytes_accessed=0, transcendentals=0),
     )(value, first)
 
 
@@ -280,8 +280,9 @@
         jnp.broadcast_to(own[None], (n_col,) + own.shape), "col", 0, 0, tiled=True
     ).reshape(n_col * quarter, width + PAD)
     sums = tiles([pair, other_pair], col, rates)
-    one_away = after(one_away, sums[0])
-    sums = tiles([two_away, other_core(two_away)], col, rates, sums, False)
+    other_two_away = after(other_core(two_away), sums[0], FLOPS // 20)
+    one_away = after(one_away, other_two_away, 0)
+    sums = tiles([two_away, other_two_away], col, rates, sums, False)
     part = tiles([one_away, other_core(one_away)], col, rates, sums, True)
     parts = lax.all_to_all(part.reshape(n_col, quarter, width), "col", 0, 0, tiled=True)
     grad = jnp.sum(parts.astype(f32), axis=0).astype(bf16)

time: 128 us -> 128 us (level)
  transfers between devices with their start and end apart: 11 -> 11, of which waited for: 7 -> 5; matrix products, arithmetic and copies ran while one was open for 1% -> 1% of each run, Pallas kernels for 4% -> 4%
where the time goes in v5:
time: 128 us; the launch traced here: 127 us
  starting transfers between devices  73.3 us (57%)
  blocking collectives  22.7 us (18%)
  waiting for transfers between devices  14.7 us (11%)
  Pallas kernels  12.5 us (10%)
  other arithmetic  2.56 us (2%)
    ppermute x10, starting transfers between devices, move(): return lax.ppermute(value, ZLINE, line_permutation(shift, n_row))  66.6 us
    all_to_all x1, blocking collectives, shards(): lax.all_to_all(part.reshape(n_col, quarter, width), 'col', 0, 0, tiled=True)  22.7 us
    ppermute x10, waiting for transfers between devices, move(): return lax.ppermute(value, ZLINE, line_permutation(shift, n_row))  14.7 us
    pallas_call x3, Pallas kernels, tiles(): pl.pallas_call(functools.partial(tile_kernel, len(pieces), bool(held), la...  7.21 us
    all_to_all x1, starting transfers between devices, shards(): lax.all_to_all(jnp.broadcast_to(own[None], (n_col,) + own.shape), 'col',...  6.74 us
    pallas_call x1, Pallas kernels, projection(): pl.pallas_call(projection_kernel, out_shape=(jax.ShapeDtypeStruct((rows /...  3.15 us
  transfers between devices with their start and end apart: 11, of which 5 were waited for; matrix products, arithmetic and copies ran while one was open for 1% of the time, Pallas kernels for 4%

profile of v5, /device:TPU:1, one launch (start us, length us, event | category | flops | bytes accessed | tf_op | source)
XLA Modules:
  0.0 127.1 jit_solution(17314805831701726780)
XLA Ops:
  0.0 3.2 %shard_map.46 = (bf16[64,1024]{1,0:T(8,128)(2,1)}, f32[64,1024]{1,0:T(8,128)}) custom-call(s32[1]{0:T(128)} %bitcast.core_ref, bf16[128,1536]{1,0:T(8,128)(2,1)} %features_ref.1, bf16[1536,1024]{1,0:T(8,128)(2,1)} %w_ref.3), custom_call_target="tpu_custom_call" | custom-call | flops 402653184 | bytes 3145728 | tf_op jit(solution)/shard_map/pallas_call | solution.py:67
  3.2 8.8 %collective-permute-start = (bf16[64,1024]{1,0:T(8,128)(2,1)}, bf16[64,1024]{1,0:T(8,128)(2,1)S(1)}, u32[]{:S(2)}, u32[]{:S(2)}) collective-permute-start(bf16[64,1024]{1,0:T(8,128)(2,1)} %get-tuple-element.12), channel_id=1, source_target_pairs={{0,128},{128,0},{16,144},{144,16},{32,160},{160,32},{48,176},{176,... | collective-permute-start | bytes 393224 | tf_op jit(solution)/shard_map/ppermute | solution.py:259
  12.0 1.1 collective-permute-done
  13.1 1.0 add_convert_fusion.near_ref
  14.1 10.1 %collective-permute-start.1 = (bf16[64,1024]{1,0:T(8,128)(2,1)S(1)}, bf16[64,1024]{1,0:T(8,128)(2,1)S(1)}, u32[]{:S(2)}, u32[]{:S(2)}) collective-permute-start(bf16[64,1024]{1,0:T(8,128)(2,1)S(1)} %add_convert_fusion.near_ref), channel_id=1, source_target_pairs={{0,256},{128,384},{16,272},{144,400},{32,288},{160,416},{48,304},{... | collective-permute-start | bytes 393224 | tf_op jit(solution)/shard_map/ppermute | solution.py:259
  24.2 0.1 broadcast_select_fusion
  24.3 5.2 %collective-permute-done.1.far_ref = bf16[64,1024]{1,0:T(8,128)(2,1)S(1)} collective-permute-done((bf16[64,1024]{1,0:T(8,128)(2,1)S(1)}, bf16[64,1024]{1,0:T(8,128)(2,1)S(1)}, u32[]{:S(2)}, u32[]{:S(2)}) %collective-permute-start.1) | collective-permute-done | bytes 131104 | tf_op jit(solution)/shard_map/ppermute | solution.py:259
  29.4 0.1 broadcast_in_dim.4.signs_ref
  29.5 0.1 shard_map.47.first_ref
  29.6 7.1 %collective-permute-start.2 = (bf16[64,1152]{1,0:T(8,128)(2,1)S(1)}, bf16[64,1152]{1,0:T(8,128)(2,1)S(1)}, u32[]{:S(2)}, u32[]{:S(2)}) collective-permute-start(bf16[64,1152]{1,0:T(8,128)(2,1)S(1)} %shard_map.47.first_ref), channel_id=1, source_target_pairs={{0,64},{128,448},{16,80},{144,464},{32,96},{160,480},{48,112},{176... | collective-permute-start | bytes 442376 | tf_op jit(solution)/shard_map/ppermute | solution.py:259
  36.8 1.1 broadcast_in_dim.5
  37.9 6.7 %all-to-all-start = ((bf16[16,32,1152]{2,1,0:T(8,128)(2,1)}), bf16[16,32,1152]{2,1,0:T(8,128)(2,1)S(1)}, u32[]{:S(2)}, u32[]{:S(2)}) async-start(bf16[16,32,1152]{2,1,0:T(8,128)(2,1)} %broadcast_in_dim.5), calls=%async_computation | async-start | bytes 2359296 | tf_op jit(solution)/shard_map/all_to_all | solution.py:279
  44.6 0.0 copy-start.1
  44.7 7.0 %collective-permute-start.3 = (bf16[128,1152]{1,0:T(8,128)(2,1)S(1)}, bf16[128,1152]{1,0:T(8,128)(2,1)S(1)}, u32[]{:S(2)}, u32[]{:S(2)}) collective-permute-start(bf16[128,1152]{1,0:T(8,128)(2,1)S(1)} %shard_map.48.first_ref.refs_2_), channel_id=1, source_target_pairs={{0,128},{128,0},{16,144},{144,16},{32,160},{160,32},{48,176},{176,... | collective-permute-start | bytes 884744 | tf_op jit(solution)/shard_map/ppermute | solution.py:259
  51.6 8.6 %collective-permute-start.5 = (bf16[128,1152]{1,0:T(8,128)(2,1)S(1)}, bf16[128,1152]{1,0:T(8,128)(2,1)S(1)}, u32[]{:S(2)}, u32[]{:S(2)}) collective-permute-start(bf16[128,1152]{1,0:T(8,128)(2,1)S(1)} %shard_map.48.first_ref.refs_2_), channel_id=1, source_target_pairs={{0,32},{128,480},{16,48},{144,496},{32,64},{160,128},{48,80},{176,... | collective-permute-start | bytes 884744 | tf_op jit(solution)/shard_map/ppermute | solution.py:259
  60.3 1.9 %collective-permute-start.4 = (bf16[256,1152]{1,0:T(8,128)(2,1)S(1)}, bf16[256,1152]{1,0:T(8,128)(2,1)S(1)}, u32[]{:S(2)}, u32[]{:S(2)}) collective-permute-start(bf16[256,1152]{1,0:T(8,128)(2,1)S(1)} %shard_map.49), channel_id=1, source_target_pairs={{0,16},{128,496},{16,32},{144,128},{32,48},{160,144},{48,64},{176,... | collective-permute-start | bytes 1769480 | tf_op jit(solution)/shard_map/ppermute | solution.py:259
  62.3 1.7 %collective-permute-done.5.refs_2_ = bf16[128,1152]{1,0:T(8,128)(2,1)S(1)} collective-permute-done((bf16[128,1152]{1,0:T(8,128)(2,1)S(1)}, bf16[128,1152]{1,0:T(8,128)(2,1)S(1)}, u32[]{:S(2)}, u32[]{:S(2)}) %collective-permute-start.5) | collective-permute-done | bytes 294944 | tf_op jit(solution)/shard_map/ppermute | solution.py:259
  64.0 5.7 %collective-permute-start.6 = (bf16[128,1152]{1,0:T(8,128)(2,1)S(1)}, bf16[128,1152]{1,0:T(8,128)(2,1)S(1)}, u32[]{:S(2)}, u32[]{:S(2)}) collective-permute-start(bf16[128,1152]{1,0:T(8,128)(2,1)S(1)} %collective-permute-done.5.refs_2_), channel_id=1, source_target_pairs={{0,128},{128,0},{16,144},{144,16},{32,160},{160,32},{48,176},{176,... | collective-permute-start | bytes 884744 | tf_op jit(solution)/shard_map/ppermute | solution.py:259
  69.7 0.0 all-to-all-done
  69.7 2.2 %shard_map.50 = (f32[512,128]{1,0:T(8,128)S(1)}, f32[512,1024]{1,0:T(8,128)S(1)}) custom-call(f32[5]{0:T(128)S(1)} %copy-done.1, bf16[512,1152]{1,0:T(8,128)(2,1)S(1)} %bitcast.3, bf16[128,1152]{1,0:T(8,128)(2,1)S(1)} %shard_map.48.first_ref.refs_2_, bf16[128,1152]{1,0:T(8,128)(2,1)S(1)} %collective-permute-done.3.second_ref.refs_3_), custom_call_target="tpu_custom_call" | custom-call | flops 536870912 | bytes 2097152 | tf_op jit(solution)/shard_map/pallas_call | solution.py:235
  71.9 0.0 collective-permute-done.6.value_ref
  71.9 3.9 %collective-permute-start.7 = (bf16[256,1152]{1,0:T(8,128)(2,1)S(1)}, bf16[256,1152]{1,0:T(8,128)(2,1)S(1)}, u32[]{:S(2)}, u32[]{:S(2)}) collective-permute-start(bf16[256,1152]{1,0:T(8,128)(2,1)S(1)} %shard_map.52.refs_2_), channel_id=1, source_target_pairs={{0,128},{128,0},{16,144},{144,16},{32,160},{160,32},{48,176},{176,... | collective-permute-start | bytes 1769480 | tf_op jit(solution)/shard_map/ppermute | solution.py:259
  75.9 2.2 %shard_map.53 = (f32[512,128]{1,0:T(8,128)S(1)}, f32[512,1024]{1,0:T(8,128)S(1)}) custom-call(f32[5]{0:T(128)S(1)} %copy-done.1, bf16[512,1152]{1,0:T(8,128)(2,1)S(1)} %bitcast.4, bf16[128,1152]{1,0:T(8,128)(2,1)S(1)} %collective-permute-done.5.refs_2_, bf16[128,1152]{1,0:T(8,128)(2,1)S(1)} %shard_map.51.first_ref.refs_3_, ...), custom_call_target="tpu_custom_call" | custom-call | flops 536870912 | bytes 2097152 | tf_op jit(solution)/shard_map/pallas_call | solution.py:235
  78.1 2.8 %shard_map.54 = bf16[512,1024]{1,0:T(8,128)(2,1)S(1)} custom-call(f32[5]{0:T(128)S(1)} %copy-done.1, bf16[512,1152]{1,0:T(8,128)(2,1)S(1)} %bitcast.5, bf16[256,1152]{1,0:T(8,128)(2,1)S(1)} %shard_map.52.refs_2_, bf16[256,1152]{1,0:T(8,128)(2,1)S(1)} %collective-permute-done.7.refs_3_, f32[512,128]{1,0:T(8,128)S(1)} %get-tuple-element.15.refs_4_, ...), custom_call_target="tpu_custom_call" | custom-call | flops 1073741824 | bytes 2097152 | tf_op jit(solution)/shard_map/pallas_call | solution.py:235
  80.9 0.0 copy-start
  80.9 22.7 %all_to_all.10 = bf16[16,32,1024]{2,1,0:T(8,128)(2,1)} all-to-all(bf16[16,32,1024]{2,1,0:T(8,128)(2,1)S(1)} %bitcast.6), channel_id=1, replica_groups=mesh['tensor'=4,'row'=8,'col'=16] {'col'}, dimensions={0} | all-to-all | bytes 2097152 | tf_op jit(solution)/shard_map/all_to_all | solution.py:287
  103.6 1.4 %reduce_sum.12 = bf16[32,1024]{1,0:T(8,128)(2,1)S(1)} reduce(bf16[16,32,1024]{2,1,0:T(8,128)(2,1)} %all_to_all.10, bf16[]{:T(256)} %constant.37.clone.1), dimensions={0}, to_apply=%region_0.1 | reduce | flops 491520 | bytes 1114114 | tf_op jit(solution)/shard_map/reduce_sum | solution.py:288
  105.0 8.1 %collective-permute-start.8 = (bf16[32,1024]{1,0:T(8,128)(2,1)S(1)}, bf16[32,1024]{1,0:T(8,128)(2,1)S(1)}, u32[]{:S(2)}, u32[]{:S(2)}) collective-permute-start(bf16[32,1024]{1,0:T(8,128)(2,1)S(1)} %reduce_sum.12), channel_id=1, source_target_pairs={{0,256},{128,384},{16,272},{144,400},{32,288},{160,416},{48,304},{... | collective-permute-start | bytes 196616 | tf_op jit(solution)/shard_map/ppermute | solution.py:259
  113.1 5.7 %collective-permute-done.8 = bf16[32,1024]{1,0:T(8,128)(2,1)S(1)} collective-permute-done((bf16[32,1024]{1,0:T(8,128)(2,1)S(1)}, bf16[32,1024]{1,0:T(8,128)(2,1)S(1)}, u32[]{:S(2)}, u32[]{:S(2)}) %collective-permute-start.8) | collective-permute-done | bytes 65568 | tf_op jit(solution)/shard_map/ppermute | solution.py:259
  118.8 5.4 %collective-permute-start.9 = (bf16[64,1024]{1,0:T(8,128)(2,1)S(1)}, bf16[64,1024]{1,0:T(8,128)(2,1)S(1)}, u32[]{:S(2)}, u32[]{:S(2)}) collective-permute-start(bf16[64,1024]{1,0:T(8,128)(2,1)S(1)} %maximum_select_fusion.1), channel_id=1, source_target_pairs={{0,128},{128,0},{16,144},{144,16},{32,160},{160,32},{48,176},{176,... | collective-permute-start | bytes 393224 | tf_op jit(solution)/shard_map/ppermute | solution.py:259
  124.2 1.0 collective-permute-done.9
  125.2 1.9 %shard_map.55 = bf16[128,1536]{1,0:T(8,128)(2,1)} custom-call(bf16[128,1024]{1,0:T(8,128)(2,1)S(1)} %maximum_select_fusion.grad_ref, bf16[1536,1024]{1,0:T(8,128)(2,1)S(1)} %copy-done), custom_call_target="tpu_custom_call" | custom-call | flops 402653184 | bytes 3145728 | tf_op jit(solution)/shard_map/pallas_call | solution.py:128
  (16 shorter events, 0.2 us)
Async XLA Ops:
  0.0 12.0 %copy-start.2 = (s32[128]{0:T(128)S(1)}, s32[128]{0:T(128)}, u32[]{:S(2)}) copy-start(s32[128]{0:T(128)} %param.6) | copy-start | bytes 1540
  3.2 10.0 %collective-permute-start = (bf16[64,1024]{1,0:T(8,128)(2,1)}, bf16[64,1024]{1,0:T(8,128)(2,1)S(1)}, u32[]{:S(2)}, u32[]{:S(2)}) collective-permute-start(bf16[64,1024]{1,0:T(8,128)(2,1)} %get-tuple-element.12), channel_id=1, source_target_pairs={{0,128},{128,0},{16,144},{144,16},{32,160},{160,32},{48,176},{176,... | collective-permute-start | bytes 393224 | tf_op jit(solution)/shard_map/ppermute | solution.py:259
  14.1 15.3 %collective-permute-start.1 = (bf16[64,1024]{1,0:T(8,128)(2,1)S(1)}, bf16[64,1024]{1,0:T(8,128)(2,1)S(1)}, u32[]{:S(2)}, u32[]{:S(2)}) collective-permute-start(bf16[64,1024]{1,0:T(8,128)(2,1)S(1)} %add_convert_fusion.near_ref), channel_id=1, source_target_pairs={{0,256},{128,384},{16,272},{144,400},{32,288},{160,416},{48,304},{... | collective-permute-start | bytes 393224 | tf_op jit(solution)/shard_map/ppermute | solution.py:259
  29.6 15.0 %collective-permute-start.2 = (bf16[64,1152]{1,0:T(8,128)(2,1)S(1)}, bf16[64,1152]{1,0:T(8,128)(2,1)S(1)}, u32[]{:S(2)}, u32[]{:S(2)}) collective-permute-start(bf16[64,1152]{1,0:T(8,128)(2,1)S(1)} %shard_map.47.first_ref), channel_id=1, source_target_pairs={{0,64},{128,448},{16,80},{144,464},{32,96},{160,480},{48,112},{176... | collective-permute-start | bytes 442376 | tf_op jit(solution)/shard_map/ppermute | solution.py:259
  37.9 31.8 %all-to-all-start = ((bf16[16,32,1152]{2,1,0:T(8,128)(2,1)}), bf16[16,32,1152]{2,1,0:T(8,128)(2,1)S(1)}, u32[]{:S(2)}, u32[]{:S(2)}) async-start(bf16[16,32,1152]{2,1,0:T(8,128)(2,1)} %broadcast_in_dim.5), calls=%async_computation | async-start | bytes 2359296 | tf_op jit(solution)/shard_map/all_to_all | solution.py:279
  44.6 25.0 %copy-start.1 = (f32[5]{0:T(128)S(1)}, f32[5]{0:T(128)}, u32[]{:S(2)}) copy-start(f32[5]{0:T(128)} %refs_0_.5) | copy-start | bytes 64
  44.7 15.6 %collective-permute-start.3 = (bf16[128,1152]{1,0:T(8,128)(2,1)S(1)}, bf16[128,1152]{1,0:T(8,128)(2,1)S(1)}, u32[]{:S(2)}, u32[]{:S(2)}) collective-permute-start(bf16[128,1152]{1,0:T(8,128)(2,1)S(1)} %shard_map.48.first_ref.refs_2_), channel_id=1, source_target_pairs={{0,128},{128,0},{16,144},{144,16},{32,160},{160,32},{48,176},{176,... | collective-permute-start | bytes 884744 | tf_op jit(solution)/shard_map/ppermute | solution.py:259
  51.6 12.3 %collective-permute-start.5 = (bf16[128,1152]{1,0:T(8,128)(2,1)S(1)}, bf16[128,1152]{1,0:T(8,128)(2,1)S(1)}, u32[]{:S(2)}, u32[]{:S(2)}) collective-permute-start(bf16[128,1152]{1,0:T(8,128)(2,1)S(1)} %shard_map.48.first_ref.refs_2_), channel_id=1, source_target_pairs={{0,32},{128,480},{16,48},{144,496},{32,64},{160,128},{48,80},{176,... | collective-permute-start | bytes 884744 | tf_op jit(solution)/shard_map/ppermute | solution.py:259
  60.3 11.6 %collective-permute-start.4 = (bf16[256,1152]{1,0:T(8,128)(2,1)S(1)}, bf16[256,1152]{1,0:T(8,128)(2,1)S(1)}, u32[]{:S(2)}, u32[]{:S(2)}) collective-permute-start(bf16[256,1152]{1,0:T(8,128)(2,1)S(1)} %shard_map.49), channel_id=1, source_target_pairs={{0,16},{128,496},{16,32},{144,128},{32,48},{160,144},{48,64},{176,... | collective-permute-start | bytes 1769480 | tf_op jit(solution)/shard_map/ppermute | solution.py:259
  64.0 7.9 %collective-permute-start.6 = (bf16[128,1152]{1,0:T(8,128)(2,1)S(1)}, bf16[128,1152]{1,0:T(8,128)(2,1)S(1)}, u32[]{:S(2)}, u32[]{:S(2)}) collective-permute-start(bf16[128,1152]{1,0:T(8,128)(2,1)S(1)} %collective-permute-done.5.refs_2_), channel_id=1, source_target_pairs={{0,128},{128,0},{16,144},{144,16},{32,160},{160,32},{48,176},{176,... | collective-permute-start | bytes 884744 | tf_op jit(solution)/shard_map/ppermute | solution.py:259
  71.9 6.2 %collective-permute-start.7 = (bf16[256,1152]{1,0:T(8,128)(2,1)S(1)}, bf16[256,1152]{1,0:T(8,128)(2,1)S(1)}, u32[]{:S(2)}, u32[]{:S(2)}) collective-permute-start(bf16[256,1152]{1,0:T(8,128)(2,1)S(1)} %shard_map.52.refs_2_), channel_id=1, source_target_pairs={{0,128},{128,0},{16,144},{144,16},{32,160},{160,32},{48,176},{176,... | collective-permute-start | bytes 1769480 | tf_op jit(solution)/shard_map/ppermute | solution.py:259
  80.9 44.3 %copy-start = (bf16[1536,1024]{1,0:T(8,128)(2,1)S(1)}, bf16[1536,1024]{1,0:T(8,128)(2,1)}, u32[]{:S(2)}) copy-start(bf16[1536,1024]{1,0:T(8,128)(2,1)} %w_ref.3) | copy-start | bytes 9437188
  105.0 13.8 %collective-permute-start.8 = (bf16[32,1024]{1,0:T(8,128)(2,1)S(1)}, bf16[32,1024]{1,0:T(8,128)(2,1)S(1)}, u32[]{:S(2)}, u32[]{:S(2)}) collective-permute-start(bf16[32,1024]{1,0:T(8,128)(2,1)S(1)} %reduce_sum.12), channel_id=1, source_target_pairs={{0,256},{128,384},{16,272},{144,400},{32,288},{160,416},{48,304},{... | collective-permute-start | bytes 196616 | tf_op jit(solution)/shard_map/ppermute | solution.py:259
  118.8 6.4 %collective-permute-start.9 = (bf16[64,1024]{1,0:T(8,128)(2,1)S(1)}, bf16[64,1024]{1,0:T(8,128)(2,1)S(1)}, u32[]{:S(2)}, u32[]{:S(2)}) collective-permute-start(bf16[64,1024]{1,0:T(8,128)(2,1)S(1)} %maximum_select_fusion.1), channel_id=1, source_target_pairs={{0,128},{128,0},{16,144},{144,16},{32,160},{160,32},{48,176},{176,... | collective-permute-start | bytes 393224 | tf_op jit(solution)/shard_map/ppermute | solution.py:259

commit v6 on v5

--- a/solution.py
+++ b/solution.py
@@ -87,10 +87,10 @@
     )(core, features, w_proj)
 
 
-def block_kernel(near_ref, far_ref, signs_ref, block_ref):
+def block_kernel(near_ref, far_ref, block_ref):
     f32, bf16 = jnp.float32, jnp.bfloat16
-    half, width = near_ref.shape
-    rows = (near_ref[...].astype(f32) + far_ref[...].astype(f32)).astype(bf16)
+    half, width = far_ref.shape
+    rows = (near_ref[:, :width].astype(f32) + far_ref[...].astype(f32)).astype(bf16)
     block_ref[:, :width] = rows
     norm = jnp.sum(jnp.square(rows.astype(f32)), axis=1, keepdims=True)
     first = norm.astype(bf16).astype(f32)
@@ -98,22 +98,22 @@
     third = norm - first - second
     lane = lax.broadcasted_iota(jnp.int32, (half, PAD), 1)
     tail = jnp.where(lane == 1, first, jnp.where(lane == 2, second, third))
-    block_ref[:, width:] = jnp.where(lane == 0, signs_ref[...], tail).astype(bf16)
-
-
-def whole_block(near, far, signs):
+    block_ref[:, width:] = jnp.where(lane == 0, near_ref[:, width:].astype(f32), tail).astype(bf16)
+
+
+def whole_block(near, far):
     vmem = pl.BlockSpec(memory_space=pltpu.VMEM)
-    half, width = near.shape
+    half, width = far.shape
     return pl.pallas_call(
         block_kernel,
         out_shape=jax.ShapeDtypeStruct((half, width + PAD), near.dtype),
-        in_specs=[vmem] * 3,
+        in_specs=[vmem] * 2,
         out_specs=vmem,
         compiler_params=pltpu.CompilerParams(vmem_limit_bytes=16 * 2**20),
         cost_estimate=pl.CostEstimate(
             flops=4 * half * width, bytes_accessed=6 * half * width, transcendentals=0
         ),
-    )(near, far, signs)
+    )(near, far)
 
 
 def result_kernel(grad_ref, w_ref, out_ref):
@@ -263,12 +263,17 @@
 
     away, kept = projection(jnp.reshape(tpos % 2, (1,)), features, w_proj)
     partial = (kept + other_core(away).astype(f32)).astype(bf16)
-    far = move(partial, lambda chip, core: (chip + n_row, core))
-    signs = (1 - 2 * flags).astype(f32)
+    signs = (1 - 2 * flags).astype(bf16)
     s_half = pick(core, signs[:half], signs[half:])
-    block = whole_block(partial, far, jnp.broadcast_to(s_half[:, None], (half, PAD)))
-
-    far_block = move(block, lambda chip, core: (chip + (n_row // 2) * (1 - 2 * core), core))
+    signed = jnp.concatenate([partial, jnp.broadcast_to(s_half[:, None], (half, PAD))], axis=1)
+
+    step = n_row // 2
+    block = whole_block(
+        move(signed, lambda chip, core: (chip + step, core)),
+        move(partial, lambda chip, core: (chip - step, core)),
+    )
+
+    far_block = move(block, lambda chip, core: (chip + step * (1 - 2 * core), core))
     pair = side_by_side(block, far_block, FLOPS)
     two_away = move(pair, lambda chip, core: (chip + 2 - 4 * core, core))
     other_pair = other_core(pair)
@@ -286,9 +291,12 @@
     part = tiles([one_away, other_core(one_away)], col, rates, sums, True)
     parts = lax.all_to_all(part.reshape(n_col, quarter, width), "col", 0, 0, tiled=True)
     grad = jnp.sum(parts.astype(f32), axis=0).astype(bf16)
-    grad_far = move(grad, lambda chip, core: (chip + n_row, core))
+    above = move(grad, lambda chip, core: (chip - step, core))
+    below = move(grad, lambda chip, core: (chip + step, core))
     grad = pick(
-        high, jnp.concatenate([grad, grad_far], axis=0), jnp.concatenate([grad_far, grad], axis=0)
+        high ^ (lax.axis_index("row") >= step),
+        jnp.concatenate([above, below], axis=0),
+        jnp.concatenate([below, above], axis=0),
     )
     grad_other = other_core(grad)
     grad = pick(

time: 128 us -> 129 us (level)
  waiting for transfers between devices: 14.7 us -> 26.6 us
  starting transfers between devices: 73.3 us -> 62.6 us
    ppermute x10 -> x12, waiting for transfers between devices: 14.7 us -> 26.6 us  [move(): return lax.ppermute(value, ZLINE, line_permutation(shift, n_row))]
    ppermute x10 -> x12, starting transfers between devices: 66.6 us -> 56.2 us  [move(): return lax.ppermute(value, ZLINE, line_permutation(shift, n_row))]
  transfers between devices with their start and end apart: 11 -> 13, of which waited for: 5 -> 7; matrix products, arithmetic and copies ran while one was open for 1% -> 1% of each run, Pallas kernels for 4% -> 3%
where the time goes in v6:
time: 129 us
  starting transfers between devices  62.6 us (49%)
  waiting for transfers between devices  26.6 us (21%)
  blocking collectives  22.9 us (18%)
  Pallas kernels  12.5 us (10%)
  other arithmetic  2.58 us (2%)
    ppermute x12, starting transfers between devices, move(): return lax.ppermute(value, ZLINE, line_permutation(shift, n_row))  56.2 us
    ppermute x12, waiting for transfers between devices, move(): return lax.ppermute(value, ZLINE, line_permutation(shift, n_row))  26.6 us
    all_to_all x1, blocking collectives, shards(): lax.all_to_all(part.reshape(n_col, quarter, width), 'col', 0, 0, tiled=True)  22.9 us
    pallas_call x3, Pallas kernels, tiles(): pl.pallas_call(functools.partial(tile_kernel, len(pieces), bool(held), la...  7.21 us
    all_to_all x1, starting transfers between devices, shards(): lax.all_to_all(jnp.broadcast_to(own[None], (n_col,) + own.shape), 'col',...  6.41 us
    pallas_call x1, Pallas kernels, projection(): pl.pallas_call(projection_kernel, out_shape=(jax.ShapeDtypeStruct((rows /...  3.15 us
  transfers between devices with their start and end apart: 13, of which 7 were waited for; matrix products, arithmetic and copies ran while one was open for 1% of the time, Pallas kernels for 3%

profile of v6, /device:TPU:1, one launch (start us, length us, event | category | flops | bytes accessed | tf_op | source)
XLA Modules:
  0.0 128.7 jit_solution(9984755836513700429)
XLA Ops:
  0.0 3.2 %shard_map.46 = (bf16[64,1024]{1,0:T(8,128)(2,1)}, f32[64,1024]{1,0:T(8,128)}) custom-call(s32[1]{0:T(128)} %bitcast.core_ref, bf16[128,1536]{1,0:T(8,128)(2,1)} %features_ref.1, bf16[1536,1024]{1,0:T(8,128)(2,1)} %w_ref.3), custom_call_target="tpu_custom_call" | custom-call | flops 402653184 | bytes 3145728 | tf_op jit(solution)/shard_map/pallas_call | solution.py:67
  3.2 8.8 %collective-permute-start = (bf16[64,1024]{1,0:T(8,128)(2,1)}, bf16[64,1024]{1,0:T(8,128)(2,1)S(1)}, u32[]{:S(2)}, u32[]{:S(2)}) collective-permute-start(bf16[64,1024]{1,0:T(8,128)(2,1)} %get-tuple-element.12), channel_id=1, source_target_pairs={{0,128},{128,0},{16,144},{144,16},{32,160},{160,32},{48,176},{176,... | collective-permute-start | bytes 393224 | tf_op jit(solution)/shard_map/ppermute | solution.py:259
  12.0 0.1 broadcast_select_fusion
  12.0 1.1 collective-permute-done
  13.1 1.0 add_convert_fusion
  14.1 0.1 broadcast_in_dim.4
  14.2 3.5 %collective-permute-start.1 = (bf16[64,1152]{1,0:T(8,128)(2,1)S(1)}, bf16[64,1152]{1,0:T(8,128)(2,1)S(1)}, u32[]{:S(2)}, u32[]{:S(2)}) collective-permute-start(bf16[64,1152]{1,0:T(8,128)(2,1)S(1)} %pad_maximum_fusion), channel_id=1, source_target_pairs={{0,64},{128,192},{16,80},{144,208},{32,96},{160,224},{48,112},{176... | collective-permute-start | bytes 442376 | tf_op jit(solution)/shard_map/ppermute | solution.py:259
  17.7 5.7 %collective-permute-start.2 = (bf16[64,1024]{1,0:T(8,128)(2,1)S(1)}, bf16[64,1024]{1,0:T(8,128)(2,1)S(1)}, u32[]{:S(2)}, u32[]{:S(2)}) collective-permute-start(bf16[64,1024]{1,0:T(8,128)(2,1)S(1)} %add_convert_fusion), channel_id=1, source_target_pairs={{0,320},{128,448},{16,336},{144,464},{32,352},{160,480},{48,368},{... | collective-permute-start | bytes 393224 | tf_op jit(solution)/shard_map/ppermute | solution.py:259
  23.4 15.1 %collective-permute-done.2.far_ref = bf16[64,1024]{1,0:T(8,128)(2,1)S(1)} collective-permute-done((bf16[64,1024]{1,0:T(8,128)(2,1)S(1)}, bf16[64,1024]{1,0:T(8,128)(2,1)S(1)}, u32[]{:S(2)}, u32[]{:S(2)}) %collective-permute-start.2) | collective-permute-done | bytes 131104 | tf_op jit(solution)/shard_map/ppermute | solution.py:259
  38.5 0.1 shard_map.47.first_ref
  38.7 4.4 %collective-permute-start.3 = (bf16[64,1152]{1,0:T(8,128)(2,1)S(1)}, bf16[64,1152]{1,0:T(8,128)(2,1)S(1)}, u32[]{:S(2)}, u32[]{:S(2)}) collective-permute-start(bf16[64,1152]{1,0:T(8,128)(2,1)S(1)} %shard_map.47.first_ref), channel_id=1, source_target_pairs={{0,64},{128,448},{16,80},{144,464},{32,96},{160,480},{48,112},{176... | collective-permute-start | bytes 442376 | tf_op jit(solution)/shard_map/ppermute | solution.py:259
  43.1 1.1 broadcast_in_dim.5
  44.2 6.4 %all-to-all-start = ((bf16[16,32,1152]{2,1,0:T(8,128)(2,1)}), bf16[16,32,1152]{2,1,0:T(8,128)(2,1)S(1)}, u32[]{:S(2)}, u32[]{:S(2)}) async-start(bf16[16,32,1152]{2,1,0:T(8,128)(2,1)} %broadcast_in_dim.5), calls=%async_computation | async-start | bytes 2359296 | tf_op jit(solution)/shard_map/all_to_all | solution.py:284
  50.7 6.5 %collective-permute-start.4 = (bf16[128,1152]{1,0:T(8,128)(2,1)S(1)}, bf16[128,1152]{1,0:T(8,128)(2,1)S(1)}, u32[]{:S(2)}, u32[]{:S(2)}) collective-permute-start(bf16[128,1152]{1,0:T(8,128)(2,1)S(1)} %shard_map.48.first_ref.refs_2_), channel_id=1, source_target_pairs={{0,128},{128,0},{16,144},{144,16},{32,160},{160,32},{48,176},{176,... | collective-permute-start | bytes 884744 | tf_op jit(solution)/shard_map/ppermute | solution.py:259
  57.2 1.9 %collective-permute-start.6 = (bf16[128,1152]{1,0:T(8,128)(2,1)S(1)}, bf16[128,1152]{1,0:T(8,128)(2,1)S(1)}, u32[]{:S(2)}, u32[]{:S(2)}) collective-permute-start(bf16[128,1152]{1,0:T(8,128)(2,1)S(1)} %shard_map.48.first_ref.refs_2_), channel_id=1, source_target_pairs={{0,32},{128,480},{16,48},{144,496},{32,64},{160,128},{48,80},{176,... | collective-permute-start | bytes 884744 | tf_op jit(solution)/shard_map/ppermute | solution.py:259
  59.2 1.9 %collective-permute-start.5 = (bf16[256,1152]{1,0:T(8,128)(2,1)S(1)}, bf16[256,1152]{1,0:T(8,128)(2,1)S(1)}, u32[]{:S(2)}, u32[]{:S(2)}) collective-permute-start(bf16[256,1152]{1,0:T(8,128)(2,1)S(1)} %shard_map.49), channel_id=1, source_target_pairs={{0,16},{128,496},{16,32},{144,128},{32,48},{160,144},{48,64},{176,... | collective-permute-start | bytes 1769480 | tf_op jit(solution)/shard_map/ppermute | solution.py:259
  61.1 6.6 %collective-permute-done.6.refs_2_ = bf16[128,1152]{1,0:T(8,128)(2,1)S(1)} collective-permute-done((bf16[128,1152]{1,0:T(8,128)(2,1)S(1)}, bf16[128,1152]{1,0:T(8,128)(2,1)S(1)}, u32[]{:S(2)}, u32[]{:S(2)}) %collective-permute-start.6) | collective-permute-done | bytes 294944 | tf_op jit(solution)/shard_map/ppermute | solution.py:259
  67.7 3.0 %collective-permute-start.7 = (bf16[128,1152]{1,0:T(8,128)(2,1)S(1)}, bf16[128,1152]{1,0:T(8,128)(2,1)S(1)}, u32[]{:S(2)}, u32[]{:S(2)}) collective-permute-start(bf16[128,1152]{1,0:T(8,128)(2,1)S(1)} %collective-permute-done.6.refs_2_), channel_id=1, source_target_pairs={{0,128},{128,0},{16,144},{144,16},{32,160},{160,32},{48,176},{176,... | collective-permute-start | bytes 884744 | tf_op jit(solution)/shard_map/ppermute | solution.py:259
  70.8 2.2 %shard_map.50 = (f32[512,128]{1,0:T(8,128)S(1)}, f32[512,1024]{1,0:T(8,128)S(1)}) custom-call(f32[5]{0:T(128)S(1)} %copy-done.1, bf16[512,1152]{1,0:T(8,128)(2,1)S(1)} %bitcast.3, bf16[128,1152]{1,0:T(8,128)(2,1)S(1)} %shard_map.48.first_ref.refs_2_, bf16[128,1152]{1,0:T(8,128)(2,1)S(1)} %collective-permute-done.4.second_ref.refs_3_), custom_call_target="tpu_custom_call" | custom-call | flops 536870912 | bytes 2097152 | tf_op jit(solution)/shard_map/pallas_call | solution.py:235
  73.0 0.1 collective-permute-done.5.value_ref
  73.2 3.9 %collective-permute-start.8 = (bf16[256,1152]{1,0:T(8,128)(2,1)S(1)}, bf16[256,1152]{1,0:T(8,128)(2,1)S(1)}, u32[]{:S(2)}, u32[]{:S(2)}) collective-permute-start(bf16[256,1152]{1,0:T(8,128)(2,1)S(1)} %shard_map.52.refs_2_), channel_id=1, source_target_pairs={{0,128},{128,0},{16,144},{144,16},{32,160},{160,32},{48,176},{176,... | collective-permute-start | bytes 1769480 | tf_op jit(solution)/shard_map/ppermute | solution.py:259
  77.1 2.2 %shard_map.53 = (f32[512,128]{1,0:T(8,128)S(1)}, f32[512,1024]{1,0:T(8,128)S(1)}) custom-call(f32[5]{0:T(128)S(1)} %copy-done.1, bf16[512,1152]{1,0:T(8,128)(2,1)S(1)} %bitcast.4, bf16[128,1152]{1,0:T(8,128)(2,1)S(1)} %collective-permute-done.6.refs_2_, bf16[128,1152]{1,0:T(8,128)(2,1)S(1)} %shard_map.51.first_ref.refs_3_, ...), custom_call_target="tpu_custom_call" | custom-call | flops 536870912 | bytes 2097152 | tf_op jit(solution)/shard_map/pallas_call | solution.py:235
  79.4 2.8 %shard_map.54 = bf16[512,1024]{1,0:T(8,128)(2,1)S(1)} custom-call(f32[5]{0:T(128)S(1)} %copy-done.1, bf16[512,1152]{1,0:T(8,128)(2,1)S(1)} %bitcast.5, bf16[256,1152]{1,0:T(8,128)(2,1)S(1)} %shard_map.52.refs_2_, bf16[256,1152]{1,0:T(8,128)(2,1)S(1)} %collective-permute-done.8.refs_3_, f32[512,128]{1,0:T(8,128)S(1)} %get-tuple-element.15.refs_4_, ...), custom_call_target="tpu_custom_call" | custom-call | flops 1073741824 | bytes 2097152 | tf_op jit(solution)/shard_map/pallas_call | solution.py:235
  82.2 22.9 %all_to_all.10 = bf16[16,32,1024]{2,1,0:T(8,128)(2,1)} all-to-all(bf16[16,32,1024]{2,1,0:T(8,128)(2,1)S(1)} %bitcast.6), channel_id=1, replica_groups=mesh['tensor'=4,'row'=8,'col'=16] {'col'}, dimensions={0} | all-to-all | bytes 2097152 | tf_op jit(solution)/shard_map/all_to_all | solution.py:292
  105.0 1.4 %reduce_sum.12 = bf16[32,1024]{1,0:T(8,128)(2,1)S(1)} reduce(bf16[16,32,1024]{2,1,0:T(8,128)(2,1)} %all_to_all.10, bf16[]{:T(256)} %constant.44.clone.1), dimensions={0}, to_apply=%region_0.1 | reduce | flops 491520 | bytes 1114114 | tf_op jit(solution)/shard_map/reduce_sum | solution.py:293
  106.4 2.7 %collective-permute-start.10 = (bf16[32,1024]{1,0:T(8,128)(2,1)S(1)}, bf16[32,1024]{1,0:T(8,128)(2,1)S(1)}, u32[]{:S(2)}, u32[]{:S(2)}) collective-permute-start(bf16[32,1024]{1,0:T(8,128)(2,1)S(1)} %reduce_sum.12), channel_id=1, source_target_pairs={{0,320},{128,448},{16,336},{144,464},{32,352},{160,480},{48,368},{... | collective-permute-start | bytes 196616 | tf_op jit(solution)/shard_map/ppermute | solution.py:259
  109.1 6.5 %collective-permute-start.9 = (bf16[32,1024]{1,0:T(8,128)(2,1)S(1)}, bf16[32,1024]{1,0:T(8,128)(2,1)S(1)}, u32[]{:S(2)}, u32[]{:S(2)}) collective-permute-start(bf16[32,1024]{1,0:T(8,128)(2,1)S(1)} %reduce_sum.12), channel_id=1, source_target_pairs={{0,64},{128,192},{16,80},{144,208},{32,96},{160,224},{48,112},{176... | collective-permute-start | bytes 196616 | tf_op jit(solution)/shard_map/ppermute | solution.py:259
  115.7 2.1 %collective-permute-done.10 = bf16[32,1024]{1,0:T(8,128)(2,1)S(1)} collective-permute-done((bf16[32,1024]{1,0:T(8,128)(2,1)S(1)}, bf16[32,1024]{1,0:T(8,128)(2,1)S(1)}, u32[]{:S(2)}, u32[]{:S(2)}) %collective-permute-start.10) | collective-permute-done | bytes 65568 | tf_op jit(solution)/shard_map/ppermute | solution.py:259
  117.8 0.6 collective-permute-done.9
  118.4 7.3 %collective-permute-start.11 = (bf16[64,1024]{1,0:T(8,128)(2,1)S(1)}, bf16[64,1024]{1,0:T(8,128)(2,1)S(1)}, u32[]{:S(2)}, u32[]{:S(2)}) collective-permute-start(bf16[64,1024]{1,0:T(8,128)(2,1)S(1)} %maximum_select_fusion.1), channel_id=1, source_target_pairs={{0,128},{128,0},{16,144},{144,16},{32,160},{160,32},{48,176},{176,... | collective-permute-start | bytes 393224 | tf_op jit(solution)/shard_map/ppermute | solution.py:259
  125.7 1.0 collective-permute-done.11
  126.8 1.9 %shard_map.55 = bf16[128,1536]{1,0:T(8,128)(2,1)} custom-call(bf16[128,1024]{1,0:T(8,128)(2,1)S(1)} %maximum_select_fusion.grad_ref, bf16[1536,1024]{1,0:T(8,128)(2,1)S(1)} %copy-done), custom_call_target="tpu_custom_call" | custom-call | flops 402653184 | bytes 3145728 | tf_op jit(solution)/shard_map/pallas_call | solution.py:128
  (21 shorter events, 0.2 us)
Async XLA Ops:
  0.0 11.9 %copy-start.2 = (s32[128]{0:T(128)S(1)}, s32[128]{0:T(128)}, u32[]{:S(2)}) copy-start(s32[128]{0:T(128)} %param.6) | copy-start | bytes 1540
  3.2 10.0 %collective-permute-start = (bf16[64,1024]{1,0:T(8,128)(2,1)}, bf16[64,1024]{1,0:T(8,128)(2,1)S(1)}, u32[]{:S(2)}, u32[]{:S(2)}) collective-permute-start(bf16[64,1024]{1,0:T(8,128)(2,1)} %get-tuple-element.12), channel_id=1, source_target_pairs={{0,128},{128,0},{16,144},{144,16},{32,160},{160,32},{48,176},{176,... | collective-permute-start | bytes 393224 | tf_op jit(solution)/shard_map/ppermute | solution.py:259
  14.2 24.3 %collective-permute-start.1 = (bf16[64,1152]{1,0:T(8,128)(2,1)S(1)}, bf16[64,1152]{1,0:T(8,128)(2,1)S(1)}, u32[]{:S(2)}, u32[]{:S(2)}) collective-permute-start(bf16[64,1152]{1,0:T(8,128)(2,1)S(1)} %pad_maximum_fusion), channel_id=1, source_target_pairs={{0,64},{128,192},{16,80},{144,208},{32,96},{160,224},{48,112},{176... | collective-permute-start | bytes 442376 | tf_op jit(solution)/shard_map/ppermute | solution.py:259
  17.7 20.9 %collective-permute-start.2 = (bf16[64,1024]{1,0:T(8,128)(2,1)S(1)}, bf16[64,1024]{1,0:T(8,128)(2,1)S(1)}, u32[]{:S(2)}, u32[]{:S(2)}) collective-permute-start(bf16[64,1024]{1,0:T(8,128)(2,1)S(1)} %add_convert_fusion), channel_id=1, source_target_pairs={{0,320},{128,448},{16,336},{144,464},{32,352},{160,480},{48,368},{... | collective-permute-start | bytes 393224 | tf_op jit(solution)/shard_map/ppermute | solution.py:259
  38.7 12.0 %collective-permute-start.3 = (bf16[64,1152]{1,0:T(8,128)(2,1)S(1)}, bf16[64,1152]{1,0:T(8,128)(2,1)S(1)}, u32[]{:S(2)}, u32[]{:S(2)}) collective-permute-start(bf16[64,1152]{1,0:T(8,128)(2,1)S(1)} %shard_map.47.first_ref), channel_id=1, source_target_pairs={{0,64},{128,448},{16,80},{144,464},{32,96},{160,480},{48,112},{176... | collective-permute-start | bytes 442376 | tf_op jit(solution)/shard_map/ppermute | solution.py:259
  44.2 26.6 %all-to-all-start = ((bf16[16,32,1152]{2,1,0:T(8,128)(2,1)}), bf16[16,32,1152]{2,1,0:T(8,128)(2,1)S(1)}, u32[]{:S(2)}, u32[]{:S(2)}) async-start(bf16[16,32,1152]{2,1,0:T(8,128)(2,1)} %broadcast_in_dim.5), calls=%async_computation | async-start | bytes 2359296 | tf_op jit(solution)/shard_map/all_to_all | solution.py:284
  50.6 20.2 %copy-start.1 = (f32[5]{0:T(128)S(1)}, f32[5]{0:T(128)}, u32[]{:S(2)}) copy-start(f32[5]{0:T(128)} %refs_0_.5) | copy-start | bytes 64
  50.7 8.5 %collective-permute-start.4 = (bf16[128,1152]{1,0:T(8,128)(2,1)S(1)}, bf16[128,1152]{1,0:T(8,128)(2,1)S(1)}, u32[]{:S(2)}, u32[]{:S(2)}) collective-permute-start(bf16[128,1152]{1,0:T(8,128)(2,1)S(1)} %shard_map.48.first_ref.refs_2_), channel_id=1, source_target_pairs={{0,128},{128,0},{16,144},{144,16},{32,160},{160,32},{48,176},{176,... | collective-permute-start | bytes 884744 | tf_op jit(solution)/shard_map/ppermute | solution.py:259
  57.2 10.5 %collective-permute-start.6 = (bf16[128,1152]{1,0:T(8,128)(2,1)S(1)}, bf16[128,1152]{1,0:T(8,128)(2,1)S(1)}, u32[]{:S(2)}, u32[]{:S(2)}) collective-permute-start(bf16[128,1152]{1,0:T(8,128)(2,1)S(1)} %shard_map.48.first_ref.refs_2_), channel_id=1, source_target_pairs={{0,32},{128,480},{16,48},{144,496},{32,64},{160,128},{48,80},{176,... | collective-permute-start | bytes 884744 | tf_op jit(solution)/shard_map/ppermute | solution.py:259
  59.2 14.0 %collective-permute-start.5 = (bf16[256,1152]{1,0:T(8,128)(2,1)S(1)}, bf16[256,1152]{1,0:T(8,128)(2,1)S(1)}, u32[]{:S(2)}, u32[]{:S(2)}) collective-permute-start(bf16[256,1152]{1,0:T(8,128)(2,1)S(1)} %shard_map.49), channel_id=1, source_target_pairs={{0,16},{128,496},{16,32},{144,128},{32,48},{160,144},{48,64},{176,... | collective-permute-start | bytes 1769480 | tf_op jit(solution)/shard_map/ppermute | solution.py:259
  67.7 5.3 %collective-permute-start.7 = (bf16[128,1152]{1,0:T(8,128)(2,1)S(1)}, bf16[128,1152]{1,0:T(8,128)(2,1)S(1)}, u32[]{:S(2)}, u32[]{:S(2)}) collective-permute-start(bf16[128,1152]{1,0:T(8,128)(2,1)S(1)} %collective-permute-done.6.refs_2_), channel_id=1, source_target_pairs={{0,128},{128,0},{16,144},{144,16},{32,160},{160,32},{48,176},{176,... | collective-permute-start | bytes 884744 | tf_op jit(solution)/shard_map/ppermute | solution.py:259
  73.2 6.2 %collective-permute-start.8 = (bf16[256,1152]{1,0:T(8,128)(2,1)S(1)}, bf16[256,1152]{1,0:T(8,128)(2,1)S(1)}, u32[]{:S(2)}, u32[]{:S(2)}) collective-permute-start(bf16[256,1152]{1,0:T(8,128)(2,1)S(1)} %shard_map.52.refs_2_), channel_id=1, source_target_pairs={{0,128},{128,0},{16,144},{144,16},{32,160},{160,32},{48,176},{176,... | collective-permute-start | bytes 1769480 | tf_op jit(solution)/shard_map/ppermute | solution.py:259
  82.2 44.6 %copy-start = (bf16[1536,1024]{1,0:T(8,128)(2,1)S(1)}, bf16[1536,1024]{1,0:T(8,128)(2,1)}, u32[]{:S(2)}) copy-start(bf16[1536,1024]{1,0:T(8,128)(2,1)} %w_ref.3) | copy-start | bytes 9437188
  106.4 11.3 %collective-permute-start.10 = (bf16[32,1024]{1,0:T(8,128)(2,1)S(1)}, bf16[32,1024]{1,0:T(8,128)(2,1)S(1)}, u32[]{:S(2)}, u32[]{:S(2)}) collective-permute-start(bf16[32,1024]{1,0:T(8,128)(2,1)S(1)} %reduce_sum.12), channel_id=1, source_target_pairs={{0,320},{128,448},{16,336},{144,464},{32,352},{160,480},{48,368},{... | collective-permute-start | bytes 196616 | tf_op jit(solution)/shard_map/ppermute | solution.py:259
  109.1 9.2 %collective-permute-start.9 = (bf16[32,1024]{1,0:T(8,128)(2,1)S(1)}, bf16[32,1024]{1,0:T(8,128)(2,1)S(1)}, u32[]{:S(2)}, u32[]{:S(2)}) collective-permute-start(bf16[32,1024]{1,0:T(8,128)(2,1)S(1)} %reduce_sum.12), channel_id=1, source_target_pairs={{0,64},{128,192},{16,80},{144,208},{32,96},{160,224},{48,112},{176... | collective-permute-start | bytes 196616 | tf_op jit(solution)/shard_map/ppermute | solution.py:259
  118.4 8.3 %collective-permute-start.11 = (bf16[64,1024]{1,0:T(8,128)(2,1)S(1)}, bf16[64,1024]{1,0:T(8,128)(2,1)S(1)}, u32[]{:S(2)}, u32[]{:S(2)}) collective-permute-start(bf16[64,1024]{1,0:T(8,128)(2,1)S(1)} %maximum_select_fusion.1), channel_id=1, source_target_pairs={{0,128},{128,0},{16,144},{144,16},{32,160},{160,32},{48,176},{176,... | collective-permute-start | bytes 393224 | tf_op jit(solution)/shard_map/ppermute | solution.py:259

commit v7 on v5

--- a/solution.py
+++ b/solution.py
@@ -135,6 +135,27 @@
             flops=2 * rows * w_proj.size, bytes_accessed=2 * w_proj.size, transcendentals=0
         ),
     )(grad, w_proj)
+
+
+def sum_kernel(parts_ref, out_ref):
+    total = parts_ref[0].astype(jnp.float32)
+    for index in range(1, parts_ref.shape[0]):
+        total += parts_ref[index].astype(jnp.float32)
+    out_ref[...] = total.astype(out_ref.dtype)
+
+
+def summed(parts):
+    vmem = pl.BlockSpec(memory_space=pltpu.VMEM)
+    return pl.pallas_call(
+        sum_kernel,
+        out_shape=jax.ShapeDtypeStruct(parts.shape[1:], parts.dtype),
+        in_specs=[vmem],
+        out_specs=vmem,
+        compiler_params=pltpu.CompilerParams(vmem_limit_bytes=16 * 2**20),
+        cost_estimate=pl.CostEstimate(
+            flops=parts.size, bytes_accessed=2 * parts.size, transcendentals=0
+        ),
+    )(parts)
 
 
 def pair_kernel(first_ref, second_ref, out_ref):
@@ -270,22 +291,23 @@
 
     far_block = move(block, lambda chip, core: (chip + (n_row // 2) * (1 - 2 * core), core))
     pair = side_by_side(block, far_block, FLOPS)
+    other_pair = other_core(pair)
     two_away = move(pair, lambda chip, core: (chip + 2 - 4 * core, core))
-    other_pair = other_core(pair)
-    one_away = move(
-        side_by_side(pair, other_pair, 0), lambda chip, core: (chip + 1 - 2 * core, core)
-    )
+    next_own = move(pair, lambda chip, core: (chip + 1 - 2 * core, core))
+    next_other = move(other_pair, lambda chip, core: (chip + 1 - 2 * core, core))
     own = pick(high, block[:quarter], block[quarter:])
     col = lax.all_to_all(
         jnp.broadcast_to(own[None], (n_col,) + own.shape), "col", 0, 0, tiled=True
     ).reshape(n_col * quarter, width + PAD)
     sums = tiles([pair, other_pair], col, rates)
-    other_two_away = after(other_core(two_away), sums[0], FLOPS // 20)
-    one_away = after(one_away, other_two_away, 0)
-    sums = tiles([two_away, other_two_away], col, rates, sums, False)
-    part = tiles([one_away, other_core(one_away)], col, rates, sums, True)
+    two_away = after(two_away, sums[0], 0)
+    next_own = after(next_own, sums[0], 0)
+    middle = [two_away, other_core(two_away), next_own, other_core(next_own)]
+    sums = tiles(middle, col, rates, sums, False)
+    next_other = after(next_other, middle[1], 0)
+    part = tiles([next_other, other_core(next_other)], col, rates, sums, True)
     parts = lax.all_to_all(part.reshape(n_col, quarter, width), "col", 0, 0, tiled=True)
-    grad = jnp.sum(parts.astype(f32), axis=0).astype(bf16)
+    grad = summed(parts)
     grad_far = move(grad, lambda chip, core: (chip + n_row, core))
     grad = pick(
         high, jnp.concatenate([grad, grad_far], axis=0), jnp.concatenate([grad_far, grad], axis=0)

time: 128 us -> 127 us (level)
  waiting for transfers between devices: 14.7 us -> 12.9 us
  starting transfers between devices: 73.3 us -> 75 us
  other arithmetic: 2.56 us -> 1.14 us
    ppermute x10 -> x12, waiting for transfers between devices: 14.7 us -> 12.9 us  [move(): return lax.ppermute(value, ZLINE, line_permutation(shift, n_row))]
    ppermute x10 -> x12, starting transfers between devices: 66.6 us -> 68.2 us  [move(): return lax.ppermute(value, ZLINE, line_permutation(shift, n_row))]
    reduce_sum x1 -> x0, other arithmetic: 1.42 us -> none  [shards(): grad = jnp.sum(parts.astype(f32), axis=0).astype(bf16)]
  transfers between devices with their start and end apart: 11 -> 13, of which waited for: 5 -> 4; matrix products, arithmetic and copies ran while one was open for 1% -> 1% of each run, Pallas kernels for 4% -> 4%
where the time goes in v7:
time: 127 us; the launch traced here: 126 us
  starting transfers between devices  75 us (59%)
  blocking collectives  22.6 us (18%)
  waiting for transfers between devices  12.9 us (10%)
  Pallas kernels  12.6 us (10%)
    ppermute x12, starting transfers between devices, move(): return lax.ppermute(value, ZLINE, line_permutation(shift, n_row))  68.2 us
    all_to_all x1, blocking collectives, shards(): lax.all_to_all(part.reshape(n_col, quarter, width), 'col', 0, 0, tiled=True)  22.6 us
    ppermute x12, waiting for transfers between devices, move(): return lax.ppermute(value, ZLINE, line_permutation(shift, n_row))  12.9 us
    pallas_call x3, Pallas kernels, tiles(): pl.pallas_call(functools.partial(tile_kernel, len(pieces), bool(held), la...  7.26 us
    all_to_all x1, starting transfers between devices, shards(): lax.all_to_all(jnp.broadcast_to(own[None], (n_col,) + own.shape), 'col',...  6.74 us
    pallas_call x1, Pallas kernels, projection(): pl.pallas_call(projection_kernel, out_shape=(jax.ShapeDtypeStruct((rows /...  3.15 us
  transfers between devices with their start and end apart: 13, of which 4 were waited for; matrix products, arithmetic and copies ran while one was open for 1% of the time, Pallas kernels for 4%

profile of v7, /device:TPU:1, one launch (start us, length us, event | category | flops | bytes accessed | tf_op | source)
XLA Modules:
  0.0 125.8 jit_solution(9438193455494322209)
XLA Ops:
  0.0 3.2 %shard_map.46 = (bf16[64,1024]{1,0:T(8,128)(2,1)}, f32[64,1024]{1,0:T(8,128)}) custom-call(s32[1]{0:T(128)} %bitcast.core_ref, bf16[128,1536]{1,0:T(8,128)(2,1)} %features_ref.1, bf16[1536,1024]{1,0:T(8,128)(2,1)} %w_ref.3), custom_call_target="tpu_custom_call" | custom-call | flops 402653184 | bytes 3145728 | tf_op jit(solution)/shard_map/pallas_call | solution.py:67
  3.2 8.8 %collective-permute-start = (bf16[64,1024]{1,0:T(8,128)(2,1)}, bf16[64,1024]{1,0:T(8,128)(2,1)S(1)}, u32[]{:S(2)}, u32[]{:S(2)}) collective-permute-start(bf16[64,1024]{1,0:T(8,128)(2,1)} %get-tuple-element.12), channel_id=1, source_target_pairs={{0,128},{128,0},{16,144},{144,16},{32,160},{160,32},{48,176},{176,... | collective-permute-start | bytes 393224 | tf_op jit(solution)/shard_map/ppermute | solution.py:280
  12.0 1.1 collective-permute-done
  13.1 1.0 add_convert_fusion.near_ref
  14.1 10.1 %collective-permute-start.1 = (bf16[64,1024]{1,0:T(8,128)(2,1)S(1)}, bf16[64,1024]{1,0:T(8,128)(2,1)S(1)}, u32[]{:S(2)}, u32[]{:S(2)}) collective-permute-start(bf16[64,1024]{1,0:T(8,128)(2,1)S(1)} %add_convert_fusion.near_ref), channel_id=1, source_target_pairs={{0,256},{128,384},{16,272},{144,400},{32,288},{160,416},{48,304},{... | collective-permute-start | bytes 393224 | tf_op jit(solution)/shard_map/ppermute | solution.py:280
  24.2 0.1 broadcast_select_fusion
  24.3 5.2 %collective-permute-done.1.far_ref = bf16[64,1024]{1,0:T(8,128)(2,1)S(1)} collective-permute-done((bf16[64,1024]{1,0:T(8,128)(2,1)S(1)}, bf16[64,1024]{1,0:T(8,128)(2,1)S(1)}, u32[]{:S(2)}, u32[]{:S(2)}) %collective-permute-start.1) | collective-permute-done | bytes 131104 | tf_op jit(solution)/shard_map/ppermute | solution.py:280
  29.4 0.1 broadcast_in_dim.4.signs_ref
  29.5 0.1 shard_map.47.first_ref
  29.6 7.1 %collective-permute-start.2 = (bf16[64,1152]{1,0:T(8,128)(2,1)S(1)}, bf16[64,1152]{1,0:T(8,128)(2,1)S(1)}, u32[]{:S(2)}, u32[]{:S(2)}) collective-permute-start(bf16[64,1152]{1,0:T(8,128)(2,1)S(1)} %shard_map.47.first_ref), channel_id=1, source_target_pairs={{0,64},{128,448},{16,80},{144,464},{32,96},{160,480},{48,112},{176... | collective-permute-start | bytes 442376 | tf_op jit(solution)/shard_map/ppermute | solution.py:280
  36.8 1.1 broadcast_in_dim.5
  37.9 6.7 %all-to-all-start = ((bf16[16,32,1152]{2,1,0:T(8,128)(2,1)}), bf16[16,32,1152]{2,1,0:T(8,128)(2,1)S(1)}, u32[]{:S(2)}, u32[]{:S(2)}) async-start(bf16[16,32,1152]{2,1,0:T(8,128)(2,1)} %broadcast_in_dim.5), calls=%async_computation | async-start | bytes 2359296 | tf_op jit(solution)/shard_map/all_to_all | solution.py:299
  44.7 0.0 copy-start.1
  44.7 7.0 %collective-permute-start.3 = (bf16[128,1152]{1,0:T(8,128)(2,1)S(1)}, bf16[128,1152]{1,0:T(8,128)(2,1)S(1)}, u32[]{:S(2)}, u32[]{:S(2)}) collective-permute-start(bf16[128,1152]{1,0:T(8,128)(2,1)S(1)} %shard_map.48.refs_2_), channel_id=1, source_target_pairs={{0,128},{128,0},{16,144},{144,16},{32,160},{160,32},{48,176},{176,... | collective-permute-start | bytes 884744 | tf_op jit(solution)/shard_map/ppermute | solution.py:280
  51.7 8.6 %collective-permute-start.5 = (bf16[128,1152]{1,0:T(8,128)(2,1)S(1)}, bf16[128,1152]{1,0:T(8,128)(2,1)S(1)}, u32[]{:S(2)}, u32[]{:S(2)}) collective-permute-start(bf16[128,1152]{1,0:T(8,128)(2,1)S(1)} %shard_map.48.refs_2_), channel_id=1, source_target_pairs={{0,32},{128,480},{16,48},{144,496},{32,64},{160,128},{48,80},{176,... | collective-permute-start | bytes 884744 | tf_op jit(solution)/shard_map/ppermute | solution.py:280
  60.3 1.9 %collective-permute-start.8 = (bf16[128,1152]{1,0:T(8,128)(2,1)S(1)}, bf16[128,1152]{1,0:T(8,128)(2,1)S(1)}, u32[]{:S(2)}, u32[]{:S(2)}) collective-permute-start(bf16[128,1152]{1,0:T(8,128)(2,1)S(1)} %shard_map.48.refs_2_), channel_id=1, source_target_pairs={{0,16},{128,496},{16,32},{144,128},{32,48},{160,144},{48,64},{176,... | collective-permute-start | bytes 884744 | tf_op jit(solution)/shard_map/ppermute | solution.py:280
  62.2 2.2 %collective-permute-start.4 = (bf16[128,1152]{1,0:T(8,128)(2,1)S(1)}, bf16[128,1152]{1,0:T(8,128)(2,1)S(1)}, u32[]{:S(2)}, u32[]{:S(2)}) collective-permute-start(bf16[128,1152]{1,0:T(8,128)(2,1)S(1)} %collective-permute-done.3.refs_3_), channel_id=1, source_target_pairs={{0,16},{128,496},{16,32},{144,128},{32,48},{160,144},{48,64},{176,... | collective-permute-start | bytes 884744 | tf_op jit(solution)/shard_map/ppermute | solution.py:280
  64.4 2.2 %shard_map.49 = (f32[512,128]{1,0:T(8,128)S(1)}, f32[512,1024]{1,0:T(8,128)S(1)}) custom-call(f32[5]{0:T(128)S(1)} %copy-done.1, bf16[512,1152]{1,0:T(8,128)(2,1)S(1)} %bitcast.3, bf16[128,1152]{1,0:T(8,128)(2,1)S(1)} %shard_map.48.refs_2_, bf16[128,1152]{1,0:T(8,128)(2,1)S(1)} %collective-permute-done.3.refs_3_), custom_call_target="tpu_custom_call" | custom-call | flops 536870912 | bytes 2097152 | tf_op jit(solution)/shard_map/pallas_call | solution.py:256
  66.6 0.0 collective-permute-done.5.value_ref
  66.7 3.0 %collective-permute-start.6 = (bf16[128,1152]{1,0:T(8,128)(2,1)S(1)}, bf16[128,1152]{1,0:T(8,128)(2,1)S(1)}, u32[]{:S(2)}, u32[]{:S(2)}) collective-permute-start(bf16[128,1152]{1,0:T(8,128)(2,1)S(1)} %shard_map.50.refs_2_), channel_id=1, source_target_pairs={{0,128},{128,0},{16,144},{144,16},{32,160},{160,32},{48,176},{176,... | collective-permute-start | bytes 884744 | tf_op jit(solution)/shard_map/ppermute | solution.py:280
  69.7 3.0 %collective-permute-start.9 = (bf16[128,1152]{1,0:T(8,128)(2,1)S(1)}, bf16[128,1152]{1,0:T(8,128)(2,1)S(1)}, u32[]{:S(2)}, u32[]{:S(2)}) collective-permute-start(bf16[128,1152]{1,0:T(8,128)(2,1)S(1)} %shard_map.52.refs_4_), channel_id=1, source_target_pairs={{0,128},{128,0},{16,144},{144,16},{32,160},{160,32},{48,176},{176,... | collective-permute-start | bytes 884744 | tf_op jit(solution)/shard_map/ppermute | solution.py:280
  72.8 3.1 %collective-permute-start.7 = (bf16[128,1152]{1,0:T(8,128)(2,1)S(1)}, bf16[128,1152]{1,0:T(8,128)(2,1)S(1)}, u32[]{:S(2)}, u32[]{:S(2)}) collective-permute-start(bf16[128,1152]{1,0:T(8,128)(2,1)S(1)} %shard_map.51.refs_2_), channel_id=1, source_target_pairs={{0,128},{128,0},{16,144},{144,16},{32,160},{160,32},{48,176},{176,... | collective-permute-start | bytes 884744 | tf_op jit(solution)/shard_map/ppermute | solution.py:280
  75.9 2.7 %shard_map.53 = (f32[512,128]{1,0:T(8,128)S(1)}, f32[512,1024]{1,0:T(8,128)S(1)}) custom-call(f32[5]{0:T(128)S(1)} %copy-done.1, bf16[512,1152]{1,0:T(8,128)(2,1)S(1)} %bitcast.4, bf16[128,1152]{1,0:T(8,128)(2,1)S(1)} %shard_map.50.refs_2_, bf16[128,1152]{1,0:T(8,128)(2,1)S(1)} %collective-permute-done.6.first_ref.refs_3_, ...), custom_call_target="tpu_custom_call" | custom-call | flops 1073741824 | bytes 2097152 | tf_op jit(solution)/shard_map/pallas_call | solution.py:256
  78.6 2.4 %shard_map.54 = bf16[512,1024]{1,0:T(8,128)(2,1)S(1)} custom-call(f32[5]{0:T(128)S(1)} %copy-done.1, bf16[512,1152]{1,0:T(8,128)(2,1)S(1)} %bitcast.5, bf16[128,1152]{1,0:T(8,128)(2,1)S(1)} %shard_map.51.refs_2_, bf16[128,1152]{1,0:T(8,128)(2,1)S(1)} %collective-permute-done.7.refs_3_, f32[512,128]{1,0:T(8,128)S(1)} %get-tuple-element.15.refs_4_, ...), custom_call_target="tpu_custom_call" | custom-call | flops 536870912 | bytes 2097152 | tf_op jit(solution)/shard_map/pallas_call | solution.py:256
  81.0 0.0 copy-start
  81.0 22.6 %all_to_all.10.parts_ref = bf16[16,32,1024]{2,1,0:T(8,128)(2,1)S(1)} all-to-all(bf16[16,32,1024]{2,1,0:T(8,128)(2,1)S(1)} %bitcast.6), channel_id=1, replica_groups=mesh['tensor'=4,'row'=8,'col'=16] {'col'}, dimensions={0} | all-to-all | bytes 2097152 | tf_op jit(solution)/shard_map/all_to_all | solution.py:309
  103.5 0.1 shard_map.55
  103.7 8.1 %collective-permute-start.10 = (bf16[32,1024]{1,0:T(8,128)(2,1)S(1)}, bf16[32,1024]{1,0:T(8,128)(2,1)S(1)}, u32[]{:S(2)}, u32[]{:S(2)}) collective-permute-start(bf16[32,1024]{1,0:T(8,128)(2,1)S(1)} %shard_map.55), channel_id=1, source_target_pairs={{0,256},{128,384},{16,272},{144,400},{32,288},{160,416},{48,304},{... | collective-permute-start | bytes 196616 | tf_op jit(solution)/shard_map/ppermute | solution.py:280
  111.8 5.6 %collective-permute-done.10 = bf16[32,1024]{1,0:T(8,128)(2,1)S(1)} collective-permute-done((bf16[32,1024]{1,0:T(8,128)(2,1)S(1)}, bf16[32,1024]{1,0:T(8,128)(2,1)S(1)}, u32[]{:S(2)}, u32[]{:S(2)}) %collective-permute-start.10) | collective-permute-done | bytes 65568 | tf_op jit(solution)/shard_map/ppermute | solution.py:280
  117.4 5.4 %collective-permute-start.11 = (bf16[64,1024]{1,0:T(8,128)(2,1)S(1)}, bf16[64,1024]{1,0:T(8,128)(2,1)S(1)}, u32[]{:S(2)}, u32[]{:S(2)}) collective-permute-start(bf16[64,1024]{1,0:T(8,128)(2,1)S(1)} %maximum_select_fusion.1), channel_id=1, source_target_pairs={{0,128},{128,0},{16,144},{144,16},{32,160},{160,32},{48,176},{176,... | collective-permute-start | bytes 393224 | tf_op jit(solution)/shard_map/ppermute | solution.py:280
  122.8 1.0 collective-permute-done.11
  123.9 1.9 %shard_map.56 = bf16[128,1536]{1,0:T(8,128)(2,1)} custom-call(bf16[128,1024]{1,0:T(8,128)(2,1)S(1)} %maximum_select_fusion.grad_ref, bf16[1536,1024]{1,0:T(8,128)(2,1)S(1)} %copy-done), custom_call_target="tpu_custom_call" | custom-call | flops 402653184 | bytes 3145728 | tf_op jit(solution)/shard_map/pallas_call | solution.py:128
  (20 shorter events, 0.2 us)
Async XLA Ops:
  0.0 12.0 %copy-start.2 = (s32[128]{0:T(128)S(1)}, s32[128]{0:T(128)}, u32[]{:S(2)}) copy-start(s32[128]{0:T(128)} %param.6) | copy-start | bytes 1540
  3.2 10.0 %collective-permute-start = (bf16[64,1024]{1,0:T(8,128)(2,1)}, bf16[64,1024]{1,0:T(8,128)(2,1)S(1)}, u32[]{:S(2)}, u32[]{:S(2)}) collective-permute-start(bf16[64,1024]{1,0:T(8,128)(2,1)} %get-tuple-element.12), channel_id=1, source_target_pairs={{0,128},{128,0},{16,144},{144,16},{32,160},{160,32},{48,176},{176,... | collective-permute-start | bytes 393224 | tf_op jit(solution)/shard_map/ppermute | solution.py:280
  14.1 15.3 %collective-permute-start.1 = (bf16[64,1024]{1,0:T(8,128)(2,1)S(1)}, bf16[64,1024]{1,0:T(8,128)(2,1)S(1)}, u32[]{:S(2)}, u32[]{:S(2)}) collective-permute-start(bf16[64,1024]{1,0:T(8,128)(2,1)S(1)} %add_convert_fusion.near_ref), channel_id=1, source_target_pairs={{0,256},{128,384},{16,272},{144,400},{32,288},{160,416},{48,304},{... | collective-permute-start | bytes 393224 | tf_op jit(solution)/shard_map/ppermute | solution.py:280
  29.6 15.0 %collective-permute-start.2 = (bf16[64,1152]{1,0:T(8,128)(2,1)S(1)}, bf16[64,1152]{1,0:T(8,128)(2,1)S(1)}, u32[]{:S(2)}, u32[]{:S(2)}) collective-permute-start(bf16[64,1152]{1,0:T(8,128)(2,1)S(1)} %shard_map.47.first_ref), channel_id=1, source_target_pairs={{0,64},{128,448},{16,80},{144,464},{32,96},{160,480},{48,112},{176... | collective-permute-start | bytes 442376 | tf_op jit(solution)/shard_map/ppermute | solution.py:280
  37.9 26.5 %all-to-all-start = ((bf16[16,32,1152]{2,1,0:T(8,128)(2,1)}), bf16[16,32,1152]{2,1,0:T(8,128)(2,1)S(1)}, u32[]{:S(2)}, u32[]{:S(2)}) async-start(bf16[16,32,1152]{2,1,0:T(8,128)(2,1)} %broadcast_in_dim.5), calls=%async_computation | async-start | bytes 2359296 | tf_op jit(solution)/shard_map/all_to_all | solution.py:299
  44.7 19.8 %copy-start.1 = (f32[5]{0:T(128)S(1)}, f32[5]{0:T(128)}, u32[]{:S(2)}) copy-start(f32[5]{0:T(128)} %refs_0_.5) | copy-start | bytes 64
  44.7 17.5 %collective-permute-start.3 = (bf16[128,1152]{1,0:T(8,128)(2,1)S(1)}, bf16[128,1152]{1,0:T(8,128)(2,1)S(1)}, u32[]{:S(2)}, u32[]{:S(2)}) collective-permute-start(bf16[128,1152]{1,0:T(8,128)(2,1)S(1)} %shard_map.48.refs_2_), channel_id=1, source_target_pairs={{0,128},{128,0},{16,144},{144,16},{32,160},{160,32},{48,176},{176,... | collective-permute-start | bytes 884744 | tf_op jit(solution)/shard_map/ppermute | solution.py:280
  51.7 15.0 %collective-permute-start.5 = (bf16[128,1152]{1,0:T(8,128)(2,1)S(1)}, bf16[128,1152]{1,0:T(8,128)(2,1)S(1)}, u32[]{:S(2)}, u32[]{:S(2)}) collective-permute-start(bf16[128,1152]{1,0:T(8,128)(2,1)S(1)} %shard_map.48.refs_2_), channel_id=1, source_target_pairs={{0,32},{128,480},{16,48},{144,496},{32,64},{160,128},{48,80},{176,... | collective-permute-start | bytes 884744 | tf_op jit(solution)/shard_map/ppermute | solution.py:280
  60.3 9.4 %collective-permute-start.8 = (bf16[128,1152]{1,0:T(8,128)(2,1)S(1)}, bf16[128,1152]{1,0:T(8,128)(2,1)S(1)}, u32[]{:S(2)}, u32[]{:S(2)}) collective-permute-start(bf16[128,1152]{1,0:T(8,128)(2,1)S(1)} %shard_map.48.refs_2_), channel_id=1, source_target_pairs={{0,16},{128,496},{16,32},{144,128},{32,48},{160,144},{48,64},{176,... | collective-permute-start | bytes 884744 | tf_op jit(solution)/shard_map/ppermute | solution.py:280
  62.2 10.5 %collective-permute-start.4 = (bf16[128,1152]{1,0:T(8,128)(2,1)S(1)}, bf16[128,1152]{1,0:T(8,128)(2,1)S(1)}, u32[]{:S(2)}, u32[]{:S(2)}) collective-permute-start(bf16[128,1152]{1,0:T(8,128)(2,1)S(1)} %collective-permute-done.3.refs_3_), channel_id=1, source_target_pairs={{0,16},{128,496},{16,32},{144,128},{32,48},{160,144},{48,64},{176,... | collective-permute-start | bytes 884744 | tf_op jit(solution)/shard_map/ppermute | solution.py:280
  66.7 6.1 %collective-permute-start.6 = (bf16[128,1152]{1,0:T(8,128)(2,1)S(1)}, bf16[128,1152]{1,0:T(8,128)(2,1)S(1)}, u32[]{:S(2)}, u32[]{:S(2)}) collective-permute-start(bf16[128,1152]{1,0:T(8,128)(2,1)S(1)} %shard_map.50.refs_2_), channel_id=1, source_target_pairs={{0,128},{128,0},{16,144},{144,16},{32,160},{160,32},{48,176},{176,... | collective-permute-start | bytes 884744 | tf_op jit(solution)/shard_map/ppermute | solution.py:280
  69.7 6.2 %collective-permute-start.9 = (bf16[128,1152]{1,0:T(8,128)(2,1)S(1)}, bf16[128,1152]{1,0:T(8,128)(2,1)S(1)}, u32[]{:S(2)}, u32[]{:S(2)}) collective-permute-start(bf16[128,1152]{1,0:T(8,128)(2,1)S(1)} %shard_map.52.refs_4_), channel_id=1, source_target_pairs={{0,128},{128,0},{16,144},{144,16},{32,160},{160,32},{48,176},{176,... | collective-permute-start | bytes 884744 | tf_op jit(solution)/shard_map/ppermute | solution.py:280
  72.8 5.9 %collective-permute-start.7 = (bf16[128,1152]{1,0:T(8,128)(2,1)S(1)}, bf16[128,1152]{1,0:T(8,128)(2,1)S(1)}, u32[]{:S(2)}, u32[]{:S(2)}) collective-permute-start(bf16[128,1152]{1,0:T(8,128)(2,1)S(1)} %shard_map.51.refs_2_), channel_id=1, source_target_pairs={{0,128},{128,0},{16,144},{144,16},{32,160},{160,32},{48,176},{176,... | collective-permute-start | bytes 884744 | tf_op jit(solution)/shard_map/ppermute | solution.py:280
  81.0 42.9 %copy-start = (bf16[1536,1024]{1,0:T(8,128)(2,1)S(1)}, bf16[1536,1024]{1,0:T(8,128)(2,1)}, u32[]{:S(2)}) copy-start(bf16[1536,1024]{1,0:T(8,128)(2,1)} %w_ref.3) | copy-start | bytes 9437188
  103.7 13.7 %collective-permute-start.10 = (bf16[32,1024]{1,0:T(8,128)(2,1)S(1)}, bf16[32,1024]{1,0:T(8,128)(2,1)S(1)}, u32[]{:S(2)}, u32[]{:S(2)}) collective-permute-start(bf16[32,1024]{1,0:T(8,128)(2,1)S(1)} %shard_map.55), channel_id=1, source_target_pairs={{0,256},{128,384},{16,272},{144,400},{32,288},{160,416},{48,304},{... | collective-permute-start | bytes 196616 | tf_op jit(solution)/shard_map/ppermute | solution.py:280
  117.4 6.3 %collective-permute-start.11 = (bf16[64,1024]{1,0:T(8,128)(2,1)S(1)}, bf16[64,1024]{1,0:T(8,128)(2,1)S(1)}, u32[]{:S(2)}, u32[]{:S(2)}) collective-permute-start(bf16[64,1024]{1,0:T(8,128)(2,1)S(1)} %maximum_select_fusion.1), channel_id=1, source_target_pairs={{0,128},{128,0},{16,144},{144,16},{32,160},{160,32},{48,176},{176,... | collective-permute-start | bytes 393224 | tf_op jit(solution)/shard_map/ppermute | solution.py:280

commit v8 on v7

--- a/solution.py
+++ b/solution.py
@@ -54,11 +54,14 @@
         term = jnp.dot(rows[:, place], weights[place], preferred_element_type=jnp.float32)
         value = term if value is None else value + term
     total[...] = value
-    half = kept_ref.shape[0]
+    quarter = kept_ref.shape[0] // 2
     core = core_ref[0]
-    away = total[pl.ds(pl.multiple_of((1 - core) * half, half), half)]
-    away_ref[...] = away.astype(away_ref.dtype)
-    kept_ref[...] = total[pl.ds(pl.multiple_of(core * half, half), half)]
+    for index in range(2):
+        place = slice(index * quarter, (index + 1) * quarter)
+        start = pl.multiple_of((2 * index + 1 - core) * quarter, quarter)
+        away_ref[place] = total[pl.ds(start, quarter)].astype(away_ref.dtype)
+        start = pl.multiple_of((2 * index + core) * quarter, quarter)
+        kept_ref[place] = total[pl.ds(start, quarter)]
 
 
 def projection(core, features, w_proj):
@@ -285,8 +288,8 @@
     away, kept = projection(jnp.reshape(tpos % 2, (1,)), features, w_proj)
     partial = (kept + other_core(away).astype(f32)).astype(bf16)
     far = move(partial, lambda chip, core: (chip + n_row, core))
-    signs = (1 - 2 * flags).astype(f32)
-    s_half = pick(core, signs[:half], signs[half:])
+    signs = (1 - 2 * flags).astype(f32).reshape(2, 2, quarter)
+    s_half = pick(core, signs[:, 0], signs[:, 1]).reshape(half)
     block = whole_block(partial, far, jnp.broadcast_to(s_half[:, None], (half, PAD)))
 
     far_block = move(block, lambda chip, core: (chip + (n_row // 2) * (1 - 2 * core), core))
@@ -308,16 +311,7 @@
     part = tiles([next_other, other_core(next_other)], col, rates, sums, True)
     parts = lax.all_to_all(part.reshape(n_col, quarter, width), "col", 0, 0, tiled=True)
     grad = summed(parts)
-    grad_far = move(grad, lambda chip, core: (chip + n_row, core))
-    grad = pick(
-        high, jnp.concatenate([grad, grad_far], axis=0), jnp.concatenate([grad_far, grad], axis=0)
-    )
-    grad_other = other_core(grad)
-    grad = pick(
-        core,
-        jnp.concatenate([grad, grad_other], axis=0),
-        jnp.concatenate([grad_other, grad], axis=0),
-    )
+    grad = lax.all_gather(grad, "tensor", axis=0, tiled=True)
     return result(grad, w_proj)
 
 

time: 127 us -> 123 us (0.969)
  blocking collectives: 22.6 us -> 39.2 us
  starting transfers between devices: 75 us -> 61.5 us
  waiting for transfers between devices: 12.9 us -> 6.21 us
    all_gather x0 -> x1, blocking collectives: none -> 16.6 us  [shards(): grad = lax.all_gather(grad, 'tensor', axis=0, tiled=True)]
    ppermute x12 -> x10, starting transfers between devices: 68.2 us -> 54.8 us  [move(): return lax.ppermute(value, ZLINE, line_permutation(shift, n_row))]
    ppermute x12 -> x10, waiting for transfers between devices: 12.9 us -> 6.2 us  [move(): return lax.ppermute(value, ZLINE, line_permutation(shift, n_row))]
  transfers between devices with their start and end apart: 13 -> 11, of which waited for: 4 -> 2; matrix products, arithmetic and copies ran while one was open for 1% -> 1% of each run, Pallas kernels for 4% -> 4%
where the time goes in v8:
time: 123 us; the launch traced here: 122 us
  starting transfers between devices  61.5 us (50%)
  blocking collectives  39.2 us (32%)
  Pallas kernels  12.6 us (10%)
  waiting for transfers between devices  6.21 us (5%)
  local copies, waits for them, and re-layouts  1.37 us (1%)
    ppermute x10, starting transfers between devices, move(): return lax.ppermute(value, ZLINE, line_permutation(shift, n_row))  54.8 us
    all_to_all x1, blocking collectives, shards(): lax.all_to_all(part.reshape(n_col, quarter, width), 'col', 0, 0, tiled=True)  22.6 us
    all_gather x1, blocking collectives, shards(): grad = lax.all_gather(grad, 'tensor', axis=0, tiled=True)  16.6 us
    pallas_call x3, Pallas kernels, tiles(): pl.pallas_call(functools.partial(tile_kernel, len(pieces), bool(held), la...  7.27 us
    all_to_all x1, starting transfers between devices, shards(): lax.all_to_all(jnp.broadcast_to(own[None], (n_col,) + own.shape), 'col',...  6.74 us
    ppermute x10, waiting for transfers between devices, move(): return lax.ppermute(value, ZLINE, line_permutation(shift, n_row))  6.2 us
    pallas_call x1, Pallas kernels, projection(): pl.pallas_call(projection_kernel, out_shape=(jax.ShapeDtypeStruct((rows /...  3.15 us
  transfers between devices with their start and end apart: 11, of which 2 were waited for; matrix products, arithmetic and copies ran while one was open for 1% of the time, Pallas kernels for 4%

profile of v8, /device:TPU:1, one launch (start us, length us, event | category | flops | bytes accessed | tf_op | source)
XLA Modules:
  0.0 122.3 jit_solution(8520276355428991880)
XLA Ops:
  0.0 3.2 %shard_map.46 = (bf16[64,1024]{1,0:T(8,128)(2,1)}, f32[64,1024]{1,0:T(8,128)}) custom-call(s32[1]{0:T(128)} %bitcast.core_ref, bf16[128,1536]{1,0:T(8,128)(2,1)} %features_ref.1, bf16[1536,1024]{1,0:T(8,128)(2,1)} %w_ref.3), custom_call_target="tpu_custom_call" | custom-call | flops 402653184 | bytes 3145728 | tf_op jit(solution)/shard_map/pallas_call | solution.py:70
  3.2 8.8 %collective-permute-start = (bf16[64,1024]{1,0:T(8,128)(2,1)}, bf16[64,1024]{1,0:T(8,128)(2,1)S(1)}, u32[]{:S(2)}, u32[]{:S(2)}) collective-permute-start(bf16[64,1024]{1,0:T(8,128)(2,1)} %get-tuple-element.12), channel_id=1, source_target_pairs={{0,128},{128,0},{16,144},{144,16},{32,160},{160,32},{48,176},{176,... | collective-permute-start | bytes 393224 | tf_op jit(solution)/shard_map/ppermute | solution.py:283
  11.9 1.2 collective-permute-done
  13.1 1.0 add_convert_fusion.near_ref
  14.1 10.1 %collective-permute-start.1 = (bf16[64,1024]{1,0:T(8,128)(2,1)S(1)}, bf16[64,1024]{1,0:T(8,128)(2,1)S(1)}, u32[]{:S(2)}, u32[]{:S(2)}) collective-permute-start(bf16[64,1024]{1,0:T(8,128)(2,1)S(1)} %add_convert_fusion.near_ref), channel_id=1, source_target_pairs={{0,256},{128,384},{16,272},{144,400},{32,288},{160,416},{48,304},{... | collective-permute-start | bytes 393224 | tf_op jit(solution)/shard_map/ppermute | solution.py:283
  24.2 0.1 reshape.25
  24.3 0.1 select_n.41
  24.4 5.0 %collective-permute-done.1.far_ref = bf16[64,1024]{1,0:T(8,128)(2,1)S(1)} collective-permute-done((bf16[64,1024]{1,0:T(8,128)(2,1)S(1)}, bf16[64,1024]{1,0:T(8,128)(2,1)S(1)}, u32[]{:S(2)}, u32[]{:S(2)}) %collective-permute-start.1) | collective-permute-done | bytes 131104 | tf_op jit(solution)/shard_map/ppermute | solution.py:283
  29.4 0.1 broadcast_in_dim.4.signs_ref
  29.5 0.1 shard_map.47.first_ref
  29.6 7.1 %collective-permute-start.2 = (bf16[64,1152]{1,0:T(8,128)(2,1)S(1)}, bf16[64,1152]{1,0:T(8,128)(2,1)S(1)}, u32[]{:S(2)}, u32[]{:S(2)}) collective-permute-start(bf16[64,1152]{1,0:T(8,128)(2,1)S(1)} %shard_map.47.first_ref), channel_id=1, source_target_pairs={{0,64},{128,448},{16,80},{144,464},{32,96},{160,480},{48,112},{176... | collective-permute-start | bytes 442376 | tf_op jit(solution)/shard_map/ppermute | solution.py:283
  36.8 1.1 broadcast_in_dim.5
  37.9 6.7 %all-to-all-start = ((bf16[16,32,1152]{2,1,0:T(8,128)(2,1)}), bf16[16,32,1152]{2,1,0:T(8,128)(2,1)S(1)}, u32[]{:S(2)}, u32[]{:S(2)}) async-start(bf16[16,32,1152]{2,1,0:T(8,128)(2,1)} %broadcast_in_dim.5), calls=%async_computation | async-start | bytes 2359296 | tf_op jit(solution)/shard_map/all_to_all | solution.py:302
  44.6 0.0 copy-start.1
  44.7 0.0 collective-permute-done.2.second_ref
  44.7 7.0 %collective-permute-start.3 = (bf16[128,1152]{1,0:T(8,128)(2,1)S(1)}, bf16[128,1152]{1,0:T(8,128)(2,1)S(1)}, u32[]{:S(2)}, u32[]{:S(2)}) collective-permute-start(bf16[128,1152]{1,0:T(8,128)(2,1)S(1)} %shard_map.48.refs_2_), channel_id=1, source_target_pairs={{0,128},{128,0},{16,144},{144,16},{32,160},{160,32},{48,176},{176,... | collective-permute-start | bytes 884744 | tf_op jit(solution)/shard_map/ppermute | solution.py:283
  51.7 8.6 %collective-permute-start.5 = (bf16[128,1152]{1,0:T(8,128)(2,1)S(1)}, bf16[128,1152]{1,0:T(8,128)(2,1)S(1)}, u32[]{:S(2)}, u32[]{:S(2)}) collective-permute-start(bf16[128,1152]{1,0:T(8,128)(2,1)S(1)} %shard_map.48.refs_2_), channel_id=1, source_target_pairs={{0,32},{128,480},{16,48},{144,496},{32,64},{160,128},{48,80},{176,... | collective-permute-start | bytes 884744 | tf_op jit(solution)/shard_map/ppermute | solution.py:283
  60.3 1.9 %collective-permute-start.8 = (bf16[128,1152]{1,0:T(8,128)(2,1)S(1)}, bf16[128,1152]{1,0:T(8,128)(2,1)S(1)}, u32[]{:S(2)}, u32[]{:S(2)}) collective-permute-start(bf16[128,1152]{1,0:T(8,128)(2,1)S(1)} %shard_map.48.refs_2_), channel_id=1, source_target_pairs={{0,16},{128,496},{16,32},{144,128},{32,48},{160,144},{48,64},{176,... | collective-permute-start | bytes 884744 | tf_op jit(solution)/shard_map/ppermute | solution.py:283
  62.2 0.0 collective-permute-done.3.refs_3_
  62.2 2.2 %collective-permute-start.4 = (bf16[128,1152]{1,0:T(8,128)(2,1)S(1)}, bf16[128,1152]{1,0:T(8,128)(2,1)S(1)}, u32[]{:S(2)}, u32[]{:S(2)}) collective-permute-start(bf16[128,1152]{1,0:T(8,128)(2,1)S(1)} %collective-permute-done.3.refs_3_), channel_id=1, source_target_pairs={{0,16},{128,496},{16,32},{144,128},{32,48},{160,144},{48,64},{176,... | collective-permute-start | bytes 884744 | tf_op jit(solution)/shard_map/ppermute | solution.py:283
  64.4 2.2 %shard_map.49 = (f32[512,128]{1,0:T(8,128)S(1)}, f32[512,1024]{1,0:T(8,128)S(1)}) custom-call(f32[5]{0:T(128)S(1)} %copy-done.1, bf16[512,1152]{1,0:T(8,128)(2,1)S(1)} %bitcast.3, bf16[128,1152]{1,0:T(8,128)(2,1)S(1)} %shard_map.48.refs_2_, bf16[128,1152]{1,0:T(8,128)(2,1)S(1)} %collective-permute-done.3.refs_3_), custom_call_target="tpu_custom_call" | custom-call | flops 536870912 | bytes 2097152 | tf_op jit(solution)/shard_map/pallas_call | solution.py:259
  66.7 3.0 %collective-permute-start.6 = (bf16[128,1152]{1,0:T(8,128)(2,1)S(1)}, bf16[128,1152]{1,0:T(8,128)(2,1)S(1)}, u32[]{:S(2)}, u32[]{:S(2)}) collective-permute-start(bf16[128,1152]{1,0:T(8,128)(2,1)S(1)} %shard_map.50.refs_2_), channel_id=1, source_target_pairs={{0,128},{128,0},{16,144},{144,16},{32,160},{160,32},{48,176},{176,... | collective-permute-start | bytes 884744 | tf_op jit(solution)/shard_map/ppermute | solution.py:283
  69.7 3.0 %collective-permute-start.9 = (bf16[128,1152]{1,0:T(8,128)(2,1)S(1)}, bf16[128,1152]{1,0:T(8,128)(2,1)S(1)}, u32[]{:S(2)}, u32[]{:S(2)}) collective-permute-start(bf16[128,1152]{1,0:T(8,128)(2,1)S(1)} %shard_map.52.refs_4_), channel_id=1, source_target_pairs={{0,128},{128,0},{16,144},{144,16},{32,160},{160,32},{48,176},{176,... | collective-permute-start | bytes 884744 | tf_op jit(solution)/shard_map/ppermute | solution.py:283
  72.7 0.0 collective-permute-done.4.value_ref
  72.8 3.1 %collective-permute-start.7 = (bf16[128,1152]{1,0:T(8,128)(2,1)S(1)}, bf16[128,1152]{1,0:T(8,128)(2,1)S(1)}, u32[]{:S(2)}, u32[]{:S(2)}) collective-permute-start(bf16[128,1152]{1,0:T(8,128)(2,1)S(1)} %shard_map.51.refs_2_), channel_id=1, source_target_pairs={{0,128},{128,0},{16,144},{144,16},{32,160},{160,32},{48,176},{176,... | collective-permute-start | bytes 884744 | tf_op jit(solution)/shard_map/ppermute | solution.py:283
  75.9 2.7 %shard_map.53 = (f32[512,128]{1,0:T(8,128)S(1)}, f32[512,1024]{1,0:T(8,128)S(1)}) custom-call(f32[5]{0:T(128)S(1)} %copy-done.1, bf16[512,1152]{1,0:T(8,128)(2,1)S(1)} %bitcast.4, bf16[128,1152]{1,0:T(8,128)(2,1)S(1)} %shard_map.50.refs_2_, bf16[128,1152]{1,0:T(8,128)(2,1)S(1)} %collective-permute-done.6.first_ref.refs_3_, ...), custom_call_target="tpu_custom_call" | custom-call | flops 1073741824 | bytes 2097152 | tf_op jit(solution)/shard_map/pallas_call | solution.py:259
  78.6 2.4 %shard_map.54 = bf16[512,1024]{1,0:T(8,128)(2,1)S(1)} custom-call(f32[5]{0:T(128)S(1)} %copy-done.1, bf16[512,1152]{1,0:T(8,128)(2,1)S(1)} %bitcast.5, bf16[128,1152]{1,0:T(8,128)(2,1)S(1)} %shard_map.51.refs_2_, bf16[128,1152]{1,0:T(8,128)(2,1)S(1)} %collective-permute-done.7.refs_3_, f32[512,128]{1,0:T(8,128)S(1)} %get-tuple-element.15.refs_4_, ...), custom_call_target="tpu_custom_call" | custom-call | flops 536870912 | bytes 2097152 | tf_op jit(solution)/shard_map/pallas_call | solution.py:259
  81.0 0.0 copy-start
  81.0 22.6 %all_to_all.10.parts_ref = bf16[16,32,1024]{2,1,0:T(8,128)(2,1)S(1)} all-to-all(bf16[16,32,1024]{2,1,0:T(8,128)(2,1)S(1)} %bitcast.6), channel_id=1, replica_groups=mesh['tensor'=4,'row'=8,'col'=16] {'col'}, dimensions={0} | all-to-all | bytes 2097152 | tf_op jit(solution)/shard_map/all_to_all | solution.py:312
  103.6 0.1 shard_map.55
  103.7 16.6 %all_gather.3.grad_ref = bf16[128,1024]{1,0:T(8,128)(2,1)S(1)} all-gather(bf16[32,1024]{1,0:T(8,128)(2,1)S(1)} %shard_map.55), channel_id=1, replica_groups=mesh['tensor'=4,'row'=8,'col'=16] {'tensor'}, dimensions={0}, use_global_device_ids=true | all-gather | bytes 327680 | tf_op jit(solution)/shard_map/all_gather | solution.py:314
  120.4 1.9 %shard_map.56 = bf16[128,1536]{1,0:T(8,128)(2,1)} custom-call(bf16[128,1024]{1,0:T(8,128)(2,1)S(1)} %all_gather.3.grad_ref, bf16[1536,1024]{1,0:T(8,128)(2,1)S(1)} %copy-done), custom_call_target="tpu_custom_call" | custom-call | flops 402653184 | bytes 3145728 | tf_op jit(solution)/shard_map/pallas_call | solution.py:131
  (17 shorter events, 0.1 us)
Async XLA Ops:
  0.0 24.2 %copy-start.2 = (s32[128]{0:T(128)S(1)}, s32[128]{0:T(128)}, u32[]{:S(2)}) copy-start(s32[128]{0:T(128)} %param.6) | copy-start | bytes 1540
  3.2 10.0 %collective-permute-start = (bf16[64,1024]{1,0:T(8,128)(2,1)}, bf16[64,1024]{1,0:T(8,128)(2,1)S(1)}, u32[]{:S(2)}, u32[]{:S(2)}) collective-permute-start(bf16[64,1024]{1,0:T(8,128)(2,1)} %get-tuple-element.12), channel_id=1, source_target_pairs={{0,128},{128,0},{16,144},{144,16},{32,160},{160,32},{48,176},{176,... | collective-permute-start | bytes 393224 | tf_op jit(solution)/shard_map/ppermute | solution.py:283
  14.1 15.3 %collective-permute-start.1 = (bf16[64,1024]{1,0:T(8,128)(2,1)S(1)}, bf16[64,1024]{1,0:T(8,128)(2,1)S(1)}, u32[]{:S(2)}, u32[]{:S(2)}) collective-permute-start(bf16[64,1024]{1,0:T(8,128)(2,1)S(1)} %add_convert_fusion.near_ref), channel_id=1, source_target_pairs={{0,256},{128,384},{16,272},{144,400},{32,288},{160,416},{48,304},{... | collective-permute-start | bytes 393224 | tf_op jit(solution)/shard_map/ppermute | solution.py:283
  29.6 15.0 %collective-permute-start.2 = (bf16[64,1152]{1,0:T(8,128)(2,1)S(1)}, bf16[64,1152]{1,0:T(8,128)(2,1)S(1)}, u32[]{:S(2)}, u32[]{:S(2)}) collective-permute-start(bf16[64,1152]{1,0:T(8,128)(2,1)S(1)} %shard_map.47.first_ref), channel_id=1, source_target_pairs={{0,64},{128,448},{16,80},{144,464},{32,96},{160,480},{48,112},{176... | collective-permute-start | bytes 442376 | tf_op jit(solution)/shard_map/ppermute | solution.py:283
  37.9 26.5 %all-to-all-start = ((bf16[16,32,1152]{2,1,0:T(8,128)(2,1)}), bf16[16,32,1152]{2,1,0:T(8,128)(2,1)S(1)}, u32[]{:S(2)}, u32[]{:S(2)}) async-start(bf16[16,32,1152]{2,1,0:T(8,128)(2,1)} %broadcast_in_dim.5), calls=%async_computation | async-start | bytes 2359296 | tf_op jit(solution)/shard_map/all_to_all | solution.py:302
  44.6 19.8 %copy-start.1 = (f32[5]{0:T(128)S(1)}, f32[5]{0:T(128)}, u32[]{:S(2)}) copy-start(f32[5]{0:T(128)} %refs_0_.5) | copy-start | bytes 64
  44.7 17.5 %collective-permute-start.3 = (bf16[128,1152]{1,0:T(8,128)(2,1)S(1)}, bf16[128,1152]{1,0:T(8,128)(2,1)S(1)}, u32[]{:S(2)}, u32[]{:S(2)}) collective-permute-start(bf16[128,1152]{1,0:T(8,128)(2,1)S(1)} %shard_map.48.refs_2_), channel_id=1, source_target_pairs={{0,128},{128,0},{16,144},{144,16},{32,160},{160,32},{48,176},{176,... | collective-permute-start | bytes 884744 | tf_op jit(solution)/shard_map/ppermute | solution.py:283
  51.7 15.0 %collective-permute-start.5 = (bf16[128,1152]{1,0:T(8,128)(2,1)S(1)}, bf16[128,1152]{1,0:T(8,128)(2,1)S(1)}, u32[]{:S(2)}, u32[]{:S(2)}) collective-permute-start(bf16[128,1152]{1,0:T(8,128)(2,1)S(1)} %shard_map.48.refs_2_), channel_id=1, source_target_pairs={{0,32},{128,480},{16,48},{144,496},{32,64},{160,128},{48,80},{176,... | collective-permute-start | bytes 884744 | tf_op jit(solution)/shard_map/ppermute | solution.py:283
  60.3 9.4 %collective-permute-start.8 = (bf16[128,1152]{1,0:T(8,128)(2,1)S(1)}, bf16[128,1152]{1,0:T(8,128)(2,1)S(1)}, u32[]{:S(2)}, u32[]{:S(2)}) collective-permute-start(bf16[128,1152]{1,0:T(8,128)(2,1)S(1)} %shard_map.48.refs_2_), channel_id=1, source_target_pairs={{0,16},{128,496},{16,32},{144,128},{32,48},{160,144},{48,64},{176,... | collective-permute-start | bytes 884744 | tf_op jit(solution)/shard_map/ppermute | solution.py:283
  62.2 10.5 %collective-permute-start.4 = (bf16[128,1152]{1,0:T(8,128)(2,1)S(1)}, bf16[128,1152]{1,0:T(8,128)(2,1)S(1)}, u32[]{:S(2)}, u32[]{:S(2)}) collective-permute-start(bf16[128,1152]{1,0:T(8,128)(2,1)S(1)} %collective-permute-done.3.refs_3_), channel_id=1, source_target_pairs={{0,16},{128,496},{16,32},{144,128},{32,48},{160,144},{48,64},{176,... | collective-permute-start | bytes 884744 | tf_op jit(solution)/shard_map/ppermute | solution.py:283
  66.7 6.1 %collective-permute-start.6 = (bf16[128,1152]{1,0:T(8,128)(2,1)S(1)}, bf16[128,1152]{1,0:T(8,128)(2,1)S(1)}, u32[]{:S(2)}, u32[]{:S(2)}) collective-permute-start(bf16[128,1152]{1,0:T(8,128)(2,1)S(1)} %shard_map.50.refs_2_), channel_id=1, source_target_pairs={{0,128},{128,0},{16,144},{144,16},{32,160},{160,32},{48,176},{176,... | collective-permute-start | bytes 884744 | tf_op jit(solution)/shard_map/ppermute | solution.py:283
  69.7 6.2 %collective-permute-start.9 = (bf16[128,1152]{1,0:T(8,128)(2,1)S(1)}, bf16[128,1152]{1,0:T(8,128)(2,1)S(1)}, u32[]{:S(2)}, u32[]{:S(2)}) collective-permute-start(bf16[128,1152]{1,0:T(8,128)(2,1)S(1)} %shard_map.52.refs_4_), channel_id=1, source_target_pairs={{0,128},{128,0},{16,144},{144,16},{32,160},{160,32},{48,176},{176,... | collective-permute-start | bytes 884744 | tf_op jit(solution)/shard_map/ppermute | solution.py:283
  72.8 5.9 %collective-permute-start.7 = (bf16[128,1152]{1,0:T(8,128)(2,1)S(1)}, bf16[128,1152]{1,0:T(8,128)(2,1)S(1)}, u32[]{:S(2)}, u32[]{:S(2)}) collective-permute-start(bf16[128,1152]{1,0:T(8,128)(2,1)S(1)} %shard_map.51.refs_2_), channel_id=1, source_target_pairs={{0,128},{128,0},{16,144},{144,16},{32,160},{160,32},{48,176},{176,... | collective-permute-start | bytes 884744 | tf_op jit(solution)/shard_map/ppermute | solution.py:283
  81.0 39.4 %copy-start = (bf16[1536,1024]{1,0:T(8,128)(2,1)S(1)}, bf16[1536,1024]{1,0:T(8,128)(2,1)}, u32[]{:S(2)}) copy-start(bf16[1536,1024]{1,0:T(8,128)(2,1)} %w_ref.3) | copy-start | bytes 9437188

commit v9 on v8

--- a/solution.py
+++ b/solution.py
@@ -11,7 +11,6 @@
 ZLINE = ("tensor", "row")
 PAD = 128
 LOG2E = math.log2(math.e)
-FLOPS = 4 * 10**10
 
 
 def line_permutation(shift, n_row):
@@ -90,33 +89,39 @@
     )(core, features, w_proj)
 
 
-def block_kernel(near_ref, far_ref, signs_ref, block_ref):
+def pair_kernel(gathered_ref, pair_ref):
     f32, bf16 = jnp.float32, jnp.bfloat16
-    half, width = near_ref.shape
-    rows = (near_ref[...].astype(f32) + far_ref[...].astype(f32)).astype(bf16)
-    block_ref[:, :width] = rows
-    norm = jnp.sum(jnp.square(rows.astype(f32)), axis=1, keepdims=True)
-    first = norm.astype(bf16).astype(f32)
-    second = (norm - first).astype(bf16).astype(f32)
-    third = norm - first - second
-    lane = lax.broadcasted_iota(jnp.int32, (half, PAD), 1)
-    tail = jnp.where(lane == 1, first, jnp.where(lane == 2, second, third))
-    block_ref[:, width:] = jnp.where(lane == 0, signs_ref[...], tail).astype(bf16)
-
-
-def whole_block(near, far, signs):
+    half = pair_ref.shape[0] // 2
+    width = pair_ref.shape[1] - PAD
+    for index in range(2):
+        near = slice(index * half, (index + 1) * half)
+        far = slice((index + 2) * half, (index + 3) * half)
+        rows = gathered_ref[near, :width].astype(f32) + gathered_ref[far, :width].astype(f32)
+        rows = rows.astype(bf16)
+        pair_ref[near, :width] = rows
+        norm = jnp.sum(jnp.square(rows.astype(f32)), axis=1, keepdims=True)
+        first = norm.astype(bf16).astype(f32)
+        second = (norm - first).astype(bf16).astype(f32)
+        third = norm - first - second
+        lane = lax.broadcasted_iota(jnp.int32, (half, PAD), 1)
+        tail = jnp.where(lane == 1, first, jnp.where(lane == 2, second, third))
+        sign = gathered_ref[near, width:].astype(f32)
+        pair_ref[near, width:] = jnp.where(lane == 0, sign, tail).astype(bf16)
+
+
+def whole_pair(gathered):
     vmem = pl.BlockSpec(memory_space=pltpu.VMEM)
-    half, width = near.shape
-    return pl.pallas_call(
-        block_kernel,
-        out_shape=jax.ShapeDtypeStruct((half, width + PAD), near.dtype),
-        in_specs=[vmem] * 3,
+    rows, columns = gathered.shape
+    return pl.pallas_call(
+        pair_kernel,
+        out_shape=jax.ShapeDtypeStruct((rows // 2, columns), gathered.dtype),
+        in_specs=[vmem],
         out_specs=vmem,
         compiler_params=pltpu.CompilerParams(vmem_limit_bytes=16 * 2**20),
         cost_estimate=pl.CostEstimate(
-            flops=4 * half * width, bytes_accessed=6 * half * width, transcendentals=0
-        ),
-    )(near, far, signs)
+            flops=4 * rows * columns, bytes_accessed=3 * rows * columns, transcendentals=0
+        ),
+    )(gathered)
 
 
 def result_kernel(grad_ref, w_ref, out_ref):
@@ -159,24 +164,6 @@
             flops=parts.size, bytes_accessed=2 * parts.size, transcendentals=0
         ),
     )(parts)
-
-
-def pair_kernel(first_ref, second_ref, out_ref):
-    half = first_ref.shape[0]
-    out_ref[:half] = first_ref[...]
-    out_ref[half:] = second_ref[...]
-
-
-def side_by_side(first, second, flops):
-    vmem = pl.BlockSpec(memory_space=pltpu.VMEM)
-    return pl.pallas_call(
-        pair_kernel,
-        out_shape=jax.ShapeDtypeStruct((2 * first.shape[0], first.shape[1]), first.dtype),
-        in_specs=[vmem, vmem],
-        out_specs=vmem,
-        compiler_params=pltpu.CompilerParams(vmem_limit_bytes=16 * 2**20),
-        cost_estimate=pl.CostEstimate(flops=flops, bytes_accessed=0, transcendentals=0),
-    )(first, second)
 
 
 def after_kernel(value_ref, first_ref, same_ref):
@@ -287,18 +274,24 @@
 
     away, kept = projection(jnp.reshape(tpos % 2, (1,)), features, w_proj)
     partial = (kept + other_core(away).astype(f32)).astype(bf16)
-    far = move(partial, lambda chip, core: (chip + n_row, core))
-    signs = (1 - 2 * flags).astype(f32).reshape(2, 2, quarter)
+    signs = (1 - 2 * flags).astype(bf16).reshape(2, 2, quarter)
     s_half = pick(core, signs[:, 0], signs[:, 1]).reshape(half)
-    block = whole_block(partial, far, jnp.broadcast_to(s_half[:, None], (half, PAD)))
-
-    far_block = move(block, lambda chip, core: (chip + (n_row // 2) * (1 - 2 * core), core))
-    pair = side_by_side(block, far_block, FLOPS)
+    signed = jnp.concatenate([partial, jnp.broadcast_to(s_half[:, None], (half, PAD))], axis=1)
+
+    step = n_row // 2
+    meeting = [
+        [((chip // n_row) * 2 + side) * n_row + chip % n_row for chip in range(first, 2 * n_row, step)]
+        for first in range(step)
+        for side in range(2)
+    ]
+    gathered = lax.all_gather(signed, ZLINE, axis=0, tiled=True, axis_index_groups=meeting)
+    pair = whole_pair(gathered)
     other_pair = other_core(pair)
     two_away = move(pair, lambda chip, core: (chip + 2 - 4 * core, core))
     next_own = move(pair, lambda chip, core: (chip + 1 - 2 * core, core))
     next_other = move(other_pair, lambda chip, core: (chip + 1 - 2 * core, core))
-    own = pick(high, block[:quarter], block[quarter:])
+    place = jnp.where(lax.axis_index("row") < step, 0, half) + jnp.where(high, quarter, 0)
+    own = lax.dynamic_slice_in_dim(pair, place, quarter, 0)
     col = lax.all_to_all(
         jnp.broadcast_to(own[None], (n_col,) + own.shape), "col", 0, 0, tiled=True
     ).reshape(n_col * quarter, width + PAD)

time: 123 us -> 125 us (1.016)
  blocking collectives: 39.2 us -> 67.5 us
  starting transfers between devices: 61.5 us -> 40.2 us
  waiting for transfers between devices: 6.21 us -> 2.04 us
    all_gather x0 -> x1, blocking collectives: none -> 27.2 us  [shards(): lax.all_gather(signed, ZLINE, axis=0, tiled=True, axis_index_groups=meeting)]
    ppermute x10 -> x8, starting transfers between devices: 54.8 us -> 33.6 us  [move(): return lax.ppermute(value, ZLINE, line_permutation(shift, n_row))]
    ppermute x10 -> x8, waiting for transfers between devices: 6.2 us -> 2.04 us  [move(): return lax.ppermute(value, ZLINE, line_permutation(shift, n_row))]
    all_gather x1, blocking collectives: 16.6 us -> 18.3 us  [shards(): grad = lax.all_gather(grad, 'tensor', axis=0, tiled=True)]
  transfers between devices with their start and end apart: 11 -> 9, of which waited for: 2 -> 2; matrix products, arithmetic and copies ran while one was open for 1% -> 0% of each run, Pallas kernels for 4% -> 4%
where the time goes in v9:
time: 125 us
  blocking collectives  67.5 us (54%)
  starting transfers between devices  40.2 us (32%)
  Pallas kernels  12.6 us (10%)
  waiting for transfers between devices  2.04 us (2%)
  local copies, waits for them, and re-layouts  1.39 us (1%)
    ppermute x8, starting transfers between devices, move(): return lax.ppermute(value, ZLINE, line_permutation(shift, n_row))  33.6 us
    all_gather x1, blocking collectives, shards(): lax.all_gather(signed, ZLINE, axis=0, tiled=True, axis_index_groups=meeting)  27.2 us
    all_to_all x1, blocking collectives, shards(): lax.all_to_all(part.reshape(n_col, quarter, width), 'col', 0, 0, tiled=True)  21.9 us
    all_gather x1, blocking collectives, shards(): grad = lax.all_gather(grad, 'tensor', axis=0, tiled=True)  18.3 us
    pallas_call x3, Pallas kernels, tiles(): pl.pallas_call(functools.partial(tile_kernel, len(pieces), bool(held), la...  7.26 us
    all_to_all x1, starting transfers between devices, shards(): lax.all_to_all(jnp.broadcast_to(own[None], (n_col,) + own.shape), 'col',...  6.54 us
    pallas_call x1, Pallas kernels, projection(): pl.pallas_call(projection_kernel, out_shape=(jax.ShapeDtypeStruct((rows /...  3.15 us
  transfers between devices with their start and end apart: 9, of which 2 were waited for; matrix products, arithmetic and copies ran while one was open for 0% of the time, Pallas kernels for 4%

profile of v9, /device:TPU:1, one launch (start us, length us, event | category | flops | bytes accessed | tf_op | source)
XLA Modules:
  0.0 125.0 jit_solution(1328612240704870636)
XLA Ops:
  0.0 3.2 %shard_map.46 = (bf16[64,1024]{1,0:T(8,128)(2,1)}, f32[64,1024]{1,0:T(8,128)}) custom-call(s32[1]{0:T(128)} %bitcast.core_ref, bf16[128,1536]{1,0:T(8,128)(2,1)} %features_ref.1, bf16[1536,1024]{1,0:T(8,128)(2,1)} %w_ref.3), custom_call_target="tpu_custom_call" | custom-call | flops 402653184 | bytes 3145728 | tf_op jit(solution)/shard_map/pallas_call | solution.py:69
  3.2 8.8 %collective-permute-start = (bf16[64,1024]{1,0:T(8,128)(2,1)}, bf16[64,1024]{1,0:T(8,128)(2,1)S(1)}, u32[]{:S(2)}, u32[]{:S(2)}) collective-permute-start(bf16[64,1024]{1,0:T(8,128)(2,1)} %get-tuple-element.12), channel_id=1, source_target_pairs={{0,128},{128,0},{16,144},{144,16},{32,160},{160,32},{48,176},{176,... | collective-permute-start | bytes 393224 | tf_op jit(solution)/shard_map/ppermute | solution.py:270
  12.0 0.1 reshape.25
  12.1 0.1 select_n.41
  12.2 0.9 collective-permute-done
  13.1 1.0 add_convert_fusion
  14.1 0.1 broadcast_in_dim.4
  14.2 27.2 %all_gather.6.gathered_ref = bf16[256,1152]{1,0:T(8,128)(2,1)S(1)} all-gather(bf16[64,1152]{1,0:T(8,128)(2,1)S(1)} %pad_maximum_fusion), channel_id=1, replica_groups={{0,64,256,320},{128,192,384,448},{16,80,272,336},{144,208,400,464},{32,..., dimensions={0}, use_global_device_ids=true | all-gather | bytes 737280 | tf_op jit(solution)/shard_map/all_gather | solution.py:287
  41.4 0.2 shard_map.47.refs_2_
  41.6 0.0 copy-start.1
  41.6 1.1 broadcast_in_dim.5
  42.7 6.5 %all-to-all-start = ((bf16[16,32,1152]{2,1,0:T(8,128)(2,1)}), bf16[16,32,1152]{2,1,0:T(8,128)(2,1)S(1)}, u32[]{:S(2)}, u32[]{:S(2)}) async-start(bf16[16,32,1152]{2,1,0:T(8,128)(2,1)} %broadcast_in_dim.5), calls=%async_computation | async-start | bytes 2359296 | tf_op jit(solution)/shard_map/all_to_all | solution.py:295
  49.3 6.3 %collective-permute-start.1 = (bf16[128,1152]{1,0:T(8,128)(2,1)S(1)}, bf16[128,1152]{1,0:T(8,128)(2,1)S(1)}, u32[]{:S(2)}, u32[]{:S(2)}) collective-permute-start(bf16[128,1152]{1,0:T(8,128)(2,1)S(1)} %shard_map.47.refs_2_), channel_id=1, source_target_pairs={{0,128},{128,0},{16,144},{144,16},{32,160},{160,32},{48,176},{176,... | collective-permute-start | bytes 884744 | tf_op jit(solution)/shard_map/ppermute | solution.py:270
  55.6 3.5 %collective-permute-start.3 = (bf16[128,1152]{1,0:T(8,128)(2,1)S(1)}, bf16[128,1152]{1,0:T(8,128)(2,1)S(1)}, u32[]{:S(2)}, u32[]{:S(2)}) collective-permute-start(bf16[128,1152]{1,0:T(8,128)(2,1)S(1)} %shard_map.47.refs_2_), channel_id=1, source_target_pairs={{0,32},{128,480},{16,48},{144,496},{32,64},{160,128},{48,80},{176,... | collective-permute-start | bytes 884744 | tf_op jit(solution)/shard_map/ppermute | solution.py:270
  59.1 2.3 %collective-permute-start.6 = (bf16[128,1152]{1,0:T(8,128)(2,1)S(1)}, bf16[128,1152]{1,0:T(8,128)(2,1)S(1)}, u32[]{:S(2)}, u32[]{:S(2)}) collective-permute-start(bf16[128,1152]{1,0:T(8,128)(2,1)S(1)} %shard_map.47.refs_2_), channel_id=1, source_target_pairs={{0,16},{128,496},{16,32},{144,128},{32,48},{160,144},{48,64},{176,... | collective-permute-start | bytes 884744 | tf_op jit(solution)/shard_map/ppermute | solution.py:270
  61.4 0.0 collective-permute-done.1.refs_3_
  61.4 2.7 %collective-permute-start.2 = (bf16[128,1152]{1,0:T(8,128)(2,1)S(1)}, bf16[128,1152]{1,0:T(8,128)(2,1)S(1)}, u32[]{:S(2)}, u32[]{:S(2)}) collective-permute-start(bf16[128,1152]{1,0:T(8,128)(2,1)S(1)} %collective-permute-done.1.refs_3_), channel_id=1, source_target_pairs={{0,16},{128,496},{16,32},{144,128},{32,48},{160,144},{48,64},{176,... | collective-permute-start | bytes 884744 | tf_op jit(solution)/shard_map/ppermute | solution.py:270
  64.1 2.2 %shard_map.48 = (f32[512,128]{1,0:T(8,128)S(1)}, f32[512,1024]{1,0:T(8,128)S(1)}) custom-call(f32[5]{0:T(128)S(1)} %copy-done.1, bf16[512,1152]{1,0:T(8,128)(2,1)S(1)} %bitcast.3, bf16[128,1152]{1,0:T(8,128)(2,1)S(1)} %shard_map.47.refs_2_, bf16[128,1152]{1,0:T(8,128)(2,1)S(1)} %collective-permute-done.1.refs_3_), custom_call_target="tpu_custom_call" | custom-call | flops 536870912 | bytes 2097152 | tf_op jit(solution)/shard_map/pallas_call | solution.py:246
  66.3 1.1 collective-permute-done.3.value_ref
  67.4 5.8 %collective-permute-start.4 = (bf16[128,1152]{1,0:T(8,128)(2,1)S(1)}, bf16[128,1152]{1,0:T(8,128)(2,1)S(1)}, u32[]{:S(2)}, u32[]{:S(2)}) collective-permute-start(bf16[128,1152]{1,0:T(8,128)(2,1)S(1)} %shard_map.49.refs_2_), channel_id=1, source_target_pairs={{0,128},{128,0},{16,144},{144,16},{32,160},{160,32},{48,176},{176,... | collective-permute-start | bytes 884744 | tf_op jit(solution)/shard_map/ppermute | solution.py:270
  73.2 1.9 %collective-permute-start.7 = (bf16[128,1152]{1,0:T(8,128)(2,1)S(1)}, bf16[128,1152]{1,0:T(8,128)(2,1)S(1)}, u32[]{:S(2)}, u32[]{:S(2)}) collective-permute-start(bf16[128,1152]{1,0:T(8,128)(2,1)S(1)} %shard_map.51.refs_4_), channel_id=1, source_target_pairs={{0,128},{128,0},{16,144},{144,16},{32,160},{160,32},{48,176},{176,... | collective-permute-start | bytes 884744 | tf_op jit(solution)/shard_map/ppermute | solution.py:270
  75.1 0.0 collective-permute-done.2.value_ref
  75.2 2.4 %collective-permute-start.5 = (bf16[128,1152]{1,0:T(8,128)(2,1)S(1)}, bf16[128,1152]{1,0:T(8,128)(2,1)S(1)}, u32[]{:S(2)}, u32[]{:S(2)}) collective-permute-start(bf16[128,1152]{1,0:T(8,128)(2,1)S(1)} %shard_map.50.refs_2_), channel_id=1, source_target_pairs={{0,128},{128,0},{16,144},{144,16},{32,160},{160,32},{48,176},{176,... | collective-permute-start | bytes 884744 | tf_op jit(solution)/shard_map/ppermute | solution.py:270
  77.6 0.0 collective-permute-done.7.refs_5_
  77.6 2.7 %shard_map.52 = (f32[512,128]{1,0:T(8,128)S(1)}, f32[512,1024]{1,0:T(8,128)S(1)}) custom-call(f32[5]{0:T(128)S(1)} %copy-done.1, bf16[512,1152]{1,0:T(8,128)(2,1)S(1)} %bitcast.4, bf16[128,1152]{1,0:T(8,128)(2,1)S(1)} %shard_map.49.refs_2_, bf16[128,1152]{1,0:T(8,128)(2,1)S(1)} %collective-permute-done.4.first_ref.refs_3_, ...), custom_call_target="tpu_custom_call" | custom-call | flops 1073741824 | bytes 2097152 | tf_op jit(solution)/shard_map/pallas_call | solution.py:246
  80.3 0.0 collective-permute-done.5.refs_3_
  80.3 2.4 %shard_map.53 = bf16[512,1024]{1,0:T(8,128)(2,1)S(1)} custom-call(f32[5]{0:T(128)S(1)} %copy-done.1, bf16[512,1152]{1,0:T(8,128)(2,1)S(1)} %bitcast.5, bf16[128,1152]{1,0:T(8,128)(2,1)S(1)} %shard_map.50.refs_2_, bf16[128,1152]{1,0:T(8,128)(2,1)S(1)} %collective-permute-done.5.refs_3_, f32[512,128]{1,0:T(8,128)S(1)} %get-tuple-element.15.refs_4_, ...), custom_call_target="tpu_custom_call" | custom-call | flops 536870912 | bytes 2097152 | tf_op jit(solution)/shard_map/pallas_call | solution.py:246
  82.7 0.0 copy-start
  82.7 21.9 %all_to_all.10.parts_ref = bf16[16,32,1024]{2,1,0:T(8,128)(2,1)S(1)} all-to-all(bf16[16,32,1024]{2,1,0:T(8,128)(2,1)S(1)} %bitcast.6), channel_id=1, replica_groups=mesh['tensor'=4,'row'=8,'col'=16] {'col'}, dimensions={0} | all-to-all | bytes 2097152 | tf_op jit(solution)/shard_map/all_to_all | solution.py:305
  104.6 0.1 shard_map.54
  104.8 18.3 %all_gather.7.grad_ref = bf16[128,1024]{1,0:T(8,128)(2,1)S(1)} all-gather(bf16[32,1024]{1,0:T(8,128)(2,1)S(1)} %shard_map.54), channel_id=1, replica_groups=mesh['tensor'=4,'row'=8,'col'=16] {'tensor'}, dimensions={0}, use_global_device_ids=true | all-gather | bytes 327680 | tf_op jit(solution)/shard_map/all_gather | solution.py:307
  123.1 1.9 %shard_map.55 = bf16[128,1536]{1,0:T(8,128)(2,1)} custom-call(bf16[128,1024]{1,0:T(8,128)(2,1)S(1)} %all_gather.7.grad_ref, bf16[1536,1024]{1,0:T(8,128)(2,1)S(1)} %copy-done), custom_call_target="tpu_custom_call" | custom-call | flops 402653184 | bytes 3145728 | tf_op jit(solution)/shard_map/pallas_call | solution.py:136
  (14 shorter events, 0.1 us)
Async XLA Ops:
  0.0 11.9 %copy-start.2 = (s32[128]{0:T(128)S(1)}, s32[128]{0:T(128)}, u32[]{:S(2)}) copy-start(s32[128]{0:T(128)} %param.6) | copy-start | bytes 1540
  3.2 10.0 %collective-permute-start = (bf16[64,1024]{1,0:T(8,128)(2,1)}, bf16[64,1024]{1,0:T(8,128)(2,1)S(1)}, u32[]{:S(2)}, u32[]{:S(2)}) collective-permute-start(bf16[64,1024]{1,0:T(8,128)(2,1)} %get-tuple-element.12), channel_id=1, source_target_pairs={{0,128},{128,0},{16,144},{144,16},{32,160},{160,32},{48,176},{176,... | collective-permute-start | bytes 393224 | tf_op jit(solution)/shard_map/ppermute | solution.py:270
  41.6 22.5 %copy-start.1 = (f32[5]{0:T(128)S(1)}, f32[5]{0:T(128)}, u32[]{:S(2)}) copy-start(f32[5]{0:T(128)} %refs_0_.5) | copy-start | bytes 64
  42.7 21.4 %all-to-all-start = ((bf16[16,32,1152]{2,1,0:T(8,128)(2,1)}), bf16[16,32,1152]{2,1,0:T(8,128)(2,1)S(1)}, u32[]{:S(2)}, u32[]{:S(2)}) async-start(bf16[16,32,1152]{2,1,0:T(8,128)(2,1)} %broadcast_in_dim.5), calls=%async_computation | async-start | bytes 2359296 | tf_op jit(solution)/shard_map/all_to_all | solution.py:295
  49.3 12.1 %collective-permute-start.1 = (bf16[128,1152]{1,0:T(8,128)(2,1)S(1)}, bf16[128,1152]{1,0:T(8,128)(2,1)S(1)}, u32[]{:S(2)}, u32[]{:S(2)}) collective-permute-start(bf16[128,1152]{1,0:T(8,128)(2,1)S(1)} %shard_map.47.refs_2_), channel_id=1, source_target_pairs={{0,128},{128,0},{16,144},{144,16},{32,160},{160,32},{48,176},{176,... | collective-permute-start | bytes 884744 | tf_op jit(solution)/shard_map/ppermute | solution.py:270
  55.6 11.9 %collective-permute-start.3 = (bf16[128,1152]{1,0:T(8,128)(2,1)S(1)}, bf16[128,1152]{1,0:T(8,128)(2,1)S(1)}, u32[]{:S(2)}, u32[]{:S(2)}) collective-permute-start(bf16[128,1152]{1,0:T(8,128)(2,1)S(1)} %shard_map.47.refs_2_), channel_id=1, source_target_pairs={{0,32},{128,480},{16,48},{144,496},{32,64},{160,128},{48,80},{176,... | collective-permute-start | bytes 884744 | tf_op jit(solution)/shard_map/ppermute | solution.py:270
  59.1 14.1 %collective-permute-start.6 = (bf16[128,1152]{1,0:T(8,128)(2,1)S(1)}, bf16[128,1152]{1,0:T(8,128)(2,1)S(1)}, u32[]{:S(2)}, u32[]{:S(2)}) collective-permute-start(bf16[128,1152]{1,0:T(8,128)(2,1)S(1)} %shard_map.47.refs_2_), channel_id=1, source_target_pairs={{0,16},{128,496},{16,32},{144,128},{32,48},{160,144},{48,64},{176,... | collective-permute-start | bytes 884744 | tf_op jit(solution)/shard_map/ppermute | solution.py:270
  61.4 13.7 %collective-permute-start.2 = (bf16[128,1152]{1,0:T(8,128)(2,1)S(1)}, bf16[128,1152]{1,0:T(8,128)(2,1)S(1)}, u32[]{:S(2)}, u32[]{:S(2)}) collective-permute-start(bf16[128,1152]{1,0:T(8,128)(2,1)S(1)} %collective-permute-done.1.refs_3_), channel_id=1, source_target_pairs={{0,16},{128,496},{16,32},{144,128},{32,48},{160,144},{48,64},{176,... | collective-permute-start | bytes 884744 | tf_op jit(solution)/shard_map/ppermute | solution.py:270
  67.4 7.7 %collective-permute-start.4 = (bf16[128,1152]{1,0:T(8,128)(2,1)S(1)}, bf16[128,1152]{1,0:T(8,128)(2,1)S(1)}, u32[]{:S(2)}, u32[]{:S(2)}) collective-permute-start(bf16[128,1152]{1,0:T(8,128)(2,1)S(1)} %shard_map.49.refs_2_), channel_id=1, source_target_pairs={{0,128},{128,0},{16,144},{144,16},{32,160},{160,32},{48,176},{176,... | collective-permute-start | bytes 884744 | tf_op jit(solution)/shard_map/ppermute | solution.py:270
  73.2 4.4 %collective-permute-start.7 = (bf16[128,1152]{1,0:T(8,128)(2,1)S(1)}, bf16[128,1152]{1,0:T(8,128)(2,1)S(1)}, u32[]{:S(2)}, u32[]{:S(2)}) collective-permute-start(bf16[128,1152]{1,0:T(8,128)(2,1)S(1)} %shard_map.51.refs_4_), channel_id=1, source_target_pairs={{0,128},{128,0},{16,144},{144,16},{32,160},{160,32},{48,176},{176,... | collective-permute-start | bytes 884744 | tf_op jit(solution)/shard_map/ppermute | solution.py:270
  75.2 5.1 %collective-permute-start.5 = (bf16[128,1152]{1,0:T(8,128)(2,1)S(1)}, bf16[128,1152]{1,0:T(8,128)(2,1)S(1)}, u32[]{:S(2)}, u32[]{:S(2)}) collective-permute-start(bf16[128,1152]{1,0:T(8,128)(2,1)S(1)} %shard_map.50.refs_2_), channel_id=1, source_target_pairs={{0,128},{128,0},{16,144},{144,16},{32,160},{160,32},{48,176},{176,... | collective-permute-start | bytes 884744 | tf_op jit(solution)/shard_map/ppermute | solution.py:270
  82.7 40.4 %copy-start = (bf16[1536,1024]{1,0:T(8,128)(2,1)S(1)}, bf16[1536,1024]{1,0:T(8,128)(2,1)}, u32[]{:S(2)}) copy-start(bf16[1536,1024]{1,0:T(8,128)(2,1)} %w_ref.3) | copy-start | bytes 9437188

commit v10 on v8

--- a/solution.py
+++ b/solution.py
@@ -90,10 +90,10 @@
     )(core, features, w_proj)
 
 
-def block_kernel(near_ref, far_ref, signs_ref, block_ref):
+def block_kernel(both_ref, signs_ref, block_ref):
     f32, bf16 = jnp.float32, jnp.bfloat16
-    half, width = near_ref.shape
-    rows = (near_ref[...].astype(f32) + far_ref[...].astype(f32)).astype(bf16)
+    half, width = both_ref.shape[0] // 2, both_ref.shape[1]
+    rows = (both_ref[:half].astype(f32) + both_ref[half:].astype(f32)).astype(bf16)
     block_ref[:, :width] = rows
     norm = jnp.sum(jnp.square(rows.astype(f32)), axis=1, keepdims=True)
     first = norm.astype(bf16).astype(f32)
@@ -104,19 +104,19 @@
     block_ref[:, width:] = jnp.where(lane == 0, signs_ref[...], tail).astype(bf16)
 
 
-def whole_block(near, far, signs):
-    vmem = pl.BlockSpec(memory_space=pltpu.VMEM)
-    half, width = near.shape
+def whole_block(both, signs):
+    vmem = pl.BlockSpec(memory_space=pltpu.VMEM)
+    half, width = both.shape[0] // 2, both.shape[1]
     return pl.pallas_call(
         block_kernel,
-        out_shape=jax.ShapeDtypeStruct((half, width + PAD), near.dtype),
-        in_specs=[vmem] * 3,
+        out_shape=jax.ShapeDtypeStruct((half, width + PAD), both.dtype),
+        in_specs=[vmem] * 2,
         out_specs=vmem,
         compiler_params=pltpu.CompilerParams(vmem_limit_bytes=16 * 2**20),
         cost_estimate=pl.CostEstimate(
             flops=4 * half * width, bytes_accessed=6 * half * width, transcendentals=0
         ),
-    )(near, far, signs)
+    )(both, signs)
 
 
 def result_kernel(grad_ref, w_ref, out_ref):
@@ -287,10 +287,13 @@
 
     away, kept = projection(jnp.reshape(tpos % 2, (1,)), features, w_proj)
     partial = (kept + other_core(away).astype(f32)).astype(bf16)
-    far = move(partial, lambda chip, core: (chip + n_row, core))
+    holders = [
+        [(side + 2 * end) * n_row + row for end in range(2)] for row in range(n_row) for side in range(2)
+    ]
+    both = lax.all_gather(partial, ZLINE, axis=0, tiled=True, axis_index_groups=holders)
     signs = (1 - 2 * flags).astype(f32).reshape(2, 2, quarter)
     s_half = pick(core, signs[:, 0], signs[:, 1]).reshape(half)
-    block = whole_block(partial, far, jnp.broadcast_to(s_half[:, None], (half, PAD)))
+    block = whole_block(both, jnp.broadcast_to(s_half[:, None], (half, PAD)))
 
     far_block = move(block, lambda chip, core: (chip + (n_row // 2) * (1 - 2 * core), core))
     pair = side_by_side(block, far_block, FLOPS)

time: 123 us -> 122 us (level)
  blocking collectives: 39.2 us -> 53.3 us
  starting transfers between devices: 61.5 us -> 51.4 us
  waiting for transfers between devices: 6.21 us -> 0.97 us
    all_gather x0 -> x1, blocking collectives: none -> 14.1 us  [shards(): lax.all_gather(partial, ZLINE, axis=0, tiled=True, axis_index_groups=hold...]
    ppermute x10 -> x9, starting transfers between devices: 54.8 us -> 44.7 us  [move(): return lax.ppermute(value, ZLINE, line_permutation(shift, n_row))]
    ppermute x10 -> x9, waiting for transfers between devices: 6.2 us -> 0.97 us  [move(): return lax.ppermute(value, ZLINE, line_permutation(shift, n_row))]
  transfers between devices with their start and end apart: 11 -> 10, of which waited for: 2 -> 1; matrix products, arithmetic and copies ran while one was open for 1% -> 1% of each run, Pallas kernels for 4% -> 4%
where the time goes in v10:
time: 122 us; the launch traced here: 121 us
  blocking collectives  53.3 us (44%)
  starting transfers between devices  51.4 us (42%)
  Pallas kernels  12.6 us (10%)
  local copies, waits for them, and re-layouts  1.38 us (1%)
    ppermute x9, starting transfers between devices, move(): return lax.ppermute(value, ZLINE, line_permutation(shift, n_row))  44.7 us
    all_to_all x1, blocking collectives, shards(): lax.all_to_all(part.reshape(n_col, quarter, width), 'col', 0, 0, tiled=True)  22.5 us
    all_gather x1, blocking collectives, shards(): grad = lax.all_gather(grad, 'tensor', axis=0, tiled=True)  16.7 us
    all_gather x1, blocking collectives, shards(): lax.all_gather(partial, ZLINE, axis=0, tiled=True, axis_index_groups=hold...  14.1 us
    pallas_call x3, Pallas kernels, tiles(): pl.pallas_call(functools.partial(tile_kernel, len(pieces), bool(held), la...  7.26 us
    all_to_all x1, starting transfers between devices, shards(): lax.all_to_all(jnp.broadcast_to(own[None], (n_col,) + own.shape), 'col',...  6.74 us
    pallas_call x1, Pallas kernels, projection(): pl.pallas_call(projection_kernel, out_shape=(jax.ShapeDtypeStruct((rows /...  3.15 us
  transfers between devices with their start and end apart: 10, of which 1 were waited for; matrix products, arithmetic and copies ran while one was open for 1% of the time, Pallas kernels for 4%

profile of v10, /device:TPU:1, one launch (start us, length us, event | category | flops | bytes accessed | tf_op | source)
XLA Modules:
  0.0 121.0 jit_solution(3236218170555325713)
XLA Ops:
  0.0 3.2 %shard_map.46 = (bf16[64,1024]{1,0:T(8,128)(2,1)}, f32[64,1024]{1,0:T(8,128)}) custom-call(s32[1]{0:T(128)} %bitcast.core_ref, bf16[128,1536]{1,0:T(8,128)(2,1)} %features_ref.1, bf16[1536,1024]{1,0:T(8,128)(2,1)} %w_ref.3), custom_call_target="tpu_custom_call" | custom-call | flops 402653184 | bytes 3145728 | tf_op jit(solution)/shard_map/pallas_call | solution.py:70
  3.2 8.8 %collective-permute-start = (bf16[64,1024]{1,0:T(8,128)(2,1)}, bf16[64,1024]{1,0:T(8,128)(2,1)S(1)}, u32[]{:S(2)}, u32[]{:S(2)}) collective-permute-start(bf16[64,1024]{1,0:T(8,128)(2,1)} %get-tuple-element.12), channel_id=1, source_target_pairs={{0,128},{128,0},{16,144},{144,16},{32,160},{160,32},{48,176},{176,... | collective-permute-start | bytes 393224 | tf_op jit(solution)/shard_map/ppermute | solution.py:283
  12.0 0.1 reshape.25
  12.1 0.1 select_n.41
  12.2 1.0 collective-permute-done
  13.1 1.0 add_convert_fusion
  14.1 14.1 %all_gather.6.both_ref = bf16[128,1024]{1,0:T(8,128)(2,1)S(1)} all-gather(bf16[64,1024]{1,0:T(8,128)(2,1)S(1)} %add_convert_fusion), channel_id=1, replica_groups={{0,256},{128,384},{16,272},{144,400},{32,288},{160,416},{48,304},{176,4..., dimensions={0}, use_global_device_ids=true | all-gather | bytes 393216 | tf_op jit(solution)/shard_map/all_gather | solution.py:293
  28.2 0.1 broadcast_in_dim.4.signs_ref
  28.3 0.1 shard_map.47.first_ref
  28.4 7.1 %collective-permute-start.1 = (bf16[64,1152]{1,0:T(8,128)(2,1)S(1)}, bf16[64,1152]{1,0:T(8,128)(2,1)S(1)}, u32[]{:S(2)}, u32[]{:S(2)}) collective-permute-start(bf16[64,1152]{1,0:T(8,128)(2,1)S(1)} %shard_map.47.first_ref), channel_id=1, source_target_pairs={{0,64},{128,448},{16,80},{144,464},{32,96},{160,480},{48,112},{176... | collective-permute-start | bytes 442376 | tf_op jit(solution)/shard_map/ppermute | solution.py:283
  35.5 1.1 broadcast_in_dim.5
  36.7 6.7 %all-to-all-start = ((bf16[16,32,1152]{2,1,0:T(8,128)(2,1)}), bf16[16,32,1152]{2,1,0:T(8,128)(2,1)S(1)}, u32[]{:S(2)}, u32[]{:S(2)}) async-start(bf16[16,32,1152]{2,1,0:T(8,128)(2,1)} %broadcast_in_dim.5), calls=%async_computation | async-start | bytes 2359296 | tf_op jit(solution)/shard_map/all_to_all | solution.py:305
  43.4 0.0 copy-start.1
  43.5 7.0 %collective-permute-start.2 = (bf16[128,1152]{1,0:T(8,128)(2,1)S(1)}, bf16[128,1152]{1,0:T(8,128)(2,1)S(1)}, u32[]{:S(2)}, u32[]{:S(2)}) collective-permute-start(bf16[128,1152]{1,0:T(8,128)(2,1)S(1)} %shard_map.48.refs_2_), channel_id=1, source_target_pairs={{0,128},{128,0},{16,144},{144,16},{32,160},{160,32},{48,176},{176,... | collective-permute-start | bytes 884744 | tf_op jit(solution)/shard_map/ppermute | solution.py:283
  50.4 8.6 %collective-permute-start.4 = (bf16[128,1152]{1,0:T(8,128)(2,1)S(1)}, bf16[128,1152]{1,0:T(8,128)(2,1)S(1)}, u32[]{:S(2)}, u32[]{:S(2)}) collective-permute-start(bf16[128,1152]{1,0:T(8,128)(2,1)S(1)} %shard_map.48.refs_2_), channel_id=1, source_target_pairs={{0,32},{128,480},{16,48},{144,496},{32,64},{160,128},{48,80},{176,... | collective-permute-start | bytes 884744 | tf_op jit(solution)/shard_map/ppermute | solution.py:283
  59.1 1.9 %collective-permute-start.7 = (bf16[128,1152]{1,0:T(8,128)(2,1)S(1)}, bf16[128,1152]{1,0:T(8,128)(2,1)S(1)}, u32[]{:S(2)}, u32[]{:S(2)}) collective-permute-start(bf16[128,1152]{1,0:T(8,128)(2,1)S(1)} %shard_map.48.refs_2_), channel_id=1, source_target_pairs={{0,16},{128,496},{16,32},{144,128},{32,48},{160,144},{48,64},{176,... | collective-permute-start | bytes 884744 | tf_op jit(solution)/shard_map/ppermute | solution.py:283
  61.0 2.2 %collective-permute-start.3 = (bf16[128,1152]{1,0:T(8,128)(2,1)S(1)}, bf16[128,1152]{1,0:T(8,128)(2,1)S(1)}, u32[]{:S(2)}, u32[]{:S(2)}) collective-permute-start(bf16[128,1152]{1,0:T(8,128)(2,1)S(1)} %collective-permute-done.2.refs_3_), channel_id=1, source_target_pairs={{0,16},{128,496},{16,32},{144,128},{32,48},{160,144},{48,64},{176,... | collective-permute-start | bytes 884744 | tf_op jit(solution)/shard_map/ppermute | solution.py:283
  63.2 2.2 %shard_map.49 = (f32[512,128]{1,0:T(8,128)S(1)}, f32[512,1024]{1,0:T(8,128)S(1)}) custom-call(f32[5]{0:T(128)S(1)} %copy-done.1, bf16[512,1152]{1,0:T(8,128)(2,1)S(1)} %bitcast.3, bf16[128,1152]{1,0:T(8,128)(2,1)S(1)} %shard_map.48.refs_2_, bf16[128,1152]{1,0:T(8,128)(2,1)S(1)} %collective-permute-done.2.refs_3_), custom_call_target="tpu_custom_call" | custom-call | flops 536870912 | bytes 2097152 | tf_op jit(solution)/shard_map/pallas_call | solution.py:259
  65.4 0.0 collective-permute-done.4.value_ref
  65.4 3.0 %collective-permute-start.5 = (bf16[128,1152]{1,0:T(8,128)(2,1)S(1)}, bf16[128,1152]{1,0:T(8,128)(2,1)S(1)}, u32[]{:S(2)}, u32[]{:S(2)}) collective-permute-start(bf16[128,1152]{1,0:T(8,128)(2,1)S(1)} %shard_map.50.refs_2_), channel_id=1, source_target_pairs={{0,128},{128,0},{16,144},{144,16},{32,160},{160,32},{48,176},{176,... | collective-permute-start | bytes 884744 | tf_op jit(solution)/shard_map/ppermute | solution.py:283
  68.5 0.0 collective-permute-done.7.value_ref
  68.5 3.0 %collective-permute-start.8 = (bf16[128,1152]{1,0:T(8,128)(2,1)S(1)}, bf16[128,1152]{1,0:T(8,128)(2,1)S(1)}, u32[]{:S(2)}, u32[]{:S(2)}) collective-permute-start(bf16[128,1152]{1,0:T(8,128)(2,1)S(1)} %shard_map.52.refs_4_), channel_id=1, source_target_pairs={{0,128},{128,0},{16,144},{144,16},{32,160},{160,32},{48,176},{176,... | collective-permute-start | bytes 884744 | tf_op jit(solution)/shard_map/ppermute | solution.py:283
  71.5 0.0 collective-permute-done.5.first_ref.refs_3_
  71.5 3.1 %collective-permute-start.6 = (bf16[128,1152]{1,0:T(8,128)(2,1)S(1)}, bf16[128,1152]{1,0:T(8,128)(2,1)S(1)}, u32[]{:S(2)}, u32[]{:S(2)}) collective-permute-start(bf16[128,1152]{1,0:T(8,128)(2,1)S(1)} %shard_map.51.refs_2_), channel_id=1, source_target_pairs={{0,128},{128,0},{16,144},{144,16},{32,160},{160,32},{48,176},{176,... | collective-permute-start | bytes 884744 | tf_op jit(solution)/shard_map/ppermute | solution.py:283
  74.7 0.0 collective-permute-done.8.refs_5_
  74.7 2.7 %shard_map.53 = (f32[512,128]{1,0:T(8,128)S(1)}, f32[512,1024]{1,0:T(8,128)S(1)}) custom-call(f32[5]{0:T(128)S(1)} %copy-done.1, bf16[512,1152]{1,0:T(8,128)(2,1)S(1)} %bitcast.4, bf16[128,1152]{1,0:T(8,128)(2,1)S(1)} %shard_map.50.refs_2_, bf16[128,1152]{1,0:T(8,128)(2,1)S(1)} %collective-permute-done.5.first_ref.refs_3_, ...), custom_call_target="tpu_custom_call" | custom-call | flops 1073741824 | bytes 2097152 | tf_op jit(solution)/shard_map/pallas_call | solution.py:259
  77.4 2.4 %shard_map.54 = bf16[512,1024]{1,0:T(8,128)(2,1)S(1)} custom-call(f32[5]{0:T(128)S(1)} %copy-done.1, bf16[512,1152]{1,0:T(8,128)(2,1)S(1)} %bitcast.5, bf16[128,1152]{1,0:T(8,128)(2,1)S(1)} %shard_map.51.refs_2_, bf16[128,1152]{1,0:T(8,128)(2,1)S(1)} %collective-permute-done.6.refs_3_, f32[512,128]{1,0:T(8,128)S(1)} %get-tuple-element.15.refs_4_, ...), custom_call_target="tpu_custom_call" | custom-call | flops 536870912 | bytes 2097152 | tf_op jit(solution)/shard_map/pallas_call | solution.py:259
  79.8 0.0 copy-start
  79.8 22.5 %all_to_all.10.parts_ref = bf16[16,32,1024]{2,1,0:T(8,128)(2,1)S(1)} all-to-all(bf16[16,32,1024]{2,1,0:T(8,128)(2,1)S(1)} %bitcast.6), channel_id=1, replica_groups=mesh['tensor'=4,'row'=8,'col'=16] {'col'}, dimensions={0} | all-to-all | bytes 2097152 | tf_op jit(solution)/shard_map/all_to_all | solution.py:315
  102.3 0.1 shard_map.55
  102.5 16.7 %all_gather.7.grad_ref = bf16[128,1024]{1,0:T(8,128)(2,1)S(1)} all-gather(bf16[32,1024]{1,0:T(8,128)(2,1)S(1)} %shard_map.55), channel_id=1, replica_groups=mesh['tensor'=4,'row'=8,'col'=16] {'tensor'}, dimensions={0}, use_global_device_ids=true | all-gather | bytes 327680 | tf_op jit(solution)/shard_map/all_gather | solution.py:317
  119.1 1.9 %shard_map.56 = bf16[128,1536]{1,0:T(8,128)(2,1)} custom-call(bf16[128,1024]{1,0:T(8,128)(2,1)S(1)} %all_gather.7.grad_ref, bf16[1536,1024]{1,0:T(8,128)(2,1)S(1)} %copy-done), custom_call_target="tpu_custom_call" | custom-call | flops 402653184 | bytes 3145728 | tf_op jit(solution)/shard_map/pallas_call | solution.py:131
  (16 shorter events, 0.1 us)
Async XLA Ops:
  0.0 11.9 %copy-start.2 = (s32[128]{0:T(128)S(1)}, s32[128]{0:T(128)}, u32[]{:S(2)}) copy-start(s32[128]{0:T(128)} %param.6) | copy-start | bytes 1540
  3.2 10.0 %collective-permute-start = (bf16[64,1024]{1,0:T(8,128)(2,1)}, bf16[64,1024]{1,0:T(8,128)(2,1)S(1)}, u32[]{:S(2)}, u32[]{:S(2)}) collective-permute-start(bf16[64,1024]{1,0:T(8,128)(2,1)} %get-tuple-element.12), channel_id=1, source_target_pairs={{0,128},{128,0},{16,144},{144,16},{32,160},{160,32},{48,176},{176,... | collective-permute-start | bytes 393224 | tf_op jit(solution)/shard_map/ppermute | solution.py:283
  28.4 15.0 %collective-permute-start.1 = (bf16[64,1152]{1,0:T(8,128)(2,1)S(1)}, bf16[64,1152]{1,0:T(8,128)(2,1)S(1)}, u32[]{:S(2)}, u32[]{:S(2)}) collective-permute-start(bf16[64,1152]{1,0:T(8,128)(2,1)S(1)} %shard_map.47.first_ref), channel_id=1, source_target_pairs={{0,64},{128,448},{16,80},{144,464},{32,96},{160,480},{48,112},{176... | collective-permute-start | bytes 442376 | tf_op jit(solution)/shard_map/ppermute | solution.py:283
  36.7 26.5 %all-to-all-start = ((bf16[16,32,1152]{2,1,0:T(8,128)(2,1)}), bf16[16,32,1152]{2,1,0:T(8,128)(2,1)S(1)}, u32[]{:S(2)}, u32[]{:S(2)}) async-start(bf16[16,32,1152]{2,1,0:T(8,128)(2,1)} %broadcast_in_dim.5), calls=%async_computation | async-start | bytes 2359296 | tf_op jit(solution)/shard_map/all_to_all | solution.py:305
  43.4 19.8 %copy-start.1 = (f32[5]{0:T(128)S(1)}, f32[5]{0:T(128)}, u32[]{:S(2)}) copy-start(f32[5]{0:T(128)} %refs_0_.5) | copy-start | bytes 64
  43.5 17.5 %collective-permute-start.2 = (bf16[128,1152]{1,0:T(8,128)(2,1)S(1)}, bf16[128,1152]{1,0:T(8,128)(2,1)S(1)}, u32[]{:S(2)}, u32[]{:S(2)}) collective-permute-start(bf16[128,1152]{1,0:T(8,128)(2,1)S(1)} %shard_map.48.refs_2_), channel_id=1, source_target_pairs={{0,128},{128,0},{16,144},{144,16},{32,160},{160,32},{48,176},{176,... | collective-permute-start | bytes 884744 | tf_op jit(solution)/shard_map/ppermute | solution.py:283
  50.4 15.0 %collective-permute-start.4 = (bf16[128,1152]{1,0:T(8,128)(2,1)S(1)}, bf16[128,1152]{1,0:T(8,128)(2,1)S(1)}, u32[]{:S(2)}, u32[]{:S(2)}) collective-permute-start(bf16[128,1152]{1,0:T(8,128)(2,1)S(1)} %shard_map.48.refs_2_), channel_id=1, source_target_pairs={{0,32},{128,480},{16,48},{144,496},{32,64},{160,128},{48,80},{176,... | collective-permute-start | bytes 884744 | tf_op jit(solution)/shard_map/ppermute | solution.py:283
  59.1 9.4 %collective-permute-start.7 = (bf16[128,1152]{1,0:T(8,128)(2,1)S(1)}, bf16[128,1152]{1,0:T(8,128)(2,1)S(1)}, u32[]{:S(2)}, u32[]{:S(2)}) collective-permute-start(bf16[128,1152]{1,0:T(8,128)(2,1)S(1)} %shard_map.48.refs_2_), channel_id=1, source_target_pairs={{0,16},{128,496},{16,32},{144,128},{32,48},{160,144},{48,64},{176,... | collective-permute-start | bytes 884744 | tf_op jit(solution)/shard_map/ppermute | solution.py:283
  61.0 10.5 %collective-permute-start.3 = (bf16[128,1152]{1,0:T(8,128)(2,1)S(1)}, bf16[128,1152]{1,0:T(8,128)(2,1)S(1)}, u32[]{:S(2)}, u32[]{:S(2)}) collective-permute-start(bf16[128,1152]{1,0:T(8,128)(2,1)S(1)} %collective-permute-done.2.refs_3_), channel_id=1, source_target_pairs={{0,16},{128,496},{16,32},{144,128},{32,48},{160,144},{48,64},{176,... | collective-permute-start | bytes 884744 | tf_op jit(solution)/shard_map/ppermute | solution.py:283
  65.4 6.1 %collective-permute-start.5 = (bf16[128,1152]{1,0:T(8,128)(2,1)S(1)}, bf16[128,1152]{1,0:T(8,128)(2,1)S(1)}, u32[]{:S(2)}, u32[]{:S(2)}) collective-permute-start(bf16[128,1152]{1,0:T(8,128)(2,1)S(1)} %shard_map.50.refs_2_), channel_id=1, source_target_pairs={{0,128},{128,0},{16,144},{144,16},{32,160},{160,32},{48,176},{176,... | collective-permute-start | bytes 884744 | tf_op jit(solution)/shard_map/ppermute | solution.py:283
  68.5 6.2 %collective-permute-start.8 = (bf16[128,1152]{1,0:T(8,128)(2,1)S(1)}, bf16[128,1152]{1,0:T(8,128)(2,1)S(1)}, u32[]{:S(2)}, u32[]{:S(2)}) collective-permute-start(bf16[128,1152]{1,0:T(8,128)(2,1)S(1)} %shard_map.52.refs_4_), channel_id=1, source_target_pairs={{0,128},{128,0},{16,144},{144,16},{32,160},{160,32},{48,176},{176,... | collective-permute-start | bytes 884744 | tf_op jit(solution)/shard_map/ppermute | solution.py:283
  71.5 5.9 %collective-permute-start.6 = (bf16[128,1152]{1,0:T(8,128)(2,1)S(1)}, bf16[128,1152]{1,0:T(8,128)(2,1)S(1)}, u32[]{:S(2)}, u32[]{:S(2)}) collective-permute-start(bf16[128,1152]{1,0:T(8,128)(2,1)S(1)} %shard_map.51.refs_2_), channel_id=1, source_target_pairs={{0,128},{128,0},{16,144},{144,16},{32,160},{160,32},{48,176},{176,... | collective-permute-start | bytes 884744 | tf_op jit(solution)/shard_map/ppermute | solution.py:283
  79.8 39.4 %copy-start = (bf16[1536,1024]{1,0:T(8,128)(2,1)S(1)}, bf16[1536,1024]{1,0:T(8,128)(2,1)}, u32[]{:S(2)}) copy-start(bf16[1536,1024]{1,0:T(8,128)(2,1)} %w_ref.3) | copy-start | bytes 9437188

commit v11 on v10

--- a/solution.py
+++ b/solution.py
@@ -305,11 +305,11 @@
     col = lax.all_to_all(
         jnp.broadcast_to(own[None], (n_col,) + own.shape), "col", 0, 0, tiled=True
     ).reshape(n_col * quarter, width + PAD)
-    sums = tiles([pair, other_pair], col, rates)
-    two_away = after(two_away, sums[0], 0)
-    next_own = after(next_own, sums[0], 0)
+    gate = after(other_pair, pair, FLOPS // 100)
+    two_away = after(two_away, gate, 0)
+    next_own = after(next_own, gate, 0)
     middle = [two_away, other_core(two_away), next_own, other_core(next_own)]
-    sums = tiles(middle, col, rates, sums, False)
+    sums = tiles([pair, gate] + middle, col, rates)
     next_other = after(next_other, middle[1], 0)
     part = tiles([next_other, other_core(next_other)], col, rates, sums, True)
     parts = lax.all_to_all(part.reshape(n_col, quarter, width), "col", 0, 0, tiled=True)

time: 122 us -> 127 us (1.041)
  waiting for transfers between devices: 0.97 us -> 7.15 us
  Pallas kernels: 12.6 us -> 10.8 us
    ppermute x9, waiting for transfers between devices: 0.97 us -> 7.15 us  [move(): return lax.ppermute(value, ZLINE, line_permutation(shift, n_row))]
    pallas_call x3 -> x2, Pallas kernels: 7.26 us -> 5.46 us  [tiles(): pl.pallas_call(functools.partial(tile_kernel, len(pieces), bool(held), la...]
  transfers between devices with their start and end apart: 10 -> 10, of which waited for: 1 -> 4; matrix products, arithmetic and copies ran while one was open for 1% -> 1% of each run, Pallas kernels for 4% -> 3%
where the time goes in v11:
time: 127 us; the launch traced here: 125 us
  blocking collectives  53.1 us (42%)
  starting transfers between devices  51.8 us (41%)
  Pallas kernels  10.8 us (9%)
  waiting for transfers between devices  7.15 us (6%)
  local copies, waits for them, and re-layouts  1.36 us (1%)
    ppermute x9, starting transfers between devices, move(): return lax.ppermute(value, ZLINE, line_permutation(shift, n_row))  45 us
    all_to_all x1, blocking collectives, shards(): lax.all_to_all(part.reshape(n_col, quarter, width), 'col', 0, 0, tiled=True)  22.6 us
    all_gather x1, blocking collectives, shards(): grad = lax.all_gather(grad, 'tensor', axis=0, tiled=True)  16.4 us
    all_gather x1, blocking collectives, shards(): lax.all_gather(partial, ZLINE, axis=0, tiled=True, axis_index_groups=hold...  14.1 us
    ppermute x9, waiting for transfers between devices, move(): return lax.ppermute(value, ZLINE, line_permutation(shift, n_row))  7.15 us
    all_to_all x1, starting transfers between devices, shards(): lax.all_to_all(jnp.broadcast_to(own[None], (n_col,) + own.shape), 'col',...  6.74 us
    pallas_call x2, Pallas kernels, tiles(): pl.pallas_call(functools.partial(tile_kernel, len(pieces), bool(held), la...  5.46 us
    pallas_call x1, Pallas kernels, projection(): pl.pallas_call(projection_kernel, out_shape=(jax.ShapeDtypeStruct((rows /...  3.15 us
  transfers between devices with their start and end apart: 10, of which 4 were waited for; matrix products, arithmetic and copies ran while one was open for 1% of the time, Pallas kernels for 3%

profile of v11, /device:TPU:1, one launch (start us, length us, event | category | flops | bytes accessed | tf_op | source)
XLA Modules:
  0.0 125.5 jit_solution(7070728947404982187)
XLA Ops:
  0.0 3.2 %shard_map.46 = (bf16[64,1024]{1,0:T(8,128)(2,1)}, f32[64,1024]{1,0:T(8,128)}) custom-call(s32[1]{0:T(128)} %bitcast.core_ref, bf16[128,1536]{1,0:T(8,128)(2,1)} %features_ref.1, bf16[1536,1024]{1,0:T(8,128)(2,1)} %w_ref.3), custom_call_target="tpu_custom_call" | custom-call | flops 402653184 | bytes 3145728 | tf_op jit(solution)/shard_map/pallas_call | solution.py:70
  3.2 8.8 %collective-permute-start = (bf16[64,1024]{1,0:T(8,128)(2,1)}, bf16[64,1024]{1,0:T(8,128)(2,1)S(1)}, u32[]{:S(2)}, u32[]{:S(2)}) collective-permute-start(bf16[64,1024]{1,0:T(8,128)(2,1)} %get-tuple-element.10), channel_id=1, source_target_pairs={{0,128},{128,0},{16,144},{144,16},{32,160},{160,32},{48,176},{176,... | collective-permute-start | bytes 393224 | tf_op jit(solution)/shard_map/ppermute | solution.py:283
  12.0 0.1 reshape.25
  12.1 0.1 select_n.41
  12.2 1.0 collective-permute-done
  13.1 1.0 add_convert_fusion
  14.1 14.1 %all_gather.6.both_ref = bf16[128,1024]{1,0:T(8,128)(2,1)S(1)} all-gather(bf16[64,1024]{1,0:T(8,128)(2,1)S(1)} %add_convert_fusion), channel_id=1, replica_groups={{0,256},{128,384},{16,272},{144,400},{32,288},{160,416},{48,304},{176,4..., dimensions={0}, use_global_device_ids=true | all-gather | bytes 393216 | tf_op jit(solution)/shard_map/all_gather | solution.py:293
  28.2 0.1 broadcast_in_dim.4.signs_ref
  28.3 0.1 shard_map.47.first_ref
  28.4 7.1 %collective-permute-start.1 = (bf16[64,1152]{1,0:T(8,128)(2,1)S(1)}, bf16[64,1152]{1,0:T(8,128)(2,1)S(1)}, u32[]{:S(2)}, u32[]{:S(2)}) collective-permute-start(bf16[64,1152]{1,0:T(8,128)(2,1)S(1)} %shard_map.47.first_ref), channel_id=1, source_target_pairs={{0,64},{128,448},{16,80},{144,464},{32,96},{160,480},{48,112},{176... | collective-permute-start | bytes 442376 | tf_op jit(solution)/shard_map/ppermute | solution.py:283
  35.5 1.1 broadcast_in_dim.5
  36.7 6.7 %all-to-all-start = ((bf16[16,32,1152]{2,1,0:T(8,128)(2,1)}), bf16[16,32,1152]{2,1,0:T(8,128)(2,1)S(1)}, u32[]{:S(2)}, u32[]{:S(2)}) async-start(bf16[16,32,1152]{2,1,0:T(8,128)(2,1)} %broadcast_in_dim.5), calls=%async_computation | async-start | bytes 2359296 | tf_op jit(solution)/shard_map/all_to_all | solution.py:305
  43.4 0.0 collective-permute-done.1.second_ref
  43.5 0.0 copy-start.1
  43.5 7.0 %collective-permute-start.2 = (bf16[128,1152]{1,0:T(8,128)(2,1)S(1)}, bf16[128,1152]{1,0:T(8,128)(2,1)S(1)}, u32[]{:S(2)}, u32[]{:S(2)}) collective-permute-start(bf16[128,1152]{1,0:T(8,128)(2,1)S(1)} %shard_map.48.first_ref.refs_2_), channel_id=1, source_target_pairs={{0,128},{128,0},{16,144},{144,16},{32,160},{160,32},{48,176},{176,... | collective-permute-start | bytes 884744 | tf_op jit(solution)/shard_map/ppermute | solution.py:283
  50.4 1.2 collective-permute-done.2.value_ref
  51.6 3.0 %collective-permute-start.3 = (bf16[128,1152]{1,0:T(8,128)(2,1)S(1)}, bf16[128,1152]{1,0:T(8,128)(2,1)S(1)}, u32[]{:S(2)}, u32[]{:S(2)}) collective-permute-start(bf16[128,1152]{1,0:T(8,128)(2,1)S(1)} %collective-permute-done.2.value_ref), channel_id=1, source_target_pairs={{0,16},{128,496},{16,32},{144,128},{32,48},{160,144},{48,64},{176,... | collective-permute-start | bytes 884744 | tf_op jit(solution)/shard_map/ppermute | solution.py:283
  54.6 7.6 %collective-permute-start.4 = (bf16[128,1152]{1,0:T(8,128)(2,1)S(1)}, bf16[128,1152]{1,0:T(8,128)(2,1)S(1)}, u32[]{:S(2)}, u32[]{:S(2)}) collective-permute-start(bf16[128,1152]{1,0:T(8,128)(2,1)S(1)} %shard_map.48.first_ref.refs_2_), channel_id=1, source_target_pairs={{0,32},{128,480},{16,48},{144,496},{32,64},{160,128},{48,80},{176,... | collective-permute-start | bytes 884744 | tf_op jit(solution)/shard_map/ppermute | solution.py:283
  62.2 2.2 %collective-permute-start.7 = (bf16[128,1152]{1,0:T(8,128)(2,1)S(1)}, bf16[128,1152]{1,0:T(8,128)(2,1)S(1)}, u32[]{:S(2)}, u32[]{:S(2)}) collective-permute-start(bf16[128,1152]{1,0:T(8,128)(2,1)S(1)} %shard_map.48.first_ref.refs_2_), channel_id=1, source_target_pairs={{0,16},{128,496},{16,32},{144,128},{32,48},{160,144},{48,64},{176,... | collective-permute-start | bytes 884744 | tf_op jit(solution)/shard_map/ppermute | solution.py:283
  64.4 2.6 %collective-permute-done.4.value_ref = bf16[128,1152]{1,0:T(8,128)(2,1)S(1)} collective-permute-done((bf16[128,1152]{1,0:T(8,128)(2,1)S(1)}, bf16[128,1152]{1,0:T(8,128)(2,1)S(1)}, u32[]{:S(2)}, u32[]{:S(2)}) %collective-permute-start.4) | collective-permute-done | bytes 294944 | tf_op jit(solution)/shard_map/ppermute | solution.py:283
  67.0 3.7 %collective-permute-start.5 = (bf16[128,1152]{1,0:T(8,128)(2,1)S(1)}, bf16[128,1152]{1,0:T(8,128)(2,1)S(1)}, u32[]{:S(2)}, u32[]{:S(2)}) collective-permute-start(bf16[128,1152]{1,0:T(8,128)(2,1)S(1)} %shard_map.50.refs_4_), channel_id=1, source_target_pairs={{0,128},{128,0},{16,144},{144,16},{32,160},{160,32},{48,176},{176,... | collective-permute-start | bytes 884744 | tf_op jit(solution)/shard_map/ppermute | solution.py:283
  70.7 2.4 %collective-permute-done.7.value_ref = bf16[128,1152]{1,0:T(8,128)(2,1)S(1)} collective-permute-done((bf16[128,1152]{1,0:T(8,128)(2,1)S(1)}, bf16[128,1152]{1,0:T(8,128)(2,1)S(1)}, u32[]{:S(2)}, u32[]{:S(2)}) %collective-permute-start.7) | collective-permute-done | bytes 294944 | tf_op jit(solution)/shard_map/ppermute | solution.py:283
  73.1 3.9 %collective-permute-start.8 = (bf16[128,1152]{1,0:T(8,128)(2,1)S(1)}, bf16[128,1152]{1,0:T(8,128)(2,1)S(1)}, u32[]{:S(2)}, u32[]{:S(2)}) collective-permute-start(bf16[128,1152]{1,0:T(8,128)(2,1)S(1)} %shard_map.52.refs_6_), channel_id=1, source_target_pairs={{0,128},{128,0},{16,144},{144,16},{32,160},{160,32},{48,176},{176,... | collective-permute-start | bytes 884744 | tf_op jit(solution)/shard_map/ppermute | solution.py:283
  77.0 0.0 collective-permute-done.5.first_ref.refs_5_
  77.0 1.9 %collective-permute-start.6 = (bf16[128,1152]{1,0:T(8,128)(2,1)S(1)}, bf16[128,1152]{1,0:T(8,128)(2,1)S(1)}, u32[]{:S(2)}, u32[]{:S(2)}) collective-permute-start(bf16[128,1152]{1,0:T(8,128)(2,1)S(1)} %shard_map.51.refs_2_), channel_id=1, source_target_pairs={{0,128},{128,0},{16,144},{144,16},{32,160},{160,32},{48,176},{176,... | collective-permute-start | bytes 884744 | tf_op jit(solution)/shard_map/ppermute | solution.py:283
  78.9 3.1 %shard_map.53 = (f32[512,128]{1,0:T(8,128)S(1)}, f32[512,1024]{1,0:T(8,128)S(1)}) custom-call(f32[5]{0:T(128)S(1)} %copy-done.1, bf16[512,1152]{1,0:T(8,128)(2,1)S(1)} %bitcast.3, bf16[128,1152]{1,0:T(8,128)(2,1)S(1)} %shard_map.48.first_ref.refs_2_, bf16[128,1152]{1,0:T(8,128)(2,1)S(1)} %shard_map.49.first_ref.refs_3_, ...), custom_call_target="tpu_custom_call" | custom-call | flops 1610612736 | bytes 2097152 | tf_op jit(solution)/shard_map/pallas_call | solution.py:259
  82.1 2.3 %shard_map.54 = bf16[512,1024]{1,0:T(8,128)(2,1)S(1)} custom-call(f32[5]{0:T(128)S(1)} %copy-done.1, bf16[512,1152]{1,0:T(8,128)(2,1)S(1)} %bitcast.4, bf16[128,1152]{1,0:T(8,128)(2,1)S(1)} %shard_map.51.refs_2_, bf16[128,1152]{1,0:T(8,128)(2,1)S(1)} %collective-permute-done.6.refs_3_, f32[512,128]{1,0:T(8,128)S(1)} %get-tuple-element.11.refs_4_, ...), custom_call_target="tpu_custom_call" | custom-call | flops 536870912 | bytes 2097152 | tf_op jit(solution)/shard_map/pallas_call | solution.py:259
  84.4 0.0 copy-start
  84.4 22.6 %all_to_all.10.parts_ref = bf16[16,32,1024]{2,1,0:T(8,128)(2,1)S(1)} all-to-all(bf16[16,32,1024]{2,1,0:T(8,128)(2,1)S(1)} %bitcast.5), channel_id=1, replica_groups=mesh['tensor'=4,'row'=8,'col'=16] {'col'}, dimensions={0} | all-to-all | bytes 2097152 | tf_op jit(solution)/shard_map/all_to_all | solution.py:315
  107.1 0.1 shard_map.55
  107.2 16.4 %all_gather.7.grad_ref = bf16[128,1024]{1,0:T(8,128)(2,1)S(1)} all-gather(bf16[32,1024]{1,0:T(8,128)(2,1)S(1)} %shard_map.55), channel_id=1, replica_groups=mesh['tensor'=4,'row'=8,'col'=16] {'tensor'}, dimensions={0}, use_global_device_ids=true | all-gather | bytes 327680 | tf_op jit(solution)/shard_map/all_gather | solution.py:317
  123.6 1.9 %shard_map.56 = bf16[128,1536]{1,0:T(8,128)(2,1)} custom-call(bf16[128,1024]{1,0:T(8,128)(2,1)S(1)} %all_gather.7.grad_ref, bf16[1536,1024]{1,0:T(8,128)(2,1)S(1)} %copy-done), custom_call_target="tpu_custom_call" | custom-call | flops 402653184 | bytes 3145728 | tf_op jit(solution)/shard_map/pallas_call | solution.py:131
  (16 shorter events, 0.1 us)
Async XLA Ops:
  0.0 11.9 %copy-start.2 = (s32[128]{0:T(128)S(1)}, s32[128]{0:T(128)}, u32[]{:S(2)}) copy-start(s32[128]{0:T(128)} %param.6) | copy-start | bytes 1540
  3.2 10.0 %collective-permute-start = (bf16[64,1024]{1,0:T(8,128)(2,1)}, bf16[64,1024]{1,0:T(8,128)(2,1)S(1)}, u32[]{:S(2)}, u32[]{:S(2)}) collective-permute-start(bf16[64,1024]{1,0:T(8,128)(2,1)} %get-tuple-element.10), channel_id=1, source_target_pairs={{0,128},{128,0},{16,144},{144,16},{32,160},{160,32},{48,176},{176,... | collective-permute-start | bytes 393224 | tf_op jit(solution)/shard_map/ppermute | solution.py:283
  28.4 15.0 %collective-permute-start.1 = (bf16[64,1152]{1,0:T(8,128)(2,1)S(1)}, bf16[64,1152]{1,0:T(8,128)(2,1)S(1)}, u32[]{:S(2)}, u32[]{:S(2)}) collective-permute-start(bf16[64,1152]{1,0:T(8,128)(2,1)S(1)} %shard_map.47.first_ref), channel_id=1, source_target_pairs={{0,64},{128,448},{16,80},{144,464},{32,96},{160,480},{48,112},{176... | collective-permute-start | bytes 442376 | tf_op jit(solution)/shard_map/ppermute | solution.py:283
  36.7 42.3 %all-to-all-start = ((bf16[16,32,1152]{2,1,0:T(8,128)(2,1)}), bf16[16,32,1152]{2,1,0:T(8,128)(2,1)S(1)}, u32[]{:S(2)}, u32[]{:S(2)}) async-start(bf16[16,32,1152]{2,1,0:T(8,128)(2,1)} %broadcast_in_dim.5), calls=%async_computation | async-start | bytes 2359296 | tf_op jit(solution)/shard_map/all_to_all | solution.py:305
  43.5 35.5 %copy-start.1 = (f32[5]{0:T(128)S(1)}, f32[5]{0:T(128)}, u32[]{:S(2)}) copy-start(f32[5]{0:T(128)} %refs_0_.3) | copy-start | bytes 64
  43.5 8.1 %collective-permute-start.2 = (bf16[128,1152]{1,0:T(8,128)(2,1)S(1)}, bf16[128,1152]{1,0:T(8,128)(2,1)S(1)}, u32[]{:S(2)}, u32[]{:S(2)}) collective-permute-start(bf16[128,1152]{1,0:T(8,128)(2,1)S(1)} %shard_map.48.first_ref.refs_2_), channel_id=1, source_target_pairs={{0,128},{128,0},{16,144},{144,16},{32,160},{160,32},{48,176},{176,... | collective-permute-start | bytes 884744 | tf_op jit(solution)/shard_map/ppermute | solution.py:283
  51.6 12.8 %collective-permute-start.3 = (bf16[128,1152]{1,0:T(8,128)(2,1)S(1)}, bf16[128,1152]{1,0:T(8,128)(2,1)S(1)}, u32[]{:S(2)}, u32[]{:S(2)}) collective-permute-start(bf16[128,1152]{1,0:T(8,128)(2,1)S(1)} %collective-permute-done.2.value_ref), channel_id=1, source_target_pairs={{0,16},{128,496},{16,32},{144,128},{32,48},{160,144},{48,64},{176,... | collective-permute-start | bytes 884744 | tf_op jit(solution)/shard_map/ppermute | solution.py:283
  54.6 12.4 %collective-permute-start.4 = (bf16[128,1152]{1,0:T(8,128)(2,1)S(1)}, bf16[128,1152]{1,0:T(8,128)(2,1)S(1)}, u32[]{:S(2)}, u32[]{:S(2)}) collective-permute-start(bf16[128,1152]{1,0:T(8,128)(2,1)S(1)} %shard_map.48.first_ref.refs_2_), channel_id=1, source_target_pairs={{0,32},{128,480},{16,48},{144,496},{32,64},{160,128},{48,80},{176,... | collective-permute-start | bytes 884744 | tf_op jit(solution)/shard_map/ppermute | solution.py:283
  62.2 10.9 %collective-permute-start.7 = (bf16[128,1152]{1,0:T(8,128)(2,1)S(1)}, bf16[128,1152]{1,0:T(8,128)(2,1)S(1)}, u32[]{:S(2)}, u32[]{:S(2)}) collective-permute-start(bf16[128,1152]{1,0:T(8,128)(2,1)S(1)} %shard_map.48.first_ref.refs_2_), channel_id=1, source_target_pairs={{0,16},{128,496},{16,32},{144,128},{32,48},{160,144},{48,64},{176,... | collective-permute-start | bytes 884744 | tf_op jit(solution)/shard_map/ppermute | solution.py:283
  67.0 9.9 %collective-permute-start.5 = (bf16[128,1152]{1,0:T(8,128)(2,1)S(1)}, bf16[128,1152]{1,0:T(8,128)(2,1)S(1)}, u32[]{:S(2)}, u32[]{:S(2)}) collective-permute-start(bf16[128,1152]{1,0:T(8,128)(2,1)S(1)} %shard_map.50.refs_4_), channel_id=1, source_target_pairs={{0,128},{128,0},{16,144},{144,16},{32,160},{160,32},{48,176},{176,... | collective-permute-start | bytes 884744 | tf_op jit(solution)/shard_map/ppermute | solution.py:283
  73.1 5.8 %collective-permute-start.8 = (bf16[128,1152]{1,0:T(8,128)(2,1)S(1)}, bf16[128,1152]{1,0:T(8,128)(2,1)S(1)}, u32[]{:S(2)}, u32[]{:S(2)}) collective-permute-start(bf16[128,1152]{1,0:T(8,128)(2,1)S(1)} %shard_map.52.refs_6_), channel_id=1, source_target_pairs={{0,128},{128,0},{16,144},{144,16},{32,160},{160,32},{48,176},{176,... | collective-permute-start | bytes 884744 | tf_op jit(solution)/shard_map/ppermute | solution.py:283
  77.0 5.1 %collective-permute-start.6 = (bf16[128,1152]{1,0:T(8,128)(2,1)S(1)}, bf16[128,1152]{1,0:T(8,128)(2,1)S(1)}, u32[]{:S(2)}, u32[]{:S(2)}) collective-permute-start(bf16[128,1152]{1,0:T(8,128)(2,1)S(1)} %shard_map.51.refs_2_), channel_id=1, source_target_pairs={{0,128},{128,0},{16,144},{144,16},{32,160},{160,32},{48,176},{176,... | collective-permute-start | bytes 884744 | tf_op jit(solution)/shard_map/ppermute | solution.py:283
  84.4 39.1 %copy-start = (bf16[1536,1024]{1,0:T(8,128)(2,1)S(1)}, bf16[1536,1024]{1,0:T(8,128)(2,1)}, u32[]{:S(2)}) copy-start(bf16[1536,1024]{1,0:T(8,128)(2,1)} %w_ref.3) | copy-start | bytes 9437188

commit v12 on v10

--- a/solution.py
+++ b/solution.py
@@ -30,7 +30,7 @@
 def pick(second, low, high):
     return jnp.where(second, high, low)
 
-CHUNKS = 4
+CHUNKS = 6
 
 
 def projection_kernel(core_ref, features_ref, w_ref, away_ref, kept_ref, rows, weights, total, sem):

time: 122 us -> 122 us (level)
  no operation moved by 1% of the time
where the time goes in v12:
time: 122 us; the launch traced here: 121 us
  blocking collectives  53.3 us (44%)
  starting transfers between devices  51.4 us (42%)
  Pallas kernels  12.6 us (10%)
  local copies, waits for them, and re-layouts  1.38 us (1%)
    ppermute x9, starting transfers between devices, move(): return lax.ppermute(value, ZLINE, line_permutation(shift, n_row))  44.7 us
    all_to_all x1, blocking collectives, shards(): lax.all_to_all(part.reshape(n_col, quarter, width), 'col', 0, 0, tiled=True)  22.6 us
    all_gather x1, blocking collectives, shards(): grad = lax.all_gather(grad, 'tensor', axis=0, tiled=True)  16.7 us
    all_gather x1, blocking collectives, shards(): lax.all_gather(partial, ZLINE, axis=0, tiled=True, axis_index_groups=hold...  14.1 us
    pallas_call x3, Pallas kernels, tiles(): pl.pallas_call(functools.partial(tile_kernel, len(pieces), bool(held), la...  7.26 us
    all_to_all x1, starting transfers between devices, shards(): lax.all_to_all(jnp.broadcast_to(own[None], (n_col,) + own.shape), 'col',...  6.75 us
    pallas_call x1, Pallas kernels, projection(): pl.pallas_call(projection_kernel, out_shape=(jax.ShapeDtypeStruct((rows /...  3.09 us
  transfers between devices with their start and end apart: 10, of which 1 were waited for; matrix products, arithmetic and copies ran while one was open for 1% of the time, Pallas kernels for 4%

profile of v12, /device:TPU:1, one launch (start us, length us, event | category | flops | bytes accessed | tf_op | source)
XLA Modules:
  0.0 121.0 jit_solution(15072981465591033038)
XLA Ops:
  0.0 3.1 %shard_map.46 = (bf16[64,1024]{1,0:T(8,128)(2,1)}, f32[64,1024]{1,0:T(8,128)}) custom-call(s32[1]{0:T(128)} %bitcast.core_ref, bf16[128,1536]{1,0:T(8,128)(2,1)} %features_ref.1, bf16[1536,1024]{1,0:T(8,128)(2,1)} %w_ref.3), custom_call_target="tpu_custom_call" | custom-call | flops 402653184 | bytes 3145728 | tf_op jit(solution)/shard_map/pallas_call | solution.py:70
  3.1 8.8 %collective-permute-start = (bf16[64,1024]{1,0:T(8,128)(2,1)}, bf16[64,1024]{1,0:T(8,128)(2,1)S(1)}, u32[]{:S(2)}, u32[]{:S(2)}) collective-permute-start(bf16[64,1024]{1,0:T(8,128)(2,1)} %get-tuple-element.12), channel_id=1, source_target_pairs={{0,128},{128,0},{16,144},{144,16},{32,160},{160,32},{48,176},{176,... | collective-permute-start | bytes 393224 | tf_op jit(solution)/shard_map/ppermute | solution.py:283
  11.9 0.1 reshape.25
  12.0 0.1 select_n.41
  12.1 1.0 collective-permute-done
  13.1 1.0 add_convert_fusion
  14.0 14.1 %all_gather.6.both_ref = bf16[128,1024]{1,0:T(8,128)(2,1)S(1)} all-gather(bf16[64,1024]{1,0:T(8,128)(2,1)S(1)} %add_convert_fusion), channel_id=1, replica_groups={{0,256},{128,384},{16,272},{144,400},{32,288},{160,416},{48,304},{176,4..., dimensions={0}, use_global_device_ids=true | all-gather | bytes 393216 | tf_op jit(solution)/shard_map/all_gather | solution.py:293
  28.2 0.1 broadcast_in_dim.4.signs_ref
  28.2 0.1 shard_map.47.first_ref
  28.4 7.1 %collective-permute-start.1 = (bf16[64,1152]{1,0:T(8,128)(2,1)S(1)}, bf16[64,1152]{1,0:T(8,128)(2,1)S(1)}, u32[]{:S(2)}, u32[]{:S(2)}) collective-permute-start(bf16[64,1152]{1,0:T(8,128)(2,1)S(1)} %shard_map.47.first_ref), channel_id=1, source_target_pairs={{0,64},{128,448},{16,80},{144,464},{32,96},{160,480},{48,112},{176... | collective-permute-start | bytes 442376 | tf_op jit(solution)/shard_map/ppermute | solution.py:283
  35.5 1.1 broadcast_in_dim.5
  36.6 6.8 %all-to-all-start = ((bf16[16,32,1152]{2,1,0:T(8,128)(2,1)}), bf16[16,32,1152]{2,1,0:T(8,128)(2,1)S(1)}, u32[]{:S(2)}, u32[]{:S(2)}) async-start(bf16[16,32,1152]{2,1,0:T(8,128)(2,1)} %broadcast_in_dim.5), calls=%async_computation | async-start | bytes 2359296 | tf_op jit(solution)/shard_map/all_to_all | solution.py:305
  43.4 0.0 copy-start.1
  43.4 7.0 %collective-permute-start.2 = (bf16[128,1152]{1,0:T(8,128)(2,1)S(1)}, bf16[128,1152]{1,0:T(8,128)(2,1)S(1)}, u32[]{:S(2)}, u32[]{:S(2)}) collective-permute-start(bf16[128,1152]{1,0:T(8,128)(2,1)S(1)} %shard_map.48.refs_2_), channel_id=1, source_target_pairs={{0,128},{128,0},{16,144},{144,16},{32,160},{160,32},{48,176},{176,... | collective-permute-start | bytes 884744 | tf_op jit(solution)/shard_map/ppermute | solution.py:283
  50.4 8.6 %collective-permute-start.4 = (bf16[128,1152]{1,0:T(8,128)(2,1)S(1)}, bf16[128,1152]{1,0:T(8,128)(2,1)S(1)}, u32[]{:S(2)}, u32[]{:S(2)}) collective-permute-start(bf16[128,1152]{1,0:T(8,128)(2,1)S(1)} %shard_map.48.refs_2_), channel_id=1, source_target_pairs={{0,32},{128,480},{16,48},{144,496},{32,64},{160,128},{48,80},{176,... | collective-permute-start | bytes 884744 | tf_op jit(solution)/shard_map/ppermute | solution.py:283
  59.0 1.9 %collective-permute-start.7 = (bf16[128,1152]{1,0:T(8,128)(2,1)S(1)}, bf16[128,1152]{1,0:T(8,128)(2,1)S(1)}, u32[]{:S(2)}, u32[]{:S(2)}) collective-permute-start(bf16[128,1152]{1,0:T(8,128)(2,1)S(1)} %shard_map.48.refs_2_), channel_id=1, source_target_pairs={{0,16},{128,496},{16,32},{144,128},{32,48},{160,144},{48,64},{176,... | collective-permute-start | bytes 884744 | tf_op jit(solution)/shard_map/ppermute | solution.py:283
  60.9 0.0 collective-permute-done.2.refs_3_
  60.9 2.2 %collective-permute-start.3 = (bf16[128,1152]{1,0:T(8,128)(2,1)S(1)}, bf16[128,1152]{1,0:T(8,128)(2,1)S(1)}, u32[]{:S(2)}, u32[]{:S(2)}) collective-permute-start(bf16[128,1152]{1,0:T(8,128)(2,1)S(1)} %collective-permute-done.2.refs_3_), channel_id=1, source_target_pairs={{0,16},{128,496},{16,32},{144,128},{32,48},{160,144},{48,64},{176,... | collective-permute-start | bytes 884744 | tf_op jit(solution)/shard_map/ppermute | solution.py:283
  63.1 0.0 all-to-all-done
  63.1 2.2 %shard_map.49 = (f32[512,128]{1,0:T(8,128)S(1)}, f32[512,1024]{1,0:T(8,128)S(1)}) custom-call(f32[5]{0:T(128)S(1)} %copy-done.1, bf16[512,1152]{1,0:T(8,128)(2,1)S(1)} %bitcast.3, bf16[128,1152]{1,0:T(8,128)(2,1)S(1)} %shard_map.48.refs_2_, bf16[128,1152]{1,0:T(8,128)(2,1)S(1)} %collective-permute-done.2.refs_3_), custom_call_target="tpu_custom_call" | custom-call | flops 536870912 | bytes 2097152 | tf_op jit(solution)/shard_map/pallas_call | solution.py:259
  65.4 3.0 %collective-permute-start.5 = (bf16[128,1152]{1,0:T(8,128)(2,1)S(1)}, bf16[128,1152]{1,0:T(8,128)(2,1)S(1)}, u32[]{:S(2)}, u32[]{:S(2)}) collective-permute-start(bf16[128,1152]{1,0:T(8,128)(2,1)S(1)} %shard_map.50.refs_2_), channel_id=1, source_target_pairs={{0,128},{128,0},{16,144},{144,16},{32,160},{160,32},{48,176},{176,... | collective-permute-start | bytes 884744 | tf_op jit(solution)/shard_map/ppermute | solution.py:283
  68.4 3.0 %collective-permute-start.8 = (bf16[128,1152]{1,0:T(8,128)(2,1)S(1)}, bf16[128,1152]{1,0:T(8,128)(2,1)S(1)}, u32[]{:S(2)}, u32[]{:S(2)}) collective-permute-start(bf16[128,1152]{1,0:T(8,128)(2,1)S(1)} %shard_map.52.refs_4_), channel_id=1, source_target_pairs={{0,128},{128,0},{16,144},{144,16},{32,160},{160,32},{48,176},{176,... | collective-permute-start | bytes 884744 | tf_op jit(solution)/shard_map/ppermute | solution.py:283
  71.4 0.0 collective-permute-done.3.value_ref
  71.4 0.0 collective-permute-done.5.first_ref.refs_3_
  71.5 3.1 %collective-permute-start.6 = (bf16[128,1152]{1,0:T(8,128)(2,1)S(1)}, bf16[128,1152]{1,0:T(8,128)(2,1)S(1)}, u32[]{:S(2)}, u32[]{:S(2)}) collective-permute-start(bf16[128,1152]{1,0:T(8,128)(2,1)S(1)} %shard_map.51.refs_2_), channel_id=1, source_target_pairs={{0,128},{128,0},{16,144},{144,16},{32,160},{160,32},{48,176},{176,... | collective-permute-start | bytes 884744 | tf_op jit(solution)/shard_map/ppermute | solution.py:283
  74.6 2.7 %shard_map.53 = (f32[512,128]{1,0:T(8,128)S(1)}, f32[512,1024]{1,0:T(8,128)S(1)}) custom-call(f32[5]{0:T(128)S(1)} %copy-done.1, bf16[512,1152]{1,0:T(8,128)(2,1)S(1)} %bitcast.4, bf16[128,1152]{1,0:T(8,128)(2,1)S(1)} %shard_map.50.refs_2_, bf16[128,1152]{1,0:T(8,128)(2,1)S(1)} %collective-permute-done.5.first_ref.refs_3_, ...), custom_call_target="tpu_custom_call" | custom-call | flops 1073741824 | bytes 2097152 | tf_op jit(solution)/shard_map/pallas_call | solution.py:259
  77.3 2.4 %shard_map.54 = bf16[512,1024]{1,0:T(8,128)(2,1)S(1)} custom-call(f32[5]{0:T(128)S(1)} %copy-done.1, bf16[512,1152]{1,0:T(8,128)(2,1)S(1)} %bitcast.5, bf16[128,1152]{1,0:T(8,128)(2,1)S(1)} %shard_map.51.refs_2_, bf16[128,1152]{1,0:T(8,128)(2,1)S(1)} %collective-permute-done.6.refs_3_, f32[512,128]{1,0:T(8,128)S(1)} %get-tuple-element.15.refs_4_, ...), custom_call_target="tpu_custom_call" | custom-call | flops 536870912 | bytes 2097152 | tf_op jit(solution)/shard_map/pallas_call | solution.py:259
  79.7 0.0 copy-start
  79.7 22.6 %all_to_all.10.parts_ref = bf16[16,32,1024]{2,1,0:T(8,128)(2,1)S(1)} all-to-all(bf16[16,32,1024]{2,1,0:T(8,128)(2,1)S(1)} %bitcast.6), channel_id=1, replica_groups=mesh['tensor'=4,'row'=8,'col'=16] {'col'}, dimensions={0} | all-to-all | bytes 2097152 | tf_op jit(solution)/shard_map/all_to_all | solution.py:315
  102.3 0.1 shard_map.55
  102.4 16.7 %all_gather.7.grad_ref = bf16[128,1024]{1,0:T(8,128)(2,1)S(1)} all-gather(bf16[32,1024]{1,0:T(8,128)(2,1)S(1)} %shard_map.55), channel_id=1, replica_groups=mesh['tensor'=4,'row'=8,'col'=16] {'tensor'}, dimensions={0}, use_global_device_ids=true | all-gather | bytes 327680 | tf_op jit(solution)/shard_map/all_gather | solution.py:317
  119.1 1.9 %shard_map.56 = bf16[128,1536]{1,0:T(8,128)(2,1)} custom-call(bf16[128,1024]{1,0:T(8,128)(2,1)S(1)} %all_gather.7.grad_ref, bf16[1536,1024]{1,0:T(8,128)(2,1)S(1)} %copy-done), custom_call_target="tpu_custom_call" | custom-call | flops 402653184 | bytes 3145728 | tf_op jit(solution)/shard_map/pallas_call | solution.py:131
  (16 shorter events, 0.1 us)
Async XLA Ops:
  0.0 11.9 %copy-start.2 = (s32[128]{0:T(128)S(1)}, s32[128]{0:T(128)}, u32[]{:S(2)}) copy-start(s32[128]{0:T(128)} %param.6) | copy-start | bytes 1540
  3.1 10.0 %collective-permute-start = (bf16[64,1024]{1,0:T(8,128)(2,1)}, bf16[64,1024]{1,0:T(8,128)(2,1)S(1)}, u32[]{:S(2)}, u32[]{:S(2)}) collective-permute-start(bf16[64,1024]{1,0:T(8,128)(2,1)} %get-tuple-element.12), channel_id=1, source_target_pairs={{0,128},{128,0},{16,144},{144,16},{32,160},{160,32},{48,176},{176,... | collective-permute-start | bytes 393224 | tf_op jit(solution)/shard_map/ppermute | solution.py:283
  28.4 15.0 %collective-permute-start.1 = (bf16[64,1152]{1,0:T(8,128)(2,1)S(1)}, bf16[64,1152]{1,0:T(8,128)(2,1)S(1)}, u32[]{:S(2)}, u32[]{:S(2)}) collective-permute-start(bf16[64,1152]{1,0:T(8,128)(2,1)S(1)} %shard_map.47.first_ref), channel_id=1, source_target_pairs={{0,64},{128,448},{16,80},{144,464},{32,96},{160,480},{48,112},{176... | collective-permute-start | bytes 442376 | tf_op jit(solution)/shard_map/ppermute | solution.py:283
  36.6 26.5 %all-to-all-start = ((bf16[16,32,1152]{2,1,0:T(8,128)(2,1)}), bf16[16,32,1152]{2,1,0:T(8,128)(2,1)S(1)}, u32[]{:S(2)}, u32[]{:S(2)}) async-start(bf16[16,32,1152]{2,1,0:T(8,128)(2,1)} %broadcast_in_dim.5), calls=%async_computation | async-start | bytes 2359296 | tf_op jit(solution)/shard_map/all_to_all | solution.py:305
  43.4 19.8 %copy-start.1 = (f32[5]{0:T(128)S(1)}, f32[5]{0:T(128)}, u32[]{:S(2)}) copy-start(f32[5]{0:T(128)} %refs_0_.5) | copy-start | bytes 64
  43.4 17.5 %collective-permute-start.2 = (bf16[128,1152]{1,0:T(8,128)(2,1)S(1)}, bf16[128,1152]{1,0:T(8,128)(2,1)S(1)}, u32[]{:S(2)}, u32[]{:S(2)}) collective-permute-start(bf16[128,1152]{1,0:T(8,128)(2,1)S(1)} %shard_map.48.refs_2_), channel_id=1, source_target_pairs={{0,128},{128,0},{16,144},{144,16},{32,160},{160,32},{48,176},{176,... | collective-permute-start | bytes 884744 | tf_op jit(solution)/shard_map/ppermute | solution.py:283
  50.4 15.0 %collective-permute-start.4 = (bf16[128,1152]{1,0:T(8,128)(2,1)S(1)}, bf16[128,1152]{1,0:T(8,128)(2,1)S(1)}, u32[]{:S(2)}, u32[]{:S(2)}) collective-permute-start(bf16[128,1152]{1,0:T(8,128)(2,1)S(1)} %shard_map.48.refs_2_), channel_id=1, source_target_pairs={{0,32},{128,480},{16,48},{144,496},{32,64},{160,128},{48,80},{176,... | collective-permute-start | bytes 884744 | tf_op jit(solution)/shard_map/ppermute | solution.py:283
  59.0 9.4 %collective-permute-start.7 = (bf16[128,1152]{1,0:T(8,128)(2,1)S(1)}, bf16[128,1152]{1,0:T(8,128)(2,1)S(1)}, u32[]{:S(2)}, u32[]{:S(2)}) collective-permute-start(bf16[128,1152]{1,0:T(8,128)(2,1)S(1)} %shard_map.48.refs_2_), channel_id=1, source_target_pairs={{0,16},{128,496},{16,32},{144,128},{32,48},{160,144},{48,64},{176,... | collective-permute-start | bytes 884744 | tf_op jit(solution)/shard_map/ppermute | solution.py:283
  60.9 10.5 %collective-permute-start.3 = (bf16[128,1152]{1,0:T(8,128)(2,1)S(1)}, bf16[128,1152]{1,0:T(8,128)(2,1)S(1)}, u32[]{:S(2)}, u32[]{:S(2)}) collective-permute-start(bf16[128,1152]{1,0:T(8,128)(2,1)S(1)} %collective-permute-done.2.refs_3_), channel_id=1, source_target_pairs={{0,16},{128,496},{16,32},{144,128},{32,48},{160,144},{48,64},{176,... | collective-permute-start | bytes 884744 | tf_op jit(solution)/shard_map/ppermute | solution.py:283
  65.4 6.1 %collective-permute-start.5 = (bf16[128,1152]{1,0:T(8,128)(2,1)S(1)}, bf16[128,1152]{1,0:T(8,128)(2,1)S(1)}, u32[]{:S(2)}, u32[]{:S(2)}) collective-permute-start(bf16[128,1152]{1,0:T(8,128)(2,1)S(1)} %shard_map.50.refs_2_), channel_id=1, source_target_pairs={{0,128},{128,0},{16,144},{144,16},{32,160},{160,32},{48,176},{176,... | collective-permute-start | bytes 884744 | tf_op jit(solution)/shard_map/ppermute | solution.py:283
  68.4 6.2 %collective-permute-start.8 = (bf16[128,1152]{1,0:T(8,128)(2,1)S(1)}, bf16[128,1152]{1,0:T(8,128)(2,1)S(1)}, u32[]{:S(2)}, u32[]{:S(2)}) collective-permute-start(bf16[128,1152]{1,0:T(8,128)(2,1)S(1)} %shard_map.52.refs_4_), channel_id=1, source_target_pairs={{0,128},{128,0},{16,144},{144,16},{32,160},{160,32},{48,176},{176,... | collective-permute-start | bytes 884744 | tf_op jit(solution)/shard_map/ppermute | solution.py:283
  71.5 5.9 %collective-permute-start.6 = (bf16[128,1152]{1,0:T(8,128)(2,1)S(1)}, bf16[128,1152]{1,0:T(8,128)(2,1)S(1)}, u32[]{:S(2)}, u32[]{:S(2)}) collective-permute-start(bf16[128,1152]{1,0:T(8,128)(2,1)S(1)} %shard_map.51.refs_2_), channel_id=1, source_target_pairs={{0,128},{128,0},{16,144},{144,16},{32,160},{160,32},{48,176},{176,... | collective-permute-start | bytes 884744 | tf_op jit(solution)/shard_map/ppermute | solution.py:283
  79.7 39.4 %copy-start = (bf16[1536,1024]{1,0:T(8,128)(2,1)S(1)}, bf16[1536,1024]{1,0:T(8,128)(2,1)}, u32[]{:S(2)}) copy-start(bf16[1536,1024]{1,0:T(8,128)(2,1)} %w_ref.3) | copy-start | bytes 9437188
